TPU v7x, 32 devices: a whole 2x2x4 slice. The times are simulated.
32 devices in a mesh: wide: 8 (over z, y), tm: 4 (over x, core).
Axes of the slice: x: 2, y: 2, z: 4, core: 2. Of those that a mesh axis runs over, the one named last changes fastest.
Arguments:
- voltages: bfloat16 [2, 2048, 24576], P(None, 'wide', 'tm'), may hold values from -12 to 12
- fir_taps: float32 [4, 256], replicated, may hold values from -3 to 3
- steering: float32 [512, 2048], replicated, may hold values from 0 to 8
- band_widths: int32 [8], replicated, may hold values from 1 to 64, 256 in all
- delays: int32 [128, 256], replicated, may hold values from 0 to 7, as said below
- box_widths: int32 [4], replicated, may hold values from 1 to 8, as said below
Outputs:
- significance: float32 [128, 4, 96, 512], P(None, None, 'tm', 'wide')
Inputs may be any that keep to these rules, and one draw needn't show every extreme that they name: `band_widths`: the widths sum to 256; some band has exactly 64 channels. `delays`: the value 7 occurs in every draw. `box_widths`: the value 8 occurs in every draw.
All inputs are finite; a program needn't handle non-finite values.
Results may differ from a plain program's by a relative error of at most 0.0003.
The roundings to bfloat16 on the way count: a program that leaves them out, or rounds other values in their place, can miss the bound.
Values may be sent and summed in bfloat16 or wider, within the bound.
No kernel may reach another device: no remote copies, remote signals or barrier semaphores. Data moves between devices by JAX's collectives and lax.ppermute only.
A program may use at most 128 MiB of HBM per device.

v0:
```python
import math

import jax
import jax.numpy as jnp
from jax import lax
from jax.sharding import PartitionSpec as P

MAXDELAY = 7
WMAX = 8


def shifted(value, axis, by):
    devices = lax.axis_size(axis)
    return lax.ppermute(value, axis, [(i, (i + by) % devices) for i in range(devices)])


def dft_table(channel_rows):
    positions = jnp.arange(channel_rows, dtype=jnp.int32)
    product = positions[:, None] * positions[None, :] % channel_rows
    angles = 2.0 * math.pi / channel_rows * product.astype(jnp.float32)
    cosine = jnp.cos(angles)
    sines = jnp.sin(angles)
    upper_rows = jnp.concatenate([cosine, -sines], axis=1)
    lower_rows = jnp.concatenate([sines, cosine], axis=1)
    return jnp.stack([upper_rows, lower_rows]).astype(jnp.bfloat16)


def beam_weights(channel_ids, steering, channel_rows):
    frequency = 1.0 + channel_ids.astype(jnp.float32) / channel_rows
    phases = 2.0 * math.pi * (frequency[:, None, None] * steering[None, :, :])
    return jnp.concatenate([jnp.cos(phases), jnp.sin(phases)], axis=1).astype(jnp.bfloat16)


def beam_power(products, beam_count):
    real_in = products[:, :, 0, :]
    imag_in = products[:, :, 1, :]
    beam_real = real_in[..., :beam_count] + imag_in[..., beam_count:]
    beam_imag = imag_in[..., :beam_count] - real_in[..., beam_count:]
    return beam_real * beam_real + beam_imag * beam_imag


def body(voltages, fir_taps, steering, band_widths, delays, box_widths):
    subband_count = lax.axis_size("wide")
    own_band = lax.axis_index("wide")
    antenna_local = voltages.shape[1]
    antenna_full = steering.shape[1]
    beam_count = steering.shape[0]
    beam_dev = beam_count // subband_count
    filter_tap_count = fir_taps.shape[0]
    channel_rows = fir_taps.shape[1]
    sample_count = voltages.shape[2]
    frame_rows = sample_count // channel_rows
    total_frames = frame_rows * lax.axis_size("tm")
    trials = delays.shape[0]
    lookback = (filter_tap_count - 1) * channel_rows
    earlier = shifted(voltages[:, :, sample_count - lookback :], "tm", 1)
    extended = jnp.concatenate([earlier, voltages], axis=2).reshape(
        2, antenna_local, frame_rows + filter_tap_count - 1, channel_rows
    )
    filter_output = jnp.zeros((2, antenna_local, frame_rows, channel_rows), jnp.float32)
    for tap_index in range(filter_tap_count):
        start_frame = filter_tap_count - 1 - tap_index
        filter_output = (
            filter_output
            + fir_taps[tap_index] * extended[:, :, start_frame : start_frame + frame_rows, :]
        )
    filter_output = filter_output.astype(jnp.bfloat16)
    spectrum_rows = jnp.einsum(
        "pafn,pnq->afq", filter_output, dft_table(channel_rows), preferred_element_type=jnp.float32
    )
    spectrum_rows = spectrum_rows.astype(jnp.bfloat16).reshape(
        antenna_local, frame_rows, 2, channel_rows
    )
    starts = jnp.cumsum(band_widths) - band_widths
    band_index = jnp.arange(subband_count, dtype=jnp.int32)
    delay_slot_count = 2 * channel_rows // subband_count
    offsets = jnp.arange(delay_slot_count, dtype=jnp.int32)
    send_ids = starts[:, None] + offsets[None, :]
    send_valid = (offsets[None, :] < band_widths[:, None]).astype(jnp.float32)
    send_clipped = jnp.minimum(send_ids, channel_rows - 1)
    own_ids = jnp.take(send_clipped, own_band, axis=0)
    own_valid = jnp.take(send_valid, own_band, axis=0)
    packed = jnp.take(spectrum_rows, send_clipped.reshape(-1), axis=3).reshape(
        antenna_local, frame_rows, 2, subband_count, delay_slot_count
    )
    received = lax.all_to_all(packed, "wide", split_axis=3, concat_axis=0, tiled=True).reshape(
        antenna_full, frame_rows, 2, delay_slot_count
    )
    group_size = math.gcd(delay_slot_count, 4)

    def form_group(group_index):
        first_slot = group_index * group_size
        gathered = lax.dynamic_slice_in_dim(received, first_slot, group_size, axis=3)
        slot_ids = lax.dynamic_slice_in_dim(own_ids, first_slot, group_size, axis=0)
        weights = beam_weights(slot_ids, steering, channel_rows)
        products = jnp.einsum(
            "afpm,mya->mfpy", gathered, weights, preferred_element_type=jnp.float32
        )
        return beam_power(products, beam_count)

    powers = lax.map(form_group, jnp.arange(delay_slot_count // group_size, dtype=jnp.int32))
    powers = powers.reshape(delay_slot_count, frame_rows, beam_count) * own_valid[:, None, None]
    slot_band = jnp.sum((own_ids[:, None] >= starts[None, :]).astype(jnp.int32), axis=1) - 1
    band_onehot = (slot_band[:, None] == band_index[None, :]).astype(jnp.float32)
    slot_sums = jnp.sum(powers, axis=(1, 2))
    partial_bands = jnp.sum(slot_sums[:, None] * band_onehot, axis=0)
    band_total = lax.psum(partial_bands, ("wide", "tm"))
    band_mean = band_total / (band_widths.astype(jnp.float32) * (total_frames * beam_count))
    slot_mean = jnp.sum(band_onehot * band_mean[None, :], axis=1)
    levels = (powers / slot_mean[:, None, None]).astype(jnp.bfloat16)
    outgoing = levels.reshape(delay_slot_count, frame_rows, subband_count, beam_dev)
    arrived = lax.all_to_all(outgoing, "wide", split_axis=2, concat_axis=0, tiled=True).reshape(
        subband_count * delay_slot_count, frame_rows, beam_dev
    )
    reach_frames = MAXDELAY + WMAX - 1
    following = shifted(arrived[:, :reach_frames, :], "tm", -1)
    timeline = jnp.concatenate([arrived, following], axis=1)
    span_frames = frame_rows + WMAX - 1
    stacked = jnp.stack(
        [
            timeline[:, delay_step : delay_step + span_frames, :]
            for delay_step in range(MAXDELAY + 1)
        ]
    )
    stacked = stacked.reshape(
        (MAXDELAY + 1) * subband_count * delay_slot_count, span_frames * beam_dev
    )
    slot_delays = jnp.take(delays, send_clipped.reshape(-1), axis=1)
    delay_values = jnp.arange(MAXDELAY + 1, dtype=jnp.int32)
    selector = (slot_delays[:, None, :] == delay_values[None, :, None]) & (
        send_valid.reshape(-1)[None, None, :] > 0.0
    )
    selector = selector.astype(jnp.bfloat16).reshape(
        trials, (MAXDELAY + 1) * subband_count * delay_slot_count
    )
    dedispersed = jnp.dot(selector, stacked, preferred_element_type=jnp.float32).reshape(
        trials, span_frames, beam_dev
    )
    window = jnp.zeros((trials, box_widths.shape[0], frame_rows, beam_dev), jnp.float32)
    for lag_frames in range(WMAX):
        inside = (box_widths > lag_frames).astype(jnp.float32)
        window = (
            window
            + inside[None, :, None, None]
            * dedispersed[:, None, lag_frames : lag_frames + frame_rows, :]
        )
    expected = box_widths.astype(jnp.float32) * channel_rows
    return (window - expected[None, :, None, None]) / jnp.sqrt(expected)[None, :, None, None]


def solution(mesh):
    return jax.shard_map(
        body,
        mesh=mesh,
        in_specs=(P(None, "wide", "tm"), P(), P(), P(), P(), P()),
        out_specs=P(None, None, "tm", "wide"),
        check_vma=False,
    )
```

profile of v0, /device:TPU:1, one launch (start us, length us, event | category | flops | bytes accessed | tf_op | source)
XLA Modules:
  0.0 1765.7 jit_solution(9458910041901085709)
XLA Ops:
  0.0 8.7 copy.74
  24.7 8.5 bitcast_convert_fusion
  33.3 9.7 reshape.241
  43.0 11.9 copy.77
  54.9 17.9 %gather_fusion.1 = bf16[512,256,24,2]{1,2,3,0:T(8,128)(2,1)} fusion(bf16[256,24,2,256]{0,1,2,3:T(8,128)(2,1)} %copy.77, s32[1024]{0:T(1024)S(1)} %pad_clamp_fusion), kind=kCustom, calls=%fused_computation.1 | custom fusion | bytes 25167872 | tf_op jit(solution)/shard_map/jit(_take)/gather | solution.py:83
  72.8 7.9 copy.78
  93.9 271.1 %all-to-all-done = bf16[256,24,2,8,64]{0,4,2,1,3:T(8,128)(2,1)} async-done(((bf16[256,24,2,8,64]{0,4,2,1,3:T(8,128)(2,1)}), bf16[256,24,2,8,64]{0,4,2,1,3:T(8,128)(2,1)}, u32[]{:S(2)}, u32[]{:S(2)}) %all-to-all-start) | async-done | bytes 12582944 | tf_op jit(solution)/shard_map/all_to_all | solution.py:86
  365.0 14.1 copy.88
  379.1 19.6 %reshape.321 = bf16[2048,24,2,64]{0,1,2,3:T(8,128)(2,1)} reshape(bf16[8,256,24,2,1,64]{1,0,2,3,5,4:T(8,128)(2,1)} %copy.88) | data formatting | bytes 25165824 | tf_op jit(solution)/shard_map/while | solution.py:101
  398.6 1177.5 %while.12 = (s32[]{:T(128)}, f32[16,4,24,512]{3,2,1,0:T(8,128)S(1)}, s32[16]{0:T(128)S(1)}, bf16[2048,24,2,64]{0,1,2,3:T(8,128)(2,1)}, s32[64]{0:T(128)S(1)}, /*...) while((s32[]{:T(128)}, f32[16,4,24,512]{3,2,1,0:T(8,128)S(1)}, ...), condition=%wide.region_2.3_spmd, body=%wide.region_1.2_spmd.sunk | while | flops 855883776 | bytes 41877724 | solution.py:101
  400.1 64.4 %cosine_convert_fusion.3 = (bf16[4,512,2048]{2,1,0:T(8,128)(2,1)S(1)}, bf16[4,512,2048]{2,1,0:T(8,128)(2,1)}) fusion(f32[512,2048]{1,0:T(8,128)} %get-tuple-element.200, f32[4]{0:T(128)S(1)} %multiply_add_fusion.2), kind=kLoop, calls=%fused_computation.4.clone.1 | loop fusion | flops 16777216 | bytes 20971536 | tf_op jit(solution)/shard_map/convert
  464.4 7.6 fusion.52
  473.6 64.4 %cosine_convert_fusion.3 = (bf16[4,512,2048]{2,1,0:T(8,128)(2,1)S(1)}, bf16[4,512,2048]{2,1,0:T(8,128)(2,1)}) fusion(f32[512,2048]{1,0:T(8,128)} %get-tuple-element.200, f32[4]{0:T(128)S(1)} %multiply_add_fusion.2), kind=kLoop, calls=%fused_computation.4.clone.1 | loop fusion | flops 16777216 | bytes 20971536 | tf_op jit(solution)/shard_map/convert
  538.0 7.6 fusion.52
  547.2 64.4 %cosine_convert_fusion.3 = (bf16[4,512,2048]{2,1,0:T(8,128)(2,1)S(1)}, bf16[4,512,2048]{2,1,0:T(8,128)(2,1)}) fusion(f32[512,2048]{1,0:T(8,128)} %get-tuple-element.200, f32[4]{0:T(128)S(1)} %multiply_add_fusion.2), kind=kLoop, calls=%fused_computation.4.clone.1 | loop fusion | flops 16777216 | bytes 20971536 | tf_op jit(solution)/shard_map/convert
  611.6 7.6 fusion.52
  620.8 64.4 %cosine_convert_fusion.3 = (bf16[4,512,2048]{2,1,0:T(8,128)(2,1)S(1)}, bf16[4,512,2048]{2,1,0:T(8,128)(2,1)}) fusion(f32[512,2048]{1,0:T(8,128)} %get-tuple-element.200, f32[4]{0:T(128)S(1)} %multiply_add_fusion.2), kind=kLoop, calls=%fused_computation.4.clone.1 | loop fusion | flops 16777216 | bytes 20971536 | tf_op jit(solution)/shard_map/convert
  685.2 7.6 fusion.52
  694.4 64.4 %cosine_convert_fusion.3 = (bf16[4,512,2048]{2,1,0:T(8,128)(2,1)S(1)}, bf16[4,512,2048]{2,1,0:T(8,128)(2,1)}) fusion(f32[512,2048]{1,0:T(8,128)} %get-tuple-element.200, f32[4]{0:T(128)S(1)} %multiply_add_fusion.2), kind=kLoop, calls=%fused_computation.4.clone.1 | loop fusion | flops 16777216 | bytes 20971536 | tf_op jit(solution)/shard_map/convert
  758.8 7.6 fusion.52
  768.0 64.4 %cosine_convert_fusion.3 = (bf16[4,512,2048]{2,1,0:T(8,128)(2,1)S(1)}, bf16[4,512,2048]{2,1,0:T(8,128)(2,1)}) fusion(f32[512,2048]{1,0:T(8,128)} %get-tuple-element.200, f32[4]{0:T(128)S(1)} %multiply_add_fusion.2), kind=kLoop, calls=%fused_computation.4.clone.1 | loop fusion | flops 16777216 | bytes 20971536 | tf_op jit(solution)/shard_map/convert
  832.4 7.6 fusion.52
  841.6 64.4 %cosine_convert_fusion.3 = (bf16[4,512,2048]{2,1,0:T(8,128)(2,1)S(1)}, bf16[4,512,2048]{2,1,0:T(8,128)(2,1)}) fusion(f32[512,2048]{1,0:T(8,128)} %get-tuple-element.200, f32[4]{0:T(128)S(1)} %multiply_add_fusion.2), kind=kLoop, calls=%fused_computation.4.clone.1 | loop fusion | flops 16777216 | bytes 20971536 | tf_op jit(solution)/shard_map/convert
  906.0 7.6 fusion.52
  915.2 64.4 %cosine_convert_fusion.3 = (bf16[4,512,2048]{2,1,0:T(8,128)(2,1)S(1)}, bf16[4,512,2048]{2,1,0:T(8,128)(2,1)}) fusion(f32[512,2048]{1,0:T(8,128)} %get-tuple-element.200, f32[4]{0:T(128)S(1)} %multiply_add_fusion.2), kind=kLoop, calls=%fused_computation.4.clone.1 | loop fusion | flops 16777216 | bytes 20971536 | tf_op jit(solution)/shard_map/convert
  979.6 7.6 fusion.52
  988.8 64.4 %cosine_convert_fusion.3 = (bf16[4,512,2048]{2,1,0:T(8,128)(2,1)S(1)}, bf16[4,512,2048]{2,1,0:T(8,128)(2,1)}) fusion(f32[512,2048]{1,0:T(8,128)} %get-tuple-element.200, f32[4]{0:T(128)S(1)} %multiply_add_fusion.2), kind=kLoop, calls=%fused_computation.4.clone.1 | loop fusion | flops 16777216 | bytes 20971536 | tf_op jit(solution)/shard_map/convert
  1053.2 7.6 fusion.52
  1062.4 64.4 %cosine_convert_fusion.3 = (bf16[4,512,2048]{2,1,0:T(8,128)(2,1)S(1)}, bf16[4,512,2048]{2,1,0:T(8,128)(2,1)}) fusion(f32[512,2048]{1,0:T(8,128)} %get-tuple-element.200, f32[4]{0:T(128)S(1)} %multiply_add_fusion.2), kind=kLoop, calls=%fused_computation.4.clone.1 | loop fusion | flops 16777216 | bytes 20971536 | tf_op jit(solution)/shard_map/convert
  1126.8 7.6 fusion.52
  1136.0 64.4 %cosine_convert_fusion.3 = (bf16[4,512,2048]{2,1,0:T(8,128)(2,1)S(1)}, bf16[4,512,2048]{2,1,0:T(8,128)(2,1)}) fusion(f32[512,2048]{1,0:T(8,128)} %get-tuple-element.200, f32[4]{0:T(128)S(1)} %multiply_add_fusion.2), kind=kLoop, calls=%fused_computation.4.clone.1 | loop fusion | flops 16777216 | bytes 20971536 | tf_op jit(solution)/shard_map/convert
  1200.4 7.6 fusion.52
  1209.6 64.4 %cosine_convert_fusion.3 = (bf16[4,512,2048]{2,1,0:T(8,128)(2,1)S(1)}, bf16[4,512,2048]{2,1,0:T(8,128)(2,1)}) fusion(f32[512,2048]{1,0:T(8,128)} %get-tuple-element.200, f32[4]{0:T(128)S(1)} %multiply_add_fusion.2), kind=kLoop, calls=%fused_computation.4.clone.1 | loop fusion | flops 16777216 | bytes 20971536 | tf_op jit(solution)/shard_map/convert
  1274.0 7.6 fusion.52
  1283.2 64.4 %cosine_convert_fusion.3 = (bf16[4,512,2048]{2,1,0:T(8,128)(2,1)S(1)}, bf16[4,512,2048]{2,1,0:T(8,128)(2,1)}) fusion(f32[512,2048]{1,0:T(8,128)} %get-tuple-element.200, f32[4]{0:T(128)S(1)} %multiply_add_fusion.2), kind=kLoop, calls=%fused_computation.4.clone.1 | loop fusion | flops 16777216 | bytes 20971536 | tf_op jit(solution)/shard_map/convert
  1347.6 7.6 fusion.52
  1356.8 64.4 %cosine_convert_fusion.3 = (bf16[4,512,2048]{2,1,0:T(8,128)(2,1)S(1)}, bf16[4,512,2048]{2,1,0:T(8,128)(2,1)}) fusion(f32[512,2048]{1,0:T(8,128)} %get-tuple-element.200, f32[4]{0:T(128)S(1)} %multiply_add_fusion.2), kind=kLoop, calls=%fused_computation.4.clone.1 | loop fusion | flops 16777216 | bytes 20971536 | tf_op jit(solution)/shard_map/convert
  1421.2 7.6 fusion.52
  1430.4 64.4 %cosine_convert_fusion.3 = (bf16[4,512,2048]{2,1,0:T(8,128)(2,1)S(1)}, bf16[4,512,2048]{2,1,0:T(8,128)(2,1)}) fusion(f32[512,2048]{1,0:T(8,128)} %get-tuple-element.200, f32[4]{0:T(128)S(1)} %multiply_add_fusion.2), kind=kLoop, calls=%fused_computation.4.clone.1 | loop fusion | flops 16777216 | bytes 20971536 | tf_op jit(solution)/shard_map/convert
  1494.8 7.6 fusion.52
  1504.0 64.4 %cosine_convert_fusion.3 = (bf16[4,512,2048]{2,1,0:T(8,128)(2,1)S(1)}, bf16[4,512,2048]{2,1,0:T(8,128)(2,1)}) fusion(f32[512,2048]{1,0:T(8,128)} %get-tuple-element.200, f32[4]{0:T(128)S(1)} %multiply_add_fusion.2), kind=kLoop, calls=%fused_computation.4.clone.1 | loop fusion | flops 16777216 | bytes 20971536 | tf_op jit(solution)/shard_map/convert
  1568.4 7.6 fusion.52
  1580.3 38.6 %psum.7 = f32[8]{0:T(128)S(1)} all-reduce(f32[8]{0:T(128)S(1)} %select_reduce_fusion.1), channel_id=1, replica_groups=mesh['wide'=8,'tm'=4] {'wide','tm'}, use_global_device_ids=true, to_apply=%region_6.7 | all-reduce | flops 8 | bytes 64 | tf_op jit(solution)/shard_map/psum | solution.py:107
  1626.7 7.0 reshape.329
  1633.7 14.7 all-to-all-start.1
  1649.7 33.6 %all-to-all-done.1 = bf16[8,2,49152]{2,1,0:T(2,128)(2,1)} async-done(((bf16[8,2,49152]{2,1,0:T(2,128)(2,1)}), bf16[8,2,49152]{2,1,0:T(2,128)(2,1)}, u32[]{:S(2)}, u32[]{:S(2)}) %all-to-all-start.1) | async-done | bytes 1572896 | tf_op jit(solution)/shard_map/all_to_all | solution.py:112
  1703.1 9.0 collective-permute-done.1
  1713.9 37.3 %copy.84 = bf16[8,512,31,64]{1,0,3,2:T(8,128)(2,1)S(1)} copy(bf16[8,512,31,64]{1,3,2,0:T(8,128)(2,1)S(1)} %fusion.19) | data formatting | bytes 32505856 | tf_op jit(solution)/shard_map/stack | solution.py:119
  (137 shorter events, 91.7 us)
Async XLA Ops:
  0.0 13.5 copy-start.3
  0.0 15.1 copy-start.1
  9.9 11.6 collective-permute-start
  87.7 277.3 %all-to-all-start = ((bf16[256,24,2,8,64]{0,4,2,1,3:T(8,128)(2,1)}), bf16[256,24,2,8,64]{0,4,2,1,3:T(8,128)(2,1)}, u32[]{:S(2)}, u32[]{:S(2)}) async-start(bf16[256,24,2,8,64]{0,4,2,1,3:T(8,128)(2,1)} %copy.79), calls=%async_computation | async-start | bytes 25165824 | tf_op jit(solution)/shard_map/all_to_all | solution.py:86
  1622.9 25.6 %copy-start = (s32[128,256]{1,0:T(8,128)S(1)}, s32[128,256]{1,0:T(8,128)}, u32[]{:S(2)}) copy-start(s32[128,256]{1,0:T(8,128)} %param.12) | copy-start | bytes 393220
  1633.7 49.6 %all-to-all-start.1 = ((bf16[8,2,49152]{2,1,0:T(2,128)(2,1)}), bf16[8,2,49152]{2,1,0:T(2,128)(2,1)}, u32[]{:S(2)}, u32[]{:S(2)}) async-start(bf16[8,2,49152]{2,1,0:T(2,128)(2,1)} %reshape.329), calls=%async_computation.1 | async-start | bytes 3145728 | tf_op jit(solution)/shard_map/all_to_all | solution.py:112
  1692.5 9.0 copy-start.2
  1696.7 15.5 collective-permute-start.1
where the time goes:
time: 1770 us
  other arithmetic  1050 us (59%)
  waiting for transfers between devices  320 us (18%)
  local copies, waits for them, and re-layouts  185 us (10%)
  matrix products  135 us (8%)
  blocking collectives  38.6 us (2%)
  starting transfers between devices  26.8 us (2%)
    another operation x19, other arithmetic  1030 us
    all_to_all x1, waiting for transfers between devices, body(): lax.all_to_all(packed, 'wide', split_axis=3, concat_axis=0, tiled=True)  271 us
    dot_general x16, matrix products, form_group(): jnp.einsum('afpm,mya->mfpy', gathered, weights, preferred_element_type=jn...  122 us
    psum x1, blocking collectives, body(): band_total = lax.psum(partial_bands, ('wide', 'tm'))  38.6 us
    another operation x2, local copies, waits for them, and re-layouts, body(): jnp.stack([timeline[:, delay_step:delay_step + span_frames, :] for delay_...  37.5 us
  transfers between devices with their start and end apart: 4, of which 4 were waited for; matrix products, arithmetic and copies ran while one was open for 0% of the time, Pallas kernels for 0%

commit v1 on v0

v1 whole, which is shorter than its diff:
```python
import functools
import math

import jax
import jax.numpy as jnp
import numpy as np
from jax import lax
from jax.experimental import pallas as pl
from jax.experimental.pallas import tpu as pltpu
from jax.sharding import PartitionSpec as P

MAXDELAY = 7
WMAX = 8
AXES = ("wide", "tm")
MIB = 1 << 20


def dft_rows(channel_rows):
    positions = np.arange(channel_rows, dtype=np.int64)
    product = (positions[:, None] * positions[None, :] % channel_rows).astype(np.float32)
    angles = np.float32(2.0 * math.pi / channel_rows) * product
    cosine = np.cos(angles.astype(np.float64)).astype(np.float32)
    sines = np.sin(angles.astype(np.float64)).astype(np.float32)
    real_rows = np.concatenate([cosine.T, sines.T], axis=1)
    imag_rows = np.concatenate([-sines.T, cosine.T], axis=1)
    rows = np.stack([real_rows, imag_rows], axis=1).reshape(2 * channel_rows, 2 * channel_rows)
    return rows.astype(jnp.bfloat16)


def spectra_kernel(taps_ref, table_ref, halo_ref, volt_ref, out_ref, ring_ref, part_ref):
    taps = taps_ref.shape[0]
    width = taps_ref.shape[1]
    frame = pl.program_id(0) * 8 + pl.program_id(1)
    inner = pl.program_id(1)

    @pl.when(frame == 0)
    def _():
        for back in range(1, taps):
            ring_ref[(taps - back) % taps] = halo_ref[
                :, :, (taps - 1 - back) * width : (taps - back) * width
            ]

    ring_ref[frame % taps] = volt_ref[...]
    pieces = []
    for part in range(2):
        total = None
        for back in range(taps):
            value = ring_ref[(frame + taps - back) % taps, part].astype(jnp.float32)
            term = taps_ref[back : back + 1, :] * value
            total = term if total is None else total + term
        pieces.append(total.astype(jnp.bfloat16))
    filtered = jnp.concatenate(pieces, axis=1)
    spectrum = lax.dot_general(
        table_ref[...], filtered, (((1,), (1,)), ((), ())), preferred_element_type=jnp.float32
    )
    rows, antennas = spectrum.shape
    lanes = part_ref.shape[0] * 128
    if lanes > antennas:
        spectrum = jnp.concatenate(
            [spectrum, jnp.zeros((rows, lanes - antennas), jnp.float32)], axis=1
        )
    for half in range(lanes // 128):
        part_ref[half, pl.ds(inner, rows, stride=8), :] = spectrum[:, half * 128 : half * 128 + 128]

    @pl.when(inner == 7)
    def _():
        for half in range(lanes // 128):
            size = min(128, antennas - half * 128)
            value = part_ref[half].astype(jnp.bfloat16).reshape(rows // 2, 16, 128)
            out_ref[:, 0, :, half * 128 : half * 128 + size] = value[:, :, :size]


def spectra(voltages, halo, fir_taps):
    taps, width = fir_taps.shape
    antennas = voltages.shape[1]
    frames = voltages.shape[2] // width
    groups = frames // 8
    table = jnp.asarray(dft_rows(width))
    return pl.pallas_call(
        spectra_kernel,
        grid=(groups, 8),
        in_specs=[
            pl.BlockSpec(fir_taps.shape, lambda g, i: (0, 0)),
            pl.BlockSpec(table.shape, lambda g, i: (0, 0)),
            pl.BlockSpec(halo.shape, lambda g, i: (0, 0, 0)),
            pl.BlockSpec((2, antennas, width), lambda g, i: (0, 0, g * 8 + i)),
        ],
        out_specs=pl.BlockSpec((width, 1, 16, antennas), lambda g, i: (0, g, 0, 0)),
        out_shape=jax.ShapeDtypeStruct((width, groups, 16, antennas), jnp.bfloat16),
        scratch_shapes=[
            pltpu.VMEM((taps, 2, antennas, width), jnp.bfloat16),
            pltpu.VMEM((-(-antennas // 128), 2 * width * 8, 128), jnp.float32),
        ],
        compiler_params=pltpu.CompilerParams(vmem_limit_bytes=48 * MIB),
        cost_estimate=pl.CostEstimate(
            flops=2 * frames * antennas * 4 * width * width,
            bytes_accessed=8 * frames * antennas * width,
            transcendentals=0,
        ),
        name="spectra",
    )(fir_taps, table, halo, voltages)


def sincos(phase):
    turns = jnp.round(phase * np.float32(1.0 / (2.0 * math.pi)))
    high = np.float32(6.28125)
    middle = np.float32(np.round((2.0 * math.pi - 6.28125) * 2.0**26) / 2.0**26)
    low = np.float32(2.0 * math.pi - 6.28125 - float(middle))
    rest = phase - turns * high
    rest = rest - turns * middle
    rest = rest - turns * low
    square = rest * rest
    s = np.float32(SIN_COEF[-1])
    for value in SIN_COEF[-2::-1]:
        s = s * square + np.float32(value)
    s = s * rest
    c = np.float32(COS_COEF[-1])
    for value in COS_COEF[-2::-1]:
        c = c * square + np.float32(value)
    return np.float32(1.0) - s * s, s * c


def half_angle_coefficients():
    top = (math.pi + 0.01) ** 2
    nodes = (np.cos((np.arange(400) + 0.5) * math.pi / 400) + 1.0) * 0.5 * top
    root = np.sqrt(nodes)
    fits = []
    for values, order in (
        (math.sqrt(2.0) * np.sin(root / 2) / root, 5),
        (math.sqrt(2.0) * np.cos(root / 2), 6),
    ):
        fit = np.polynomial.chebyshev.Chebyshev.fit(nodes, values, order - 1, domain=[0.0, top])
        fits.append([float(v) for v in fit.convert(kind=np.polynomial.Polynomial).coef])
    return fits


SIN_COEF, COS_COEF = half_angle_coefficients()


def weights_kernel(freq_ref, steer_ref, out_ref):
    channel = pl.program_id(1)
    beams = steer_ref.shape[1]
    frequency = freq_ref[channel]
    rows = steer_ref.shape[0]

    def step(index, carry):
        at = pl.ds(pl.multiple_of(index * 16, 16), 16)
        phase = np.float32(2.0 * math.pi) * (frequency * steer_ref[at, :])
        cosine, sines = sincos(phase)
        out_ref[0, at, :beams] = cosine.astype(jnp.bfloat16)
        out_ref[0, at, beams:] = sines.astype(jnp.bfloat16)
        return carry

    lax.fori_loop(0, rows // 16, step, 0)


def beam_weights(frequency, steering_t):
    antennas, beams = steering_t.shape
    channels = frequency.shape[0]
    block = min(512, antennas)
    return pl.pallas_call(
        weights_kernel,
        grid=(antennas // block, channels),
        in_specs=[
            pl.BlockSpec(memory_space=pltpu.SMEM),
            pl.BlockSpec((block, beams), lambda a, c: (a, 0)),
        ],
        out_specs=pl.BlockSpec((1, block, 2 * beams), lambda a, c: (c, a, 0)),
        out_shape=jax.ShapeDtypeStruct((channels, antennas, 2 * beams), jnp.bfloat16),
        compiler_params=pltpu.CompilerParams(vmem_limit_bytes=32 * MIB),
        cost_estimate=pl.CostEstimate(
            flops=30 * channels * antennas * beams,
            bytes_accessed=4 * channels * antennas * beams,
            transcendentals=2 * channels * antennas * beams,
        ),
        name="weights",
    )(frequency, steering_t)


def beam_kernel(wide, tm, data_ref, weight_ref, power_ref, sum_ref, gather_ref, acc_ref):
    channel = pl.program_id(0)
    groups = data_ref.shape[2]
    antennas = data_ref.shape[4]
    rows = groups * 16
    for w in range(wide):
        for m in range(tm):
            gather_ref[m * rows : (m + 1) * rows, w * antennas : (w + 1) * antennas] = data_ref[
                w * tm + m, 0
            ].reshape(rows, antennas)
    products = jnp.dot(gather_ref[...], weight_ref[0], preferred_element_type=jnp.float32)
    beams = products.shape[1] // 2
    products = products.reshape(tm * groups, 2, 8, 2 * beams)
    real_in = products[:, 0]
    imag_in = products[:, 1]
    beam_real = real_in[..., :beams] + imag_in[..., beams:]
    beam_imag = imag_in[..., :beams] - real_in[..., beams:]
    power = beam_real * beam_real + beam_imag * beam_imag
    power_ref[0] = power.reshape(tm * groups * 8, beams)
    total = jnp.sum(jnp.sum(power, axis=0), axis=(0, 1), keepdims=True)
    lane = lax.broadcasted_iota(jnp.int32, acc_ref.shape, 1)

    @pl.when(channel == 0)
    def _():
        acc_ref[...] = jnp.zeros_like(acc_ref)

    acc_ref[...] = jnp.where(lane == channel, total, acc_ref[...])

    @pl.when(channel == pl.num_programs(0) - 1)
    def _():
        sum_ref[...] = jnp.broadcast_to(acc_ref[...], sum_ref.shape)


def form_beams(received, weights, wide, tm):
    devices, channels, groups, _, antennas = received.shape
    _, antenna_full, twice = weights.shape
    frames = tm * groups * 8
    beams = twice // 2
    return pl.pallas_call(
        functools.partial(beam_kernel, wide, tm),
        grid=(channels,),
        in_specs=[
            pl.BlockSpec((devices, 1, groups, 16, antennas), lambda c: (0, c, 0, 0, 0)),
            pl.BlockSpec((1, antenna_full, twice), lambda c: (c, 0, 0)),
        ],
        out_specs=[
            pl.BlockSpec((1, frames, beams), lambda c: (c, 0, 0)),
            pl.BlockSpec((devices, 128), lambda c: (0, 0)),
        ],
        out_shape=[
            jax.ShapeDtypeStruct((channels, frames, beams), jnp.float32),
            jax.ShapeDtypeStruct((devices, 128), jnp.float32),
        ],
        scratch_shapes=[
            pltpu.VMEM((2 * frames, antenna_full), jnp.bfloat16),
            pltpu.VMEM((1, 128), jnp.float32),
        ],
        compiler_params=pltpu.CompilerParams(vmem_limit_bytes=48 * MIB),
        cost_estimate=pl.CostEstimate(
            flops=4 * channels * frames * antenna_full * twice,
            bytes_accessed=2 * channels * antenna_full * twice,
            transcendentals=0,
        ),
        name="beams",
    )(received, weights)


def level_kernel(wide, tm, reach, mask_ref, count_ref, sums_ref, power_ref, out_ref):
    channels, frames, beams = power_ref.shape
    own_beams = beams // wide
    own_frames = frames // tm
    per_row = max(1, 128 // own_beams)
    sums = sums_ref[...]
    means = []
    for c in range(channels):
        means.append(jnp.sum(jnp.sum(mask_ref[c] * sums, axis=0, keepdims=True), axis=1, keepdims=True))
    mean = jnp.concatenate(means, axis=0) / count_ref[...]
    span = own_frames + reach

    def level(f):
        value = jnp.concatenate([power_ref[c, f : f + 1, :] for c in range(channels)], axis=0)
        return (value / mean).astype(jnp.bfloat16)

    for start in range(0, frames, per_row):
        values = [level(f) for f in range(start, start + per_row)]
        for w in range(wide):
            piece = jnp.concatenate(
                [v[:, w * own_beams : (w + 1) * own_beams] for v in values], axis=1
            )
            for m in range(tm):
                for lap in (0, frames):
                    at = start + lap - m * own_frames
                    if 0 <= at < span:
                        width = min(per_row, span - at) * own_beams
                        out_ref[w * tm + m, :, at * own_beams : at * own_beams + width] = piece[
                            :, :width
                        ]


def form_levels(mask, count, sums, powers, wide, tm, reach):
    channels, frames, beams = powers.shape
    span = frames // tm + reach
    lanes = span * (beams // wide)
    return pl.pallas_call(
        functools.partial(level_kernel, wide, tm, reach),
        out_shape=jax.ShapeDtypeStruct((wide * tm, channels, lanes), jnp.bfloat16),
        compiler_params=pltpu.CompilerParams(vmem_limit_bytes=48 * MIB),
        name="levels",
    )(mask, count, sums, powers)


def search_kernel(own_frames, width_ref, pick_ref, level_ref, out_ref, acc_ref):
    trials = pick_ref.shape[1]
    widths = out_ref.shape[1]
    beams = out_ref.shape[3]
    channels = pick_ref.shape[2]
    span = (own_frames + WMAX - 1) * beams
    for delay in range(MAXDELAY + 1):
        value = jnp.dot(
            pick_ref[delay],
            level_ref[:, delay * beams : delay * beams + span],
            preferred_element_type=jnp.float32,
        )
        if delay == 0:
            acc_ref[...] = value
        else:
            acc_ref[...] += value
    window = own_frames * beams
    shifts = [acc_ref[:, lag * beams : lag * beams + window] for lag in range(WMAX)]
    for i in range(widths):
        total = shifts[0]
        for lag in range(1, WMAX):
            inside = (width_ref[i] > lag).astype(jnp.float32)
            total = total + inside * shifts[lag]
        expected = width_ref[i].astype(jnp.float32) * np.float32(channels)
        root = jnp.sqrt(jnp.full((1, window), expected, jnp.float32))
        result = (total - expected) / root
        for f in range(own_frames):
            out_ref[:, i, f, :] = result[:, f * beams : (f + 1) * beams]


def search(box_widths, picks, levels, own_frames, own_beams):
    trials = picks.shape[1]
    widths = box_widths.shape[0]
    return pl.pallas_call(
        functools.partial(search_kernel, own_frames),
        in_specs=[
            pl.BlockSpec(memory_space=pltpu.SMEM),
            pl.BlockSpec(memory_space=pltpu.VMEM),
            pl.BlockSpec(memory_space=pltpu.VMEM),
        ],
        out_shape=jax.ShapeDtypeStruct((trials, widths, own_frames, own_beams), jnp.float32),
        scratch_shapes=[pltpu.VMEM((trials, (own_frames + WMAX - 1) * own_beams), jnp.float32)],
        compiler_params=pltpu.CompilerParams(vmem_limit_bytes=48 * MIB),
        name="search",
    )(box_widths, picks, levels)


def exchange(value):
    return lax.all_to_all(value, AXES, split_axis=0, concat_axis=0, tiled=True)


def body(voltages, fir_taps, steering, band_widths, delays, box_widths):
    wide = lax.axis_size("wide")
    tm = lax.axis_size("tm")
    devices = wide * tm
    taps, channel_rows = fir_taps.shape
    antenna_local = voltages.shape[1]
    beam_count = steering.shape[0]
    sample_count = voltages.shape[2]
    frame_rows = sample_count // channel_rows
    total_frames = frame_rows * tm
    slots = channel_rows // devices
    own = lax.axis_index("wide") * tm + lax.axis_index("tm")
    own_ids = own * slots + jnp.arange(slots, dtype=jnp.int32)

    lookback = (taps - 1) * channel_rows
    halo = lax.ppermute(
        voltages[:, :, sample_count - lookback :], "tm", [(i, (i + 1) % tm) for i in range(tm)]
    )
    outgoing = spectra(voltages, halo, fir_taps)
    groups = frame_rows // 8
    received = exchange(outgoing.reshape(devices, slots * groups * 16, antenna_local))
    received = received.reshape(devices, slots, groups, 16, antenna_local)

    frequency = 1.0 + own_ids.astype(jnp.float32) / channel_rows
    weights = beam_weights(frequency, steering.T)
    powers, sums = form_beams(received, weights, wide, tm)

    starts = jnp.cumsum(band_widths) - band_widths
    ids = jnp.arange(channel_rows, dtype=jnp.int32)
    bands = jnp.sum((ids[:, None] >= starts[None, :]).astype(jnp.int32), axis=1) - 1
    own_band = jnp.sum((own_ids[:, None] >= starts[None, :]).astype(jnp.int32), axis=1) - 1
    mask = (own_band[:, None] == bands[None, :]).astype(jnp.float32)
    mask = jnp.pad(mask.reshape(slots, devices, slots), ((0, 0), (0, 0), (0, 128 - slots)))
    count = jnp.sum(
        jnp.where(
            own_band[:, None] == jnp.arange(band_widths.shape[0], dtype=jnp.int32)[None, :],
            band_widths.astype(jnp.float32)[None, :] * (total_frames * beam_count),
            0.0,
        ),
        axis=1,
        keepdims=True,
    )
    reach = MAXDELAY + WMAX - 1
    levels = form_levels(mask, count, exchange(sums), powers, wide, tm, reach)
    arrived = exchange(levels).reshape(channel_rows, levels.shape[2])

    steps = jnp.arange(MAXDELAY + 1, dtype=jnp.int32)
    picks = (delays[None, :, :] == steps[:, None, None]).astype(jnp.bfloat16)
    return search(box_widths, picks, arrived, frame_rows, beam_count // wide)


def solution(mesh):
    return jax.shard_map(
        body,
        mesh=mesh,
        in_specs=(P(None, "wide", "tm"), P(), P(), P(), P(), P()),
        out_specs=P(None, None, "tm", "wide"),
        check_vma=False,
    )
```

time: 1770 us -> 269 us (0.15)
  other arithmetic: 1050 us -> 0.87 us
  waiting for transfers between devices: 320 us -> 124 us
  local copies, waits for them, and re-layouts: 185 us -> 17.3 us
  matrix products: 135 us -> 0 us
  Pallas kernels: 0 us -> 108 us
  blocking collectives: 38.6 us -> 0 us
    another operation x20 -> x1, other arithmetic: 1030 us -> 0.18 us
    all_to_all x2 -> x3, waiting for transfers between devices: 305 us -> 116 us  [exchange(): return lax.all_to_all(value, AXES, split_axis=0, concat_axis=0, tiled=True)]
    dot_general x18 -> x0, matrix products: 135 us -> none  [the longest x16 122 us: form_group(): jnp.einsum('afpm,mya->mfpy', gathered, weights, preferred_element_type=jn...]
    pallas_call x0 -> x5, Pallas kernels: none -> 108 us  [the longest x1 51.5 us: beam_weights(): pl.pallas_call(weights_kernel, grid=(antennas // block, channels), in_spe...]
    psum x1 -> x0, blocking collectives: 38.6 us -> none  [body(): band_total = lax.psum(partial_bands, ('wide', 'tm'))]
    another operation x2 -> x0, local copies, waits for them, and re-layouts: 37.5 us -> none  [body(): jnp.stack([timeline[:, delay_step:delay_step + span_frames, :] for delay_...]
    while x2 -> x0, local copies, waits for them, and re-layouts: 33.6 us -> none  [body(): lax.map(form_group, jnp.arange(delay_slot_count // group_size, dtype=jnp....]
    reshape x4 -> x0, local copies, waits for them, and re-layouts: 28 us -> none  [the longest x2 21.6 us: body(): spectrum_rows.astype(jnp.bfloat16)]
  transfers between devices with their start and end apart: 4 -> 4, of which waited for: 4 -> 4; matrix products, arithmetic and copies ran while one was open for 0% -> 2% of each run, Pallas kernels for 0% -> 19%
where the time goes in v1:
time: 269 us; the launch traced here: 267 us
  waiting for transfers between devices  124 us (46%)
  Pallas kernels  108 us (40%)
  local copies, waits for them, and re-layouts  17.3 us (6%)
  starting transfers between devices  16.1 us (6%)
    all_to_all x3, waiting for transfers between devices, exchange(): return lax.all_to_all(value, AXES, split_axis=0, concat_axis=0, tiled=True)  116 us
    pallas_call x1, Pallas kernels, beam_weights(): pl.pallas_call(weights_kernel, grid=(antennas // block, channels), in_spe...  51.5 us
    pallas_call x1, Pallas kernels, spectra(): pl.pallas_call(spectra_kernel, grid=(groups, 8), in_specs=[pl.BlockSpec(f...  21.6 us
    pallas_call x1, Pallas kernels, form_beams(): pl.pallas_call(functools.partial(beam_kernel, wide, tm), grid=(channels,)...  17.1 us
    pallas_call x1, Pallas kernels, search(): pl.pallas_call(functools.partial(search_kernel, own_frames), in_specs=[pl...  15.8 us
    all_to_all x3, starting transfers between devices, exchange(): return lax.all_to_all(value, AXES, split_axis=0, concat_axis=0, tiled=True)  13.4 us
    unnamed x13, local copies, waits for them, and re-layouts  9.29 us
    ppermute x1, waiting for transfers between devices, body(): lax.ppermute(voltages[:, :, sample_count - lookback:], 'tm', [(i, (i + 1)...  8.93 us
  transfers between devices with their start and end apart: 4, of which 4 were waited for; matrix products, arithmetic and copies ran while one was open for 2% of the time, Pallas kernels for 19%

profile of v1, /device:TPU:1, one launch (start us, length us, event | category | flops | bytes accessed | tf_op | source)
XLA Modules:
  0.0 266.8 jit_solution(12542693264362825757)
XLA Ops:
  0.0 1.2 slice.3
  1.2 2.7 collective-permute-start
  3.8 8.9 %collective-permute-done.halo_ref = bf16[2,256,768]{2,1,0:T(8,128)(2,1)S(1)} collective-permute-done((bf16[2,256,768]{2,1,0:T(8,128)(2,1)S(1)}, bf16[2,256,768]{2,1,0:T(8,128)(2,1)S(1)}, u32[]{:S(2)}, u32[]{:S(2)}) %collective-permute-start) | collective-permute-done | bytes 786464 | tf_op jit(solution)/shard_map/ppermute | solution.py:357
  12.8 0.0 copy-start.1
  12.8 1.0 copy-done.1
  13.8 0.0 copy-start.2
  13.8 0.7 copy-done.2
  14.5 21.6 %spectra.1 = bf16[256,3,16,256]{3,2,1,0:T(8,128)(2,1)} custom-call(f32[4,256]{1,0:T(4,128)S(1)} %copy-done.2, bf16[512,512]{1,0:T(8,128)(2,1)S(1)} %copy-done.1, bf16[2,256,768]{2,1,0:T(8,128)(2,1)S(1)} %collective-permute-done.halo_ref, bf16[2,256,6144]{2,1,0:T(8,128)(2,1)} %volt_ref.1), custom_call_target="tpu_custom_call" | custom-call | flops 3221225472 | bytes 12582912 | tf_op jit(solution)/shard_map/spectra/pallas_call | solution.py:79
  36.1 0.0 copy-start.5
  36.1 7.0 %all-to-all-start = ((bf16[32,384,256]{2,1,0:T(8,128)(2,1)}), bf16[32,384,256]{2,1,0:T(8,128)(2,1)}, u32[]{:S(2)}, u32[]{:S(2)}) async-start(bf16[32,384,256]{2,1,0:T(8,128)(2,1)} %bitcast.15), calls=%async_computation | async-start | bytes 12582912 | tf_op jit(solution)/shard_map/all_to_all | solution.py:339
  43.1 0.0 copy-done.5
  43.1 0.2 reduce-window.9
  43.3 0.1 convert_reduce_fusion
  43.4 0.1 sub.15
  43.5 5.4 %copy.18 = f32[512,2048]{0,1:T(8,128)} copy(f32[512,2048]{1,0:T(8,128)} %param.9) | data formatting | bytes 8388608 | tf_op args[2]
  48.9 0.0 copy-start
  48.9 2.2 copy-done
  51.0 51.5 %weights.1.weight_ref = bf16[8,2048,1024]{2,1,0:T(8,128)(2,1)} custom-call(f32[8]{0:T(128)S(1)} %multiply_add_fusion.freq_ref, f32[2048,512]{1,0:T(8,128)S(1)} %bitcast.12), custom_call_target="tpu_custom_call" | custom-call | flops 251658240 | bytes 33554432 | tf_op jit(solution)/shard_map/weights/pallas_call | solution.py:161
  102.6 0.2 convert_reduce_fusion.1
  102.8 0.1 broadcast_compare_fusion
  102.9 79.7 %all-to-all-done = bf16[32,384,256]{2,1,0:T(8,128)(2,1)} async-done(((bf16[32,384,256]{2,1,0:T(8,128)(2,1)}), bf16[32,384,256]{2,1,0:T(8,128)(2,1)}, u32[]{:S(2)}, u32[]{:S(2)}) %all-to-all-start) | async-done | bytes 6291488 | tf_op jit(solution)/shard_map/all_to_all | solution.py:339
  182.6 17.1 %beams.1 = (f32[8,96,512]{2,1,0:T(8,128)S(1)}, f32[32,128]{1,0:T(8,128)}) custom-call(bf16[32,8,3,16,256]{4,3,2,1,0:T(8,128)(2,1)} %bitcast.4.data_ref, bf16[8,2048,1024]{2,1,0:T(8,128)(2,1)} %weights.1.weight_ref), custom_call_target="tpu_custom_call" | custom-call | flops 6442450944 | bytes 33554432 | tf_op jit(solution)/shard_map/beams/pallas_call | solution.py:218
  199.6 0.0 copy-start.4
  199.6 0.0 copy-start.3
  199.6 3.3 %all-to-all-start.1 = ((f32[32,1,128]{2,1,0:T(1,128)}), f32[32,1,128]{2,1,0:T(1,128)S(1)}, u32[]{:S(2)}, u32[]{:S(2)}) async-start(f32[32,1,128]{2,1,0:T(1,128)} %bitcast.7), calls=%async_computation.1 | async-start | bytes 32768 | tf_op jit(solution)/shard_map/all_to_all | solution.py:339
  203.0 0.2 select_reduce_fusion
  203.2 0.1 copy.20.count_ref
  203.2 6.4 %all-to-all-done.1 = f32[32,1,128]{2,1,0:T(1,128)S(1)} async-done(((f32[32,1,128]{2,1,0:T(1,128)}), f32[32,1,128]{2,1,0:T(1,128)S(1)}, u32[]{:S(2)}, u32[]{:S(2)}) %all-to-all-start.1) | async-done | bytes 16416 | tf_op jit(solution)/shard_map/all_to_all | solution.py:339
  209.7 2.0 levels.1
  211.6 3.1 %all-to-all-start.2 = ((bf16[32,8,2432]{2,1,0:T(8,128)(2,1)}), bf16[32,8,2432]{2,1,0:T(8,128)(2,1)S(1)}, u32[]{:S(2)}, u32[]{:S(2)}) async-start(bf16[32,8,2432]{2,1,0:T(8,128)(2,1)} %levels.1), calls=%async_computation.2 | async-start | bytes 2490368 | tf_op jit(solution)/shard_map/all_to_all | solution.py:339
  214.7 0.0 copy-done.4
  214.7 0.1 fusion.pick_ref
  214.8 29.4 %all-to-all-done.2 = bf16[32,8,2432]{2,1,0:T(8,128)(2,1)S(1)} async-done(((bf16[32,8,2432]{2,1,0:T(8,128)(2,1)}), bf16[32,8,2432]{2,1,0:T(8,128)(2,1)S(1)}, u32[]{:S(2)}, u32[]{:S(2)}) %all-to-all-start.2) | async-done | bytes 1245216 | tf_op jit(solution)/shard_map/all_to_all | solution.py:339
  244.3 0.0 copy-done.3
  244.3 15.8 %search.1 = f32[128,4,24,64]{3,2,1,0:T(8,128)} custom-call(s32[4]{0:T(128)S(1)} %copy-done.3, bf16[8,128,256]{2,1,0:T(8,128)(2,1)S(1)} %fusion.pick_ref, bf16[256,2432]{1,0:T(8,128)(2,1)S(1)} %bitcast.13), custom_call_target="tpu_custom_call" | custom-call | tf_op jit(solution)/shard_map/search/pallas_call | solution.py:324
  260.1 6.7 %copy.21 = f32[128,4,24,64]{0,3,2,1:T(8,128)} copy(f32[128,4,24,64]{3,2,1,0:T(8,128)} %search.1) | data formatting | bytes 6291456 | tf_op jit(solution)/shard_map/search/pallas_call | solution.py:324
  (6 shorter events, 0.0 us)
Async XLA Ops:
  1.2 11.6 %collective-permute-start = (bf16[2,256,768]{2,1,0:T(8,128)(2,1)S(1)}, bf16[2,256,768]{2,1,0:T(8,128)(2,1)S(1)}, u32[]{:S(2)}, u32[]{:S(2)}) collective-permute-start(bf16[2,256,768]{2,1,0:T(8,128)(2,1)S(1)} %slice.3), channel_id=1, source_target_pairs={{0,1},{1,2},{2,3},{3,0},{4,5},{5,6},{6,7},{7,4},{8,9},{9,10},{10,1... | collective-permute-start | bytes 2359304 | tf_op jit(solution)/shard_map/ppermute | solution.py:357
  12.8 1.0 copy-start.1
  13.8 0.7 copy-start.2
  36.1 7.0 %copy-start.5 = (s32[8]{0:T(128)S(1)}, s32[8]{0:T(128)}, u32[]{:S(2)}) copy-start(s32[8]{0:T(128)} %param.10) | copy-start | bytes 100
  36.1 146.5 %all-to-all-start = ((bf16[32,384,256]{2,1,0:T(8,128)(2,1)}), bf16[32,384,256]{2,1,0:T(8,128)(2,1)}, u32[]{:S(2)}, u32[]{:S(2)}) async-start(bf16[32,384,256]{2,1,0:T(8,128)(2,1)} %bitcast.15), calls=%async_computation | async-start | bytes 12582912 | tf_op jit(solution)/shard_map/all_to_all | solution.py:339
  48.9 2.2 copy-start
  199.6 15.1 %copy-start.4 = (s32[128,256]{1,0:T(8,128)S(1)}, s32[128,256]{1,0:T(8,128)}, u32[]{:S(2)}) copy-start(s32[128,256]{1,0:T(8,128)} %param.11) | copy-start | bytes 393220
  199.6 44.6 %copy-start.3 = (s32[4]{0:T(128)S(1)}, s32[4]{0:T(128)}, u32[]{:S(2)}) copy-start(s32[4]{0:T(128)} %width_ref.1) | copy-start | bytes 52
  199.6 10.0 %all-to-all-start.1 = ((f32[32,1,128]{2,1,0:T(1,128)}), f32[32,1,128]{2,1,0:T(1,128)S(1)}, u32[]{:S(2)}, u32[]{:S(2)}) async-start(f32[32,1,128]{2,1,0:T(1,128)} %bitcast.7), calls=%async_computation.1 | async-start | bytes 32768 | tf_op jit(solution)/shard_map/all_to_all | solution.py:339
  211.6 32.6 %all-to-all-start.2 = ((bf16[32,8,2432]{2,1,0:T(8,128)(2,1)}), bf16[32,8,2432]{2,1,0:T(8,128)(2,1)S(1)}, u32[]{:S(2)}, u32[]{:S(2)}) async-start(bf16[32,8,2432]{2,1,0:T(8,128)(2,1)} %levels.1), calls=%async_computation.2 | async-start | bytes 2490368 | tf_op jit(solution)/shard_map/all_to_all | solution.py:339

commit v2 on v1

--- a/solution.py
+++ b/solution.py
@@ -27,78 +27,80 @@
     return rows.astype(jnp.bfloat16)
 
 
-def spectra_kernel(taps_ref, table_ref, halo_ref, volt_ref, out_ref, ring_ref, part_ref):
+def spectra_kernel(skip, taps_ref, table_ref, past_ref, volt_ref, *rest):
+    out_ref, part_ref = rest[-2:]
     taps = taps_ref.shape[0]
     width = taps_ref.shape[1]
-    frame = pl.program_id(0) * 8 + pl.program_id(1)
-    inner = pl.program_id(1)
-
-    @pl.when(frame == 0)
-    def _():
-        for back in range(1, taps):
-            ring_ref[(taps - back) % taps] = halo_ref[
-                :, :, (taps - 1 - back) * width : (taps - back) * width
+    for inner in range(8):
+        pieces = []
+        for part in range(2):
+            total = None
+            for back in range(taps):
+                if inner >= back:
+                    at = (inner - back) * width
+                    value = volt_ref[part, :, at : at + width]
+                else:
+                    at = skip + (taps - 1 + inner - back) * width
+                    value = past_ref[part, :, at : at + width]
+                term = taps_ref[back : back + 1, :] * value.astype(jnp.float32)
+                total = term if total is None else total + term
+            pieces.append(total.astype(jnp.bfloat16))
+        filtered = jnp.concatenate(pieces, axis=1)
+        spectrum = lax.dot_general(
+            table_ref[...], filtered, (((1,), (1,)), ((), ())), preferred_element_type=jnp.float32
+        )
+        rows, antennas = spectrum.shape
+        lanes = part_ref.shape[0] * 128
+        if lanes > antennas:
+            spectrum = jnp.concatenate(
+                [spectrum, jnp.zeros((rows, lanes - antennas), jnp.float32)], axis=1
+            )
+        for half in range(lanes // 128):
+            part_ref[half, pl.ds(inner, rows, stride=8), :] = spectrum[
+                :, half * 128 : half * 128 + 128
             ]
-
-    ring_ref[frame % taps] = volt_ref[...]
-    pieces = []
-    for part in range(2):
-        total = None
-        for back in range(taps):
-            value = ring_ref[(frame + taps - back) % taps, part].astype(jnp.float32)
-            term = taps_ref[back : back + 1, :] * value
-            total = term if total is None else total + term
-        pieces.append(total.astype(jnp.bfloat16))
-    filtered = jnp.concatenate(pieces, axis=1)
-    spectrum = lax.dot_general(
-        table_ref[...], filtered, (((1,), (1,)), ((), ())), preferred_element_type=jnp.float32
-    )
-    rows, antennas = spectrum.shape
-    lanes = part_ref.shape[0] * 128
-    if lanes > antennas:
-        spectrum = jnp.concatenate(
-            [spectrum, jnp.zeros((rows, lanes - antennas), jnp.float32)], axis=1
-        )
     for half in range(lanes // 128):
-        part_ref[half, pl.ds(inner, rows, stride=8), :] = spectrum[:, half * 128 : half * 128 + 128]
-
-    @pl.when(inner == 7)
-    def _():
-        for half in range(lanes // 128):
-            size = min(128, antennas - half * 128)
-            value = part_ref[half].astype(jnp.bfloat16).reshape(rows // 2, 16, 128)
-            out_ref[:, 0, :, half * 128 : half * 128 + size] = value[:, :, :size]
-
-
-def spectra(voltages, halo, fir_taps):
+        size = min(128, antennas - half * 128)
+        value = part_ref[half].astype(jnp.bfloat16).reshape(rows // 2, 16, 128)
+        out_ref[:, 0, :, half * 128 : half * 128 + size] = value[:, :, :size]
+
+
+def spectra(table, past, voltages, fir_taps, earlier=None):
     taps, width = fir_taps.shape
     antennas = voltages.shape[1]
-    frames = voltages.shape[2] // width
-    groups = frames // 8
-    table = jnp.asarray(dft_rows(width))
+    groups = voltages.shape[2] // (8 * width)
+    first = 1 if earlier is None else 0
+    steps = groups - 1 if earlier is None else 1
+    operands = [fir_taps, table, past, voltages]
+    in_specs = [
+        pl.BlockSpec(fir_taps.shape, lambda g: (0, 0)),
+        pl.BlockSpec(table.shape, lambda g: (0, 0)),
+        pl.BlockSpec((2, antennas, 4 * width), lambda g: (0, 0, 2 * g + 1))
+        if earlier is None
+        else pl.BlockSpec(past.shape, lambda g: (0, 0, 0)),
+        pl.BlockSpec((2, antennas, 8 * width), lambda g: (0, 0, g + first)),
+    ]
+    if earlier is not None:
+        operands.append(earlier)
+        in_specs.append(pl.BlockSpec(memory_space=pl.ANY))
     return pl.pallas_call(
-        spectra_kernel,
-        grid=(groups, 8),
-        in_specs=[
-            pl.BlockSpec(fir_taps.shape, lambda g, i: (0, 0)),
-            pl.BlockSpec(table.shape, lambda g, i: (0, 0)),
-            pl.BlockSpec(halo.shape, lambda g, i: (0, 0, 0)),
-            pl.BlockSpec((2, antennas, width), lambda g, i: (0, 0, g * 8 + i)),
-        ],
-        out_specs=pl.BlockSpec((width, 1, 16, antennas), lambda g, i: (0, g, 0, 0)),
+        functools.partial(spectra_kernel, (5 - taps) * width if earlier is None else 0),
+        grid=(steps,),
+        in_specs=in_specs,
+        out_specs=pl.BlockSpec((width, 1, 16, antennas), lambda g: (0, g + first, 0, 0)),
         out_shape=jax.ShapeDtypeStruct((width, groups, 16, antennas), jnp.bfloat16),
         scratch_shapes=[
-            pltpu.VMEM((taps, 2, antennas, width), jnp.bfloat16),
             pltpu.VMEM((-(-antennas // 128), 2 * width * 8, 128), jnp.float32),
         ],
+        input_output_aliases={} if earlier is None else {4: 0},
         compiler_params=pltpu.CompilerParams(vmem_limit_bytes=48 * MIB),
         cost_estimate=pl.CostEstimate(
-            flops=2 * frames * antennas * 4 * width * width,
-            bytes_accessed=8 * frames * antennas * width,
+            flops=64 * steps * antennas * width * width,
+            bytes_accessed=64 * steps * antennas * width,
             transcendentals=0,
         ),
         name="spectra",
-    )(fir_taps, table, halo, voltages)
+    )(*operands)
 
 
 def sincos(phase):
@@ -288,48 +290,56 @@
     )(mask, count, sums, powers)
 
 
-def search_kernel(own_frames, width_ref, pick_ref, level_ref, out_ref, acc_ref):
-    trials = pick_ref.shape[1]
-    widths = out_ref.shape[1]
-    beams = out_ref.shape[3]
-    channels = pick_ref.shape[2]
-    span = (own_frames + WMAX - 1) * beams
-    for delay in range(MAXDELAY + 1):
-        value = jnp.dot(
-            pick_ref[delay],
-            level_ref[:, delay * beams : delay * beams + span],
-            preferred_element_type=jnp.float32,
+def search_kernel(own_frames, own_beams, width_ref, pick_ref, level_ref, out_ref, turn_ref, sum_ref):
+    widths = out_ref.shape[0]
+    channels, lanes = level_ref.shape
+    delays = MAXDELAY + 1
+    frames = own_frames + WMAX - 1
+    for start in range(0, lanes, 128):
+        stop = min(start + 128, lanes)
+        turn_ref[start:stop, :] = level_ref[:, start:stop].T
+    chunk = 8
+    for start in range(0, frames, chunk):
+        stop = min(start + chunk, frames)
+        held = jnp.concatenate(
+            [
+                turn_ref[(start + d) * own_beams : (stop + d) * own_beams, :]
+                for d in range(delays)
+            ],
+            axis=1,
         )
-        if delay == 0:
-            acc_ref[...] = value
-        else:
-            acc_ref[...] += value
-    window = own_frames * beams
-    shifts = [acc_ref[:, lag * beams : lag * beams + window] for lag in range(WMAX)]
+        value = jnp.dot(held, pick_ref[...], preferred_element_type=jnp.float32)
+        sum_ref[0, start * own_beams : stop * own_beams, :] = value
+    window = own_frames * own_beams
+    for at in range(0, own_frames, 4):
+        rows = pl.ds(at * own_beams, 4 * own_beams)
+        total = sum_ref[0, rows, :]
+        for lag in range(1, WMAX):
+            total = total + sum_ref[0, pl.ds((at + lag) * own_beams, 4 * own_beams), :]
+            sum_ref[lag, rows, :] = total
     for i in range(widths):
-        total = shifts[0]
-        for lag in range(1, WMAX):
-            inside = (width_ref[i] > lag).astype(jnp.float32)
-            total = total + inside * shifts[lag]
         expected = width_ref[i].astype(jnp.float32) * np.float32(channels)
-        root = jnp.sqrt(jnp.full((1, window), expected, jnp.float32))
-        result = (total - expected) / root
-        for f in range(own_frames):
-            out_ref[:, i, f, :] = result[:, f * beams : (f + 1) * beams]
+        root = jnp.sqrt(jnp.full((1, out_ref.shape[2]), expected, jnp.float32))
+        out_ref[i] = (sum_ref[width_ref[i] - 1, :window, :] - expected) / root
 
 
 def search(box_widths, picks, levels, own_frames, own_beams):
     trials = picks.shape[1]
+    channels, lanes = levels.shape
     widths = box_widths.shape[0]
+    frames = own_frames + WMAX - 1
     return pl.pallas_call(
-        functools.partial(search_kernel, own_frames),
+        functools.partial(search_kernel, own_frames, own_beams),
         in_specs=[
             pl.BlockSpec(memory_space=pltpu.SMEM),
             pl.BlockSpec(memory_space=pltpu.VMEM),
             pl.BlockSpec(memory_space=pltpu.VMEM),
         ],
-        out_shape=jax.ShapeDtypeStruct((trials, widths, own_frames, own_beams), jnp.float32),
-        scratch_shapes=[pltpu.VMEM((trials, (own_frames + WMAX - 1) * own_beams), jnp.float32)],
+        out_shape=jax.ShapeDtypeStruct((widths, own_frames * own_beams, trials), jnp.float32),
+        scratch_shapes=[
+            pltpu.VMEM((lanes, channels), jnp.bfloat16),
+            pltpu.VMEM((WMAX, frames * own_beams, trials), jnp.float32),
+        ],
         compiler_params=pltpu.CompilerParams(vmem_limit_bytes=48 * MIB),
         name="search",
     )(box_widths, picks, levels)
@@ -357,7 +367,9 @@
     halo = lax.ppermute(
         voltages[:, :, sample_count - lookback :], "tm", [(i, (i + 1) % tm) for i in range(tm)]
     )
-    outgoing = spectra(voltages, halo, fir_taps)
+    table = jnp.asarray(dft_rows(channel_rows))
+    outgoing = spectra(table, voltages, voltages, fir_taps)
+    outgoing = spectra(table, halo, voltages, fir_taps, outgoing)
     groups = frame_rows // 8
     received = exchange(outgoing.reshape(devices, slots * groups * 16, antenna_local))
     received = received.reshape(devices, slots, groups, 16, antenna_local)
@@ -386,8 +398,12 @@
     arrived = exchange(levels).reshape(channel_rows, levels.shape[2])
 
     steps = jnp.arange(MAXDELAY + 1, dtype=jnp.int32)
-    picks = (delays[None, :, :] == steps[:, None, None]).astype(jnp.bfloat16)
-    return search(box_widths, picks, arrived, frame_rows, beam_count // wide)
+    picks = (delays.T[None, :, :] == steps[:, None, None]).astype(jnp.bfloat16)
+    picks = picks.reshape((MAXDELAY + 1) * channel_rows, delays.shape[0])
+    own_beams = beam_count // wide
+    found = search(box_widths, picks, arrived, frame_rows, own_beams)
+    found = found.reshape(box_widths.shape[0], frame_rows, own_beams, delays.shape[0])
+    return found.transpose(3, 0, 1, 2)
 
 
 def solution(mesh):

time: 269 us -> 233 us (0.87)
  Pallas kernels: 108 us -> 88.9 us
  waiting for transfers between devices: 124 us -> 115 us
  local copies, waits for them, and re-layouts: 17.3 us -> 10.7 us
    pallas_call x2 -> x3, Pallas kernels: 37.4 us -> 18.4 us  [the longest x2 13.2 us: spectra(): pl.pallas_call(functools.partial(spectra_kernel, (5 - taps) * width if ea...]
    ppermute x1, waiting for transfers between devices: 8.93 us -> 0.01 us  [body(): lax.ppermute(voltages[:, :, sample_count - lookback:], 'tm', [(i, (i + 1)...]
    pallas_call x1 -> x0, local copies, waits for them, and re-layouts: 6.69 us -> none  [search(): pl.pallas_call(functools.partial(search_kernel, own_frames), in_specs=[pl...]
    unnamed x13 -> x15, local copies, waits for them, and re-layouts: 9.29 us -> 9.3 us
  transfers between devices with their start and end apart: 4 -> 4, of which waited for: 4 -> 3; matrix products, arithmetic and copies ran while one was open for 2% -> 3% of each run, Pallas kernels for 19% -> 26%
where the time goes in v2:
time: 233 us; the launch traced here: 231 us
  waiting for transfers between devices  115 us (49%)
  Pallas kernels  88.9 us (38%)
  starting transfers between devices  15.2 us (7%)
  local copies, waits for them, and re-layouts  10.7 us (5%)
    all_to_all x3, waiting for transfers between devices, exchange(): return lax.all_to_all(value, AXES, split_axis=0, concat_axis=0, tiled=True)  115 us
    pallas_call x1, Pallas kernels, beam_weights(): pl.pallas_call(weights_kernel, grid=(antennas // block, channels), in_spe...  51.5 us
    pallas_call x1, Pallas kernels, form_beams(): pl.pallas_call(functools.partial(beam_kernel, wide, tm), grid=(channels,)...  17.1 us
    pallas_call x2, Pallas kernels, spectra(): pl.pallas_call(functools.partial(spectra_kernel, (5 - taps) * width if ea...  13.2 us
    all_to_all x3, starting transfers between devices, exchange(): return lax.all_to_all(value, AXES, split_axis=0, concat_axis=0, tiled=True)  12.5 us
    unnamed x15, local copies, waits for them, and re-layouts  9.3 us
    pallas_call x1, Pallas kernels, search(): pl.pallas_call(functools.partial(search_kernel, own_frames, own_beams), i...  5.16 us
  transfers between devices with their start and end apart: 4, of which 3 were waited for; matrix products, arithmetic and copies ran while one was open for 3% of the time, Pallas kernels for 26%

profile of v2, /device:TPU:1, one launch (start us, length us, event | category | flops | bytes accessed | tf_op | source)
XLA Modules:
  0.0 231.4 jit_solution(16515549921190631934)
XLA Ops:
  0.0 1.2 slice.3
  1.2 2.7 %collective-permute-start = (bf16[2,256,768]{2,1,0:T(8,128)(2,1)S(1)}, bf16[2,256,768]{2,1,0:T(8,128)(2,1)S(1)}, u32[]{:S(2)}, u32[]{:S(2)}) collective-permute-start(bf16[2,256,768]{2,1,0:T(8,128)(2,1)S(1)} %slice.3), channel_id=1, source_target_pairs={{0,1},{1,2},{2,3},{3,0},{4,5},{5,6},{6,7},{7,4},{8,9},{9,10},{10,1... | collective-permute-start | bytes 2359304 | tf_op jit(solution)/shard_map/ppermute | solution.py:367
  3.8 0.0 copy-start.1
  3.8 1.0 copy-done.1
  4.9 0.0 copy-start.2
  4.9 0.7 copy-done.2
  5.6 7.9 %spectra.2.rest_0_ = bf16[256,3,16,256]{3,2,1,0:T(8,128)(2,1)} custom-call(f32[4,256]{1,0:T(4,128)S(1)} %copy-done.2, bf16[512,512]{1,0:T(8,128)(2,1)S(1)} %copy-done.1, bf16[2,256,6144]{2,1,0:T(8,128)(2,1)} %volt_ref.3, bf16[2,256,6144]{2,1,0:T(8,128)(2,1)} %volt_ref.3), custom_call_target="tpu_custom_call" | custom-call | flops 2147483648 | bytes 8388608 | tf_op jit(solution)/shard_map/spectra/pallas_call | solution.py:86
  13.5 0.0 collective-permute-done.past_ref
  13.5 5.3 %spectra.3 = bf16[256,3,16,256]{3,2,1,0:T(8,128)(2,1)} custom-call(f32[4,256]{1,0:T(4,128)S(1)} %copy-done.2, bf16[512,512]{1,0:T(8,128)(2,1)S(1)} %copy-done.1, bf16[2,256,768]{2,1,0:T(8,128)(2,1)S(1)} %collective-permute-done.past_ref, bf16[2,256,6144]{2,1,0:T(8,128)(2,1)} %volt_ref.3, ...), custom_call_target="tpu_custom_call", output_to_operand_aliasing={{}: (4, {})} | custom-call | flops 1073741824 | bytes 4194304 | tf_op jit(solution)/shard_map/spectra/pallas_call | solution.py:86
  18.8 0.0 copy-start.5
  18.8 6.3 %all-to-all-start = ((bf16[32,384,256]{2,1,0:T(8,128)(2,1)}), bf16[32,384,256]{2,1,0:T(8,128)(2,1)}, u32[]{:S(2)}, u32[]{:S(2)}) async-start(bf16[32,384,256]{2,1,0:T(8,128)(2,1)} %bitcast.26), calls=%async_computation | async-start | bytes 12582912 | tf_op jit(solution)/shard_map/all_to_all | solution.py:349
  25.1 0.0 copy-done.5
  25.1 0.2 reduce-window.9
  25.3 0.1 convert_reduce_fusion
  25.4 0.1 sub.15
  25.5 5.4 %copy.20 = f32[512,2048]{0,1:T(8,128)} copy(f32[512,2048]{1,0:T(8,128)} %param.9) | data formatting | bytes 8388608 | tf_op args[2]
  30.8 0.0 copy-start
  30.8 2.2 copy-done
  33.0 51.5 %weights.1.weight_ref = bf16[8,2048,1024]{2,1,0:T(8,128)(2,1)} custom-call(f32[8]{0:T(128)S(1)} %multiply_add_fusion.freq_ref, f32[2048,512]{1,0:T(8,128)S(1)} %bitcast.23), custom_call_target="tpu_custom_call" | custom-call | flops 251658240 | bytes 33554432 | tf_op jit(solution)/shard_map/weights/pallas_call | solution.py:163
  84.5 0.2 convert_reduce_fusion.1
  84.7 0.1 broadcast_compare_fusion
  84.9 79.7 %all-to-all-done = bf16[32,384,256]{2,1,0:T(8,128)(2,1)} async-done(((bf16[32,384,256]{2,1,0:T(8,128)(2,1)}), bf16[32,384,256]{2,1,0:T(8,128)(2,1)}, u32[]{:S(2)}, u32[]{:S(2)}) %all-to-all-start) | async-done | bytes 6291488 | tf_op jit(solution)/shard_map/all_to_all | solution.py:349
  164.6 17.1 %beams.1 = (f32[8,96,512]{2,1,0:T(8,128)S(1)}, f32[32,128]{1,0:T(8,128)}) custom-call(bf16[32,8,3,16,256]{4,3,2,1,0:T(8,128)(2,1)} %bitcast.6.data_ref, bf16[8,2048,1024]{2,1,0:T(8,128)(2,1)} %weights.1.weight_ref), custom_call_target="tpu_custom_call" | custom-call | flops 6442450944 | bytes 33554432 | tf_op jit(solution)/shard_map/beams/pallas_call | solution.py:220
  181.6 0.0 copy-start.4
  181.6 0.0 copy-start.3
  181.6 3.3 %all-to-all-start.1 = ((f32[32,1,128]{2,1,0:T(1,128)}), f32[32,1,128]{2,1,0:T(1,128)S(1)}, u32[]{:S(2)}, u32[]{:S(2)}) async-start(f32[32,1,128]{2,1,0:T(1,128)} %bitcast.9), calls=%async_computation.1 | async-start | bytes 32768 | tf_op jit(solution)/shard_map/all_to_all | solution.py:349
  184.9 0.2 select_reduce_fusion
  185.1 0.1 copy.22.count_ref
  185.2 6.4 %all-to-all-done.1 = f32[32,1,128]{2,1,0:T(1,128)S(1)} async-done(((f32[32,1,128]{2,1,0:T(1,128)}), f32[32,1,128]{2,1,0:T(1,128)S(1)}, u32[]{:S(2)}, u32[]{:S(2)}) %all-to-all-start.1) | async-done | bytes 16416 | tf_op jit(solution)/shard_map/all_to_all | solution.py:349
  191.6 2.0 levels.1
  193.6 2.9 %all-to-all-start.2 = ((bf16[32,8,2432]{2,1,0:T(8,128)(2,1)}), bf16[32,8,2432]{2,1,0:T(8,128)(2,1)S(1)}, u32[]{:S(2)}, u32[]{:S(2)}) async-start(bf16[32,8,2432]{2,1,0:T(8,128)(2,1)} %levels.1), calls=%async_computation.2 | async-start | bytes 2490368 | tf_op jit(solution)/shard_map/all_to_all | solution.py:349
  196.5 0.0 copy-done.4
  196.6 0.1 copy.19
  196.7 0.3 fusion.pick_ref
  197.0 29.2 %all-to-all-done.2 = bf16[32,8,2432]{2,1,0:T(8,128)(2,1)S(1)} async-done(((bf16[32,8,2432]{2,1,0:T(8,128)(2,1)}), bf16[32,8,2432]{2,1,0:T(8,128)(2,1)S(1)}, u32[]{:S(2)}, u32[]{:S(2)}) %all-to-all-start.2) | async-done | bytes 1245216 | tf_op jit(solution)/shard_map/all_to_all | solution.py:349
  226.2 0.0 copy-done.3
  226.2 5.2 %search.1 = f32[4,1536,128]{2,1,0:T(8,128)} custom-call(s32[4]{0:T(128)S(1)} %copy-done.3, bf16[2048,128]{1,0:T(8,128)(2,1)S(1)} %fusion.pick_ref, bf16[256,2432]{1,0:T(8,128)(2,1)S(1)} %bitcast.24), custom_call_target="tpu_custom_call" | custom-call | tf_op jit(solution)/shard_map/search/pallas_call | solution.py:331
  (8 shorter events, 0.1 us)
Async XLA Ops:
  1.2 12.3 %collective-permute-start = (bf16[2,256,768]{2,1,0:T(8,128)(2,1)S(1)}, bf16[2,256,768]{2,1,0:T(8,128)(2,1)S(1)}, u32[]{:S(2)}, u32[]{:S(2)}) collective-permute-start(bf16[2,256,768]{2,1,0:T(8,128)(2,1)S(1)} %slice.3), channel_id=1, source_target_pairs={{0,1},{1,2},{2,3},{3,0},{4,5},{5,6},{6,7},{7,4},{8,9},{9,10},{10,1... | collective-permute-start | bytes 2359304 | tf_op jit(solution)/shard_map/ppermute | solution.py:367
  3.8 1.0 copy-start.1
  4.9 0.7 copy-start.2
  18.8 6.3 %copy-start.5 = (s32[8]{0:T(128)S(1)}, s32[8]{0:T(128)}, u32[]{:S(2)}) copy-start(s32[8]{0:T(128)} %param.10) | copy-start | bytes 100
  18.8 145.8 %all-to-all-start = ((bf16[32,384,256]{2,1,0:T(8,128)(2,1)}), bf16[32,384,256]{2,1,0:T(8,128)(2,1)}, u32[]{:S(2)}, u32[]{:S(2)}) async-start(bf16[32,384,256]{2,1,0:T(8,128)(2,1)} %bitcast.26), calls=%async_computation | async-start | bytes 12582912 | tf_op jit(solution)/shard_map/all_to_all | solution.py:349
  30.8 2.2 copy-start
  181.6 14.9 %copy-start.4 = (s32[128,256]{1,0:T(8,128)S(1)}, s32[128,256]{1,0:T(8,128)}, u32[]{:S(2)}) copy-start(s32[128,256]{1,0:T(8,128)} %param.11) | copy-start | bytes 393220
  181.6 44.6 %copy-start.3 = (s32[4]{0:T(128)S(1)}, s32[4]{0:T(128)}, u32[]{:S(2)}) copy-start(s32[4]{0:T(128)} %width_ref.1) | copy-start | bytes 52
  181.6 10.0 %all-to-all-start.1 = ((f32[32,1,128]{2,1,0:T(1,128)}), f32[32,1,128]{2,1,0:T(1,128)S(1)}, u32[]{:S(2)}, u32[]{:S(2)}) async-start(f32[32,1,128]{2,1,0:T(1,128)} %bitcast.9), calls=%async_computation.1 | async-start | bytes 32768 | tf_op jit(solution)/shard_map/all_to_all | solution.py:349
  193.6 32.6 %all-to-all-start.2 = ((bf16[32,8,2432]{2,1,0:T(8,128)(2,1)}), bf16[32,8,2432]{2,1,0:T(8,128)(2,1)S(1)}, u32[]{:S(2)}, u32[]{:S(2)}) async-start(bf16[32,8,2432]{2,1,0:T(8,128)(2,1)} %levels.1), calls=%async_computation.2 | async-start | bytes 2490368 | tf_op jit(solution)/shard_map/all_to_all | solution.py:349

commit v3 on v2

--- a/solution.py
+++ b/solution.py
@@ -15,7 +15,12 @@
 MIB = 1 << 20
 
 
-def dft_rows(channel_rows):
+def slot_parts(slots):
+    late = max(1, slots // 8)
+    return slots - late, late
+
+
+def dft_rows(channel_rows, slots):
     positions = np.arange(channel_rows, dtype=np.int64)
     product = (positions[:, None] * positions[None, :] % channel_rows).astype(np.float32)
     angles = np.float32(2.0 * math.pi / channel_rows) * product
@@ -23,12 +28,17 @@
     sines = np.sin(angles.astype(np.float64)).astype(np.float32)
     real_rows = np.concatenate([cosine.T, sines.T], axis=1)
     imag_rows = np.concatenate([-sines.T, cosine.T], axis=1)
-    rows = np.stack([real_rows, imag_rows], axis=1).reshape(2 * channel_rows, 2 * channel_rows)
-    return rows.astype(jnp.bfloat16)
-
-
-def spectra_kernel(skip, taps_ref, table_ref, past_ref, volt_ref, *rest):
-    out_ref, part_ref = rest[-2:]
+    rows = np.stack([real_rows, imag_rows], axis=1).reshape(-1, slots, 2, 2 * channel_rows)
+    first = 0
+    ordered = []
+    for count in slot_parts(slots):
+        ordered.append(rows[:, first : first + count].reshape(-1, 2 * channel_rows))
+        first += count
+    return np.concatenate(ordered).astype(jnp.bfloat16)
+
+
+def spectra_kernel(skip, parts, taps_ref, table_ref, past_ref, volt_ref, *rest):
+    out_refs, part_ref = rest[-1 - parts : -1], rest[-1]
     taps = taps_ref.shape[0]
     width = taps_ref.shape[1]
     for inner in range(8):
@@ -61,11 +71,16 @@
             ]
     for half in range(lanes // 128):
         size = min(128, antennas - half * 128)
-        value = part_ref[half].astype(jnp.bfloat16).reshape(rows // 2, 16, 128)
-        out_ref[:, 0, :, half * 128 : half * 128 + size] = value[:, :, :size]
-
-
-def spectra(table, past, voltages, fir_taps, earlier=None):
+        first = 0
+        for out_ref in out_refs:
+            count = out_ref.shape[0]
+            value = part_ref[half, first * 16 : (first + count) * 16].astype(jnp.bfloat16)
+            value = value.reshape(count, 16, 128)
+            out_ref[:, 0, :, half * 128 : half * 128 + size] = value[:, :, :size]
+            first += count
+
+
+def spectra(counts, table, past, voltages, fir_taps, earlier=None):
     taps, width = fir_taps.shape
     antennas = voltages.shape[1]
     groups = voltages.shape[2] // (8 * width)
@@ -81,18 +96,25 @@
         pl.BlockSpec((2, antennas, 8 * width), lambda g: (0, 0, g + first)),
     ]
     if earlier is not None:
-        operands.append(earlier)
-        in_specs.append(pl.BlockSpec(memory_space=pl.ANY))
+        operands.extend(earlier)
+        in_specs.extend([pl.BlockSpec(memory_space=pl.ANY)] * len(counts))
     return pl.pallas_call(
-        functools.partial(spectra_kernel, (5 - taps) * width if earlier is None else 0),
+        functools.partial(
+            spectra_kernel, (5 - taps) * width if earlier is None else 0, len(counts)
+        ),
         grid=(steps,),
         in_specs=in_specs,
-        out_specs=pl.BlockSpec((width, 1, 16, antennas), lambda g: (0, g + first, 0, 0)),
-        out_shape=jax.ShapeDtypeStruct((width, groups, 16, antennas), jnp.bfloat16),
+        out_specs=[
+            pl.BlockSpec((count, 1, 16, antennas), lambda g: (0, g + first, 0, 0))
+            for count in counts
+        ],
+        out_shape=[
+            jax.ShapeDtypeStruct((count, groups, 16, antennas), jnp.bfloat16) for count in counts
+        ],
         scratch_shapes=[
             pltpu.VMEM((-(-antennas // 128), 2 * width * 8, 128), jnp.float32),
         ],
-        input_output_aliases={} if earlier is None else {4: 0},
+        input_output_aliases={} if earlier is None else {4 + i: i for i in range(len(counts))},
         compiler_params=pltpu.CompilerParams(vmem_limit_bytes=48 * MIB),
         cost_estimate=pl.CostEstimate(
             flops=64 * steps * antennas * width * width,
@@ -179,7 +201,7 @@
     )(frequency, steering_t)
 
 
-def beam_kernel(wide, tm, data_ref, weight_ref, power_ref, sum_ref, gather_ref, acc_ref):
+def beam_kernel(wide, tm, first, before_ref, data_ref, weight_ref, power_ref, sum_ref, gather_ref, acc_ref):
     channel = pl.program_id(0)
     groups = data_ref.shape[2]
     antennas = data_ref.shape[4]
@@ -203,26 +225,27 @@
 
     @pl.when(channel == 0)
     def _():
-        acc_ref[...] = jnp.zeros_like(acc_ref)
-
-    acc_ref[...] = jnp.where(lane == channel, total, acc_ref[...])
+        acc_ref[...] = before_ref[:1, :]
+
+    acc_ref[...] = jnp.where(lane == channel + first, total, acc_ref[...])
 
     @pl.when(channel == pl.num_programs(0) - 1)
     def _():
         sum_ref[...] = jnp.broadcast_to(acc_ref[...], sum_ref.shape)
 
 
-def form_beams(received, weights, wide, tm):
+def form_beams(received, weights, before, first, wide, tm):
     devices, channels, groups, _, antennas = received.shape
     _, antenna_full, twice = weights.shape
     frames = tm * groups * 8
     beams = twice // 2
     return pl.pallas_call(
-        functools.partial(beam_kernel, wide, tm),
+        functools.partial(beam_kernel, wide, tm, first),
         grid=(channels,),
         in_specs=[
+            pl.BlockSpec((devices, 128), lambda c: (0, 0)),
             pl.BlockSpec((devices, 1, groups, 16, antennas), lambda c: (0, c, 0, 0, 0)),
-            pl.BlockSpec((1, antenna_full, twice), lambda c: (c, 0, 0)),
+            pl.BlockSpec((1, antenna_full, twice), lambda c: (c + first, 0, 0)),
         ],
         out_specs=[
             pl.BlockSpec((1, frames, beams), lambda c: (c, 0, 0)),
@@ -243,11 +266,14 @@
             transcendentals=0,
         ),
         name="beams",
-    )(received, weights)
-
-
-def level_kernel(wide, tm, reach, mask_ref, count_ref, sums_ref, power_ref, out_ref):
-    channels, frames, beams = power_ref.shape
+    )(before, received, weights)
+
+
+def level_kernel(wide, tm, reach, mask_ref, count_ref, sums_ref, *refs):
+    power_refs, out_ref = refs[:-1], refs[-1]
+    channels = mask_ref.shape[0]
+    _, frames, beams = power_refs[0].shape
+    slots = [(ref, c) for ref in power_refs for c in range(ref.shape[0])]
     own_beams = beams // wide
     own_frames = frames // tm
     per_row = max(1, 128 // own_beams)
@@ -259,7 +285,7 @@
     span = own_frames + reach
 
     def level(f):
-        value = jnp.concatenate([power_ref[c, f : f + 1, :] for c in range(channels)], axis=0)
+        value = jnp.concatenate([ref[c, f : f + 1, :] for ref, c in slots], axis=0)
         return (value / mean).astype(jnp.bfloat16)
 
     for start in range(0, frames, per_row):
@@ -279,7 +305,8 @@
 
 
 def form_levels(mask, count, sums, powers, wide, tm, reach):
-    channels, frames, beams = powers.shape
+    channels = mask.shape[0]
+    _, frames, beams = powers[0].shape
     span = frames // tm + reach
     lanes = span * (beams // wide)
     return pl.pallas_call(
@@ -287,7 +314,7 @@
         out_shape=jax.ShapeDtypeStruct((wide * tm, channels, lanes), jnp.bfloat16),
         compiler_params=pltpu.CompilerParams(vmem_limit_bytes=48 * MIB),
         name="levels",
-    )(mask, count, sums, powers)
+    )(mask, count, sums, *powers)
 
 
 def search_kernel(own_frames, own_beams, width_ref, pick_ref, level_ref, out_ref, turn_ref, sum_ref):
@@ -367,16 +394,29 @@
     halo = lax.ppermute(
         voltages[:, :, sample_count - lookback :], "tm", [(i, (i + 1) % tm) for i in range(tm)]
     )
-    table = jnp.asarray(dft_rows(channel_rows))
-    outgoing = spectra(table, voltages, voltages, fir_taps)
-    outgoing = spectra(table, halo, voltages, fir_taps, outgoing)
+    parts = slot_parts(slots)
+    counts = [devices * part for part in parts]
+    table = pltpu.with_memory_space_constraint(
+        jnp.asarray(dft_rows(channel_rows, slots)), pltpu.HBM
+    )
+    fir_taps = pltpu.with_memory_space_constraint(fir_taps, pltpu.HBM)
+    outgoing = spectra(counts, table, voltages, voltages, fir_taps)
+    early, tail = spectra(counts, table, halo, voltages, fir_taps, outgoing)
     groups = frame_rows // 8
-    received = exchange(outgoing.reshape(devices, slots * groups * 16, antenna_local))
-    received = received.reshape(devices, slots, groups, 16, antenna_local)
+
+    def arrive(piece, part):
+        received = exchange(piece.reshape(devices, part * groups * 16, antenna_local))
+        return received.reshape(devices, part, groups, 16, antenna_local)
 
     frequency = 1.0 + own_ids.astype(jnp.float32) / channel_rows
+    early, frequency, steering = lax.optimization_barrier((early, frequency, steering))
     weights = beam_weights(frequency, steering.T)
-    powers, sums = form_beams(received, weights, wide, tm)
+    early = arrive(early, parts[0])
+    early, tail, weights = lax.optimization_barrier((early, tail, weights))
+    sums = jnp.zeros((devices, 128), jnp.float32)
+    power, sums = form_beams(early, weights, sums, 0, wide, tm)
+    late, sums = form_beams(arrive(tail, parts[1]), weights, sums, parts[0], wide, tm)
+    powers = [power, late]
 
     starts = jnp.cumsum(band_widths) - band_widths
     ids = jnp.arange(channel_rows, dtype=jnp.int32)

time: 233 us -> 227 us (0.974)
  waiting for transfers between devices: 115 us -> 104 us
  starting transfers between devices: 15.2 us -> 20.6 us
    all_to_all x3 -> x4, waiting for transfers between devices: 115 us -> 103 us  [exchange(): return lax.all_to_all(value, AXES, split_axis=0, concat_axis=0, tiled=True)]
    unnamed x15 -> x10, local copies, waits for them, and re-layouts: 9.3 us -> 2.21 us
    all_to_all x3 -> x4, starting transfers between devices: 12.5 us -> 18 us  [exchange(): return lax.all_to_all(value, AXES, split_axis=0, concat_axis=0, tiled=True)]
    optimization_barrier x0 -> x1, local copies, waits for them, and re-layouts: none -> 5.36 us  [body(): lax.optimization_barrier((early, frequency, steering))]
    pallas_call x1 -> x2, Pallas kernels: 17.1 us -> 18.6 us  [form_beams(): pl.pallas_call(functools.partial(beam_kernel, wide, tm, first), grid=(cha...]
  transfers between devices with their start and end apart: 4 -> 5, of which waited for: 3 -> 5; matrix products, arithmetic and copies ran while one was open for 3% -> 3% of each run, Pallas kernels for 26% -> 33%
where the time goes in v3:
time: 227 us; the launch traced here: 226 us
  waiting for transfers between devices  104 us (46%)
  Pallas kernels  90.6 us (40%)
  starting transfers between devices  20.6 us (9%)
  local copies, waits for them, and re-layouts  9.01 us (4%)
    all_to_all x4, waiting for transfers between devices, exchange(): return lax.all_to_all(value, AXES, split_axis=0, concat_axis=0, tiled=True)  103 us
    pallas_call x1, Pallas kernels, beam_weights(): pl.pallas_call(weights_kernel, grid=(antennas // block, channels), in_spe...  51.5 us
    pallas_call x2, Pallas kernels, form_beams(): pl.pallas_call(functools.partial(beam_kernel, wide, tm, first), grid=(cha...  18.6 us
    all_to_all x4, starting transfers between devices, exchange(): return lax.all_to_all(value, AXES, split_axis=0, concat_axis=0, tiled=True)  18 us
    pallas_call x2, Pallas kernels, spectra(): pl.pallas_call(functools.partial(spectra_kernel, (5 - taps) * width if ea...  13.3 us
    optimization_barrier x1, local copies, waits for them, and re-layouts, body(): lax.optimization_barrier((early, frequency, steering))  5.36 us
    pallas_call x1, Pallas kernels, search(): pl.pallas_call(functools.partial(search_kernel, own_frames, own_beams), i...  5.16 us
  transfers between devices with their start and end apart: 5, of which 5 were waited for; matrix products, arithmetic and copies ran while one was open for 3% of the time, Pallas kernels for 33%

profile of v3, /device:TPU:1, one launch (start us, length us, event | category | flops | bytes accessed | tf_op | source)
XLA Modules:
  0.0 225.8 jit_solution(12933387016553596317)
XLA Ops:
  0.0 1.2 slice.3
  1.2 2.7 %collective-permute-start = (bf16[2,256,768]{2,1,0:T(8,128)(2,1)S(1)}, bf16[2,256,768]{2,1,0:T(8,128)(2,1)S(1)}, u32[]{:S(2)}, u32[]{:S(2)}) collective-permute-start(bf16[2,256,768]{2,1,0:T(8,128)(2,1)S(1)} %slice.3), channel_id=1, source_target_pairs={{0,1},{1,2},{2,3},{3,0},{4,5},{5,6},{6,7},{7,4},{8,9},{9,10},{10,1... | collective-permute-start | bytes 2359304 | tf_op jit(solution)/shard_map/ppermute | solution.py:394
  3.8 8.0 %spectra.2 = (bf16[224,3,16,256]{3,2,1,0:T(8,128)(2,1)}, bf16[32,3,16,256]{3,2,1,0:T(8,128)(2,1)}) custom-call(f32[4,256]{1,0:T(4,128)} %taps_ref.3, bf16[512,512]{1,0:T(8,128)(2,1)} %constant.38.clone.table_ref, bf16[2,256,6144]{2,1,0:T(8,128)(2,1)} %volt_ref.3, bf16[2,256,6144]{2,1,0:T(8,128)(2,1)} %volt_ref.3), custom_call_target="tpu_custom_call" | custom-call | flops 2147483648 | bytes 8388608 | tf_op jit(solution)/shard_map/spectra/pallas_call | solution.py:101
  11.8 1.0 collective-permute-done.past_ref
  12.8 5.4 %spectra.3 = (bf16[224,3,16,256]{3,2,1,0:T(8,128)(2,1)}, bf16[32,3,16,256]{3,2,1,0:T(8,128)(2,1)}) custom-call(f32[4,256]{1,0:T(4,128)} %taps_ref.3, bf16[512,512]{1,0:T(8,128)(2,1)} %constant.38.clone.table_ref, bf16[2,256,768]{2,1,0:T(8,128)(2,1)S(1)} %collective-permute-done.past_ref, ...), custom_call_target="tpu_custom_call", output_to_operand_aliasing={{0}: (4, {}), {1}: (5, {})} | custom-call | flops 1073741824 | bytes 4194304 | tf_op jit(solution)/shard_map/spectra/pallas_call | solution.py:101
  18.1 0.0 copy-start.3
  18.1 7.0 %all-to-all-start = ((bf16[32,336,256]{2,1,0:T(8,128)(2,1)}), bf16[32,336,256]{2,1,0:T(8,128)(2,1)}, u32[]{:S(2)}, u32[]{:S(2)}) async-start(bf16[32,336,256]{2,1,0:T(8,128)(2,1)} %bitcast.29), calls=%async_computation | async-start | bytes 11010048 | tf_op jit(solution)/shard_map/all_to_all | solution.py:376
  25.2 0.0 copy-done.3
  25.2 0.2 reduce-window.9
  25.4 0.1 convert_reduce_fusion
  25.5 5.4 %copy.21 = f32[512,2048]{0,1:T(8,128)} copy(f32[512,2048]{1,0:T(8,128)} %param.9) | data formatting | bytes 8388608 | tf_op jit(solution)/shard_map/optimization_barrier | solution.py:412
  30.8 0.0 copy-start
  30.8 2.2 copy-done
  33.0 51.5 %weights.1.weight_ref = bf16[8,2048,1024]{2,1,0:T(8,128)(2,1)} custom-call(f32[8]{0:T(128)S(1)} %multiply_add_fusion.freq_ref, f32[2048,512]{1,0:T(8,128)S(1)} %bitcast.25), custom_call_target="tpu_custom_call" | custom-call | flops 251658240 | bytes 33554432 | tf_op jit(solution)/shard_map/weights/pallas_call | solution.py:185
  84.5 62.7 %all-to-all-done = bf16[32,336,256]{2,1,0:T(8,128)(2,1)} async-done(((bf16[32,336,256]{2,1,0:T(8,128)(2,1)}), bf16[32,336,256]{2,1,0:T(8,128)(2,1)}, u32[]{:S(2)}, u32[]{:S(2)}) %all-to-all-start) | async-done | bytes 5505056 | tf_op jit(solution)/shard_map/all_to_all | solution.py:376
  147.2 4.0 %all-to-all-start.1 = ((bf16[32,48,256]{2,1,0:T(8,128)(2,1)}), bf16[32,48,256]{2,1,0:T(8,128)(2,1)S(1)}, u32[]{:S(2)}, u32[]{:S(2)}) async-start(bf16[32,48,256]{2,1,0:T(8,128)(2,1)} %bitcast.8), calls=%async_computation.1 | async-start | bytes 1572864 | tf_op jit(solution)/shard_map/all_to_all | solution.py:376
  151.2 0.1 sub.15
  151.2 0.2 convert_reduce_fusion.1
  151.4 0.1 broadcast_compare_fusion
  151.6 14.7 %beams.2 = (f32[7,96,512]{2,1,0:T(8,128)S(1)}, f32[32,128]{1,0:T(8,128)S(1)}) custom-call(f32[32,128]{1,0:T(8,128)S(1)} %broadcast_in_dim.19.before_ref, bf16[32,7,3,16,256]{4,3,2,1,0:T(8,128)(2,1)} %bitcast.6.data_ref, bf16[8,2048,1024]{2,1,0:T(8,128)(2,1)} %weights.1.weight_ref), custom_call_target="tpu_custom_call" | custom-call | flops 5637144576 | bytes 29360128 | tf_op jit(solution)/shard_map/beams/pallas_call | solution.py:242
  166.3 5.0 %all-to-all-done.1 = bf16[32,48,256]{2,1,0:T(8,128)(2,1)S(1)} async-done(((bf16[32,48,256]{2,1,0:T(8,128)(2,1)}), bf16[32,48,256]{2,1,0:T(8,128)(2,1)S(1)}, u32[]{:S(2)}, u32[]{:S(2)}) %all-to-all-start.1) | async-done | bytes 786464 | tf_op jit(solution)/shard_map/all_to_all | solution.py:376
  171.3 3.9 %beams.3 = (f32[1,96,512]{2,1,0:T(8,128)S(1)}, f32[32,128]{1,0:T(8,128)}) custom-call(f32[32,128]{1,0:T(8,128)S(1)} %get-tuple-element.28.before_ref, bf16[32,1,3,16,256]{4,3,2,1,0:T(8,128)(2,1)S(1)} %bitcast.27, bf16[8,2048,1024]{2,1,0:T(8,128)(2,1)} %weights.1.weight_ref), custom_call_target="tpu_custom_call" | custom-call | flops 805306368 | bytes 4194304 | tf_op jit(solution)/shard_map/beams/pallas_call | solution.py:242
  175.2 0.0 copy-start.2
  175.2 0.0 copy-start.1
  175.2 4.1 %all-to-all-start.2 = ((f32[32,1,128]{2,1,0:T(1,128)}), f32[32,1,128]{2,1,0:T(1,128)S(1)}, u32[]{:S(2)}, u32[]{:S(2)}) async-start(f32[32,1,128]{2,1,0:T(1,128)} %bitcast.11), calls=%async_computation.2 | async-start | bytes 32768 | tf_op jit(solution)/shard_map/all_to_all | solution.py:376
  179.3 0.2 select_reduce_fusion
  179.5 0.1 copy.23.count_ref
  179.6 6.4 %all-to-all-done.2 = f32[32,1,128]{2,1,0:T(1,128)S(1)} async-done(((f32[32,1,128]{2,1,0:T(1,128)}), f32[32,1,128]{2,1,0:T(1,128)S(1)}, u32[]{:S(2)}, u32[]{:S(2)}) %all-to-all-start.2) | async-done | bytes 16416 | tf_op jit(solution)/shard_map/all_to_all | solution.py:376
  186.0 2.0 levels.1
  188.0 2.9 %all-to-all-start.3 = ((bf16[32,8,2432]{2,1,0:T(8,128)(2,1)}), bf16[32,8,2432]{2,1,0:T(8,128)(2,1)S(1)}, u32[]{:S(2)}, u32[]{:S(2)}) async-start(bf16[32,8,2432]{2,1,0:T(8,128)(2,1)} %levels.1), calls=%async_computation.3 | async-start | bytes 2490368 | tf_op jit(solution)/shard_map/all_to_all | solution.py:376
  190.9 0.0 copy-done.2
  190.9 0.1 copy.20
  191.0 0.3 fusion.pick_ref
  191.4 29.2 %all-to-all-done.3 = bf16[32,8,2432]{2,1,0:T(8,128)(2,1)S(1)} async-done(((bf16[32,8,2432]{2,1,0:T(8,128)(2,1)}), bf16[32,8,2432]{2,1,0:T(8,128)(2,1)S(1)}, u32[]{:S(2)}, u32[]{:S(2)}) %all-to-all-start.3) | async-done | bytes 1245216 | tf_op jit(solution)/shard_map/all_to_all | solution.py:376
  220.6 0.0 copy-done.1
  220.6 5.2 %search.1 = f32[4,1536,128]{2,1,0:T(8,128)} custom-call(s32[4]{0:T(128)S(1)} %copy-done.1, bf16[2048,128]{1,0:T(8,128)(2,1)S(1)} %fusion.pick_ref, bf16[256,2432]{1,0:T(8,128)(2,1)S(1)} %bitcast.26), custom_call_target="tpu_custom_call" | custom-call | tf_op jit(solution)/shard_map/search/pallas_call | solution.py:358
  (9 shorter events, 0.1 us)
Async XLA Ops:
  1.2 11.6 %collective-permute-start = (bf16[2,256,768]{2,1,0:T(8,128)(2,1)S(1)}, bf16[2,256,768]{2,1,0:T(8,128)(2,1)S(1)}, u32[]{:S(2)}, u32[]{:S(2)}) collective-permute-start(bf16[2,256,768]{2,1,0:T(8,128)(2,1)S(1)} %slice.3), channel_id=1, source_target_pairs={{0,1},{1,2},{2,3},{3,0},{4,5},{5,6},{6,7},{7,4},{8,9},{9,10},{10,1... | collective-permute-start | bytes 2359304 | tf_op jit(solution)/shard_map/ppermute | solution.py:394
  18.1 7.0 %copy-start.3 = (s32[8]{0:T(128)S(1)}, s32[8]{0:T(128)}, u32[]{:S(2)}) copy-start(s32[8]{0:T(128)} %param.10) | copy-start | bytes 100
  18.1 129.0 %all-to-all-start = ((bf16[32,336,256]{2,1,0:T(8,128)(2,1)}), bf16[32,336,256]{2,1,0:T(8,128)(2,1)}, u32[]{:S(2)}, u32[]{:S(2)}) async-start(bf16[32,336,256]{2,1,0:T(8,128)(2,1)} %bitcast.29), calls=%async_computation | async-start | bytes 11010048 | tf_op jit(solution)/shard_map/all_to_all | solution.py:376
  30.8 2.2 copy-start
  147.2 24.1 %all-to-all-start.1 = ((bf16[32,48,256]{2,1,0:T(8,128)(2,1)}), bf16[32,48,256]{2,1,0:T(8,128)(2,1)S(1)}, u32[]{:S(2)}, u32[]{:S(2)}) async-start(bf16[32,48,256]{2,1,0:T(8,128)(2,1)} %bitcast.8), calls=%async_computation.1 | async-start | bytes 1572864 | tf_op jit(solution)/shard_map/all_to_all | solution.py:376
  175.2 15.7 %copy-start.2 = (s32[128,256]{1,0:T(8,128)S(1)}, s32[128,256]{1,0:T(8,128)}, u32[]{:S(2)}) copy-start(s32[128,256]{1,0:T(8,128)} %param.11) | copy-start | bytes 393220
  175.2 45.4 %copy-start.1 = (s32[4]{0:T(128)S(1)}, s32[4]{0:T(128)}, u32[]{:S(2)}) copy-start(s32[4]{0:T(128)} %width_ref.1) | copy-start | bytes 52
  175.2 10.8 %all-to-all-start.2 = ((f32[32,1,128]{2,1,0:T(1,128)}), f32[32,1,128]{2,1,0:T(1,128)S(1)}, u32[]{:S(2)}, u32[]{:S(2)}) async-start(f32[32,1,128]{2,1,0:T(1,128)} %bitcast.11), calls=%async_computation.2 | async-start | bytes 32768 | tf_op jit(solution)/shard_map/all_to_all | solution.py:376
  188.0 32.6 %all-to-all-start.3 = ((bf16[32,8,2432]{2,1,0:T(8,128)(2,1)}), bf16[32,8,2432]{2,1,0:T(8,128)(2,1)S(1)}, u32[]{:S(2)}, u32[]{:S(2)}) async-start(bf16[32,8,2432]{2,1,0:T(8,128)(2,1)} %levels.1), calls=%async_computation.3 | async-start | bytes 2490368 | tf_op jit(solution)/shard_map/all_to_all | solution.py:376

commit v4 on v3

--- a/solution.py
+++ b/solution.py
@@ -269,7 +269,7 @@
     )(before, received, weights)
 
 
-def level_kernel(wide, tm, reach, mask_ref, count_ref, sums_ref, *refs):
+def level_kernel(wide, tm, mask_ref, count_ref, sums_ref, *refs):
     power_refs, out_ref = refs[:-1], refs[-1]
     channels = mask_ref.shape[0]
     _, frames, beams = power_refs[0].shape
@@ -282,7 +282,6 @@
     for c in range(channels):
         means.append(jnp.sum(jnp.sum(mask_ref[c] * sums, axis=0, keepdims=True), axis=1, keepdims=True))
     mean = jnp.concatenate(means, axis=0) / count_ref[...]
-    span = own_frames + reach
 
     def level(f):
         value = jnp.concatenate([ref[c, f : f + 1, :] for ref, c in slots], axis=0)
@@ -294,82 +293,148 @@
             piece = jnp.concatenate(
                 [v[:, w * own_beams : (w + 1) * own_beams] for v in values], axis=1
             )
-            for m in range(tm):
-                for lap in (0, frames):
-                    at = start + lap - m * own_frames
-                    if 0 <= at < span:
-                        width = min(per_row, span - at) * own_beams
-                        out_ref[w * tm + m, :, at * own_beams : at * own_beams + width] = piece[
-                            :, :width
-                        ]
-
-
-def form_levels(mask, count, sums, powers, wide, tm, reach):
+            m, at = divmod(start, own_frames)
+            at *= own_beams
+            out_ref[w * tm + m, :, at : at + per_row * own_beams] = piece
+
+
+def form_levels(mask, count, sums, powers, wide, tm):
     channels = mask.shape[0]
     _, frames, beams = powers[0].shape
-    span = frames // tm + reach
-    lanes = span * (beams // wide)
+    lanes = frames // tm * (beams // wide)
     return pl.pallas_call(
-        functools.partial(level_kernel, wide, tm, reach),
+        functools.partial(level_kernel, wide, tm),
         out_shape=jax.ShapeDtypeStruct((wide * tm, channels, lanes), jnp.bfloat16),
         compiler_params=pltpu.CompilerParams(vmem_limit_bytes=48 * MIB),
         name="levels",
     )(mask, count, sums, *powers)
 
 
-def search_kernel(own_frames, own_beams, width_ref, pick_ref, level_ref, out_ref, turn_ref, sum_ref):
-    widths = out_ref.shape[0]
-    channels, lanes = level_ref.shape
-    delays = MAXDELAY + 1
-    frames = own_frames + WMAX - 1
+def turn(source_ref, lane, lanes, target_ref, row):
     for start in range(0, lanes, 128):
-        stop = min(start + 128, lanes)
-        turn_ref[start:stop, :] = level_ref[:, start:stop].T
-    chunk = 8
+        size = min(128, lanes - start)
+        piece = source_ref[:, lane + start : lane + start + size].T
+        target_ref[row + start : row + start + size, :] = piece
+
+
+def dedisperse(turn_ref, pick_ref, sum_ref, row, frames, beams):
+    chunk = 7
     for start in range(0, frames, chunk):
         stop = min(start + chunk, frames)
         held = jnp.concatenate(
             [
-                turn_ref[(start + d) * own_beams : (stop + d) * own_beams, :]
-                for d in range(delays)
+                turn_ref[(start + d) * beams : (stop + d) * beams, :]
+                for d in range(MAXDELAY + 1)
             ],
             axis=1,
         )
-        value = jnp.dot(held, pick_ref[...], preferred_element_type=jnp.float32)
-        sum_ref[0, start * own_beams : stop * own_beams, :] = value
-    window = own_frames * own_beams
-    for at in range(0, own_frames, 4):
-        rows = pl.ds(at * own_beams, 4 * own_beams)
-        total = sum_ref[0, rows, :]
+        sum_ref[0, row + start * beams : row + stop * beams, :] = jnp.dot(
+            held, pick_ref[...], preferred_element_type=jnp.float32
+        )
+
+
+def boxcars(channels, width_ref, sum_ref, stage_ref, out_ref, sems, row, beams):
+    widths, rows, _ = stage_ref.shape
+    for at in range(0, rows, 2 * beams):
+        total = sum_ref[0, at : at + 2 * beams, :]
         for lag in range(1, WMAX):
-            total = total + sum_ref[0, pl.ds((at + lag) * own_beams, 4 * own_beams), :]
-            sum_ref[lag, rows, :] = total
+            begin = at + lag * beams
+            total = total + sum_ref[0, begin : begin + 2 * beams, :]
+            sum_ref[lag, at : at + 2 * beams, :] = total
+    copies = []
     for i in range(widths):
         expected = width_ref[i].astype(jnp.float32) * np.float32(channels)
-        root = jnp.sqrt(jnp.full((1, out_ref.shape[2]), expected, jnp.float32))
-        out_ref[i] = (sum_ref[width_ref[i] - 1, :window, :] - expected) / root
-
-
-def search(box_widths, picks, levels, own_frames, own_beams):
+        root = jnp.sqrt(jnp.full((1, stage_ref.shape[2]), expected, jnp.float32))
+        stage_ref[i] = (sum_ref[width_ref[i] - 1, :rows, :] - expected) / root
+        copy = pltpu.make_async_copy(
+            stage_ref.at[i], out_ref.at[i, pl.ds(row, rows)], sems.at[i]
+        )
+        copy.start()
+        copies.append(copy)
+    for copy in copies:
+        copy.wait()
+
+
+def search_early_kernel(
+    beams, width_ref, pick_ref, level_ref, out_ref, kept_ref, turn_ref, sum_ref, stage_ref, sems
+):
+    channels, lanes = level_ref.shape
+    turn(level_ref, 0, lanes, turn_ref, 0)
+    known = sum_ref.shape[1]
+    dedisperse(turn_ref, pick_ref, sum_ref, 0, known // beams, beams)
+    kept_ref[...] = sum_ref[0, known - kept_ref.shape[0] :, :]
+    boxcars(channels, width_ref, sum_ref, stage_ref, out_ref, sems, 0, beams)
+
+
+def search_late_kernel(
+    beams, width_ref, pick_ref, level_ref, halo_ref, kept_ref, given_ref, out_ref, turn_ref,
+    sum_ref, stage_ref, sems,
+):
+    channels, lanes = level_ref.shape
+    held = MAXDELAY * beams
+    turn(level_ref, lanes - held, held, turn_ref, 0)
+    turn(halo_ref, 0, halo_ref.shape[1], turn_ref, held)
+    kept = kept_ref.shape[0]
+    sum_ref[0, :kept, :] = kept_ref[...]
+    dedisperse(turn_ref, pick_ref, sum_ref, kept, sum_ref.shape[1] // beams - WMAX + 1, beams)
+    row = lanes - stage_ref.shape[1]
+    boxcars(channels, width_ref, sum_ref, stage_ref, out_ref, sems, row, beams)
+
+
+def search(box_widths, picks, levels, beams):
     trials = picks.shape[1]
     channels, lanes = levels.shape
     widths = box_widths.shape[0]
-    frames = own_frames + WMAX - 1
+    lags = WMAX - 1
+    frames = lanes // beams
+    known = frames - MAXDELAY
+    early = known - lags
+    late = frames - early
+    whole = pl.BlockSpec(memory_space=pltpu.VMEM)
+    params = pltpu.CompilerParams(vmem_limit_bytes=32 * MIB)
+    found, kept = pl.pallas_call(
+        functools.partial(search_early_kernel, beams),
+        in_specs=[pl.BlockSpec(memory_space=pltpu.SMEM), whole, whole],
+        out_specs=[pl.BlockSpec(memory_space=pl.ANY), whole],
+        out_shape=[
+            jax.ShapeDtypeStruct((widths, lanes, trials), jnp.float32),
+            jax.ShapeDtypeStruct((lags * beams, trials), jnp.float32),
+        ],
+        scratch_shapes=[
+            pltpu.VMEM((lanes, channels), jnp.bfloat16),
+            pltpu.VMEM((WMAX, known * beams, trials), jnp.float32),
+            pltpu.VMEM((widths, early * beams, trials), jnp.float32),
+            pltpu.SemaphoreType.DMA((widths,)),
+        ],
+        compiler_params=params,
+        name="search_early",
+    )(box_widths, picks, levels)
+    blocks = lax.axis_size("tm")
+    halo = lax.ppermute(
+        levels[:, : (MAXDELAY + lags) * beams], "tm", [(i, (i - 1) % blocks) for i in range(blocks)]
+    )
     return pl.pallas_call(
-        functools.partial(search_kernel, own_frames, own_beams),
+        functools.partial(search_late_kernel, beams),
         in_specs=[
             pl.BlockSpec(memory_space=pltpu.SMEM),
-            pl.BlockSpec(memory_space=pltpu.VMEM),
-            pl.BlockSpec(memory_space=pltpu.VMEM),
-        ],
-        out_shape=jax.ShapeDtypeStruct((widths, own_frames * own_beams, trials), jnp.float32),
+            whole,
+            whole,
+            whole,
+            whole,
+            pl.BlockSpec(memory_space=pl.ANY),
+        ],
+        out_specs=pl.BlockSpec(memory_space=pl.ANY),
+        out_shape=jax.ShapeDtypeStruct((widths, lanes, trials), jnp.float32),
         scratch_shapes=[
-            pltpu.VMEM((lanes, channels), jnp.bfloat16),
-            pltpu.VMEM((WMAX, frames * own_beams, trials), jnp.float32),
-        ],
-        compiler_params=pltpu.CompilerParams(vmem_limit_bytes=48 * MIB),
-        name="search",
-    )(box_widths, picks, levels)
+            pltpu.VMEM(((MAXDELAY + MAXDELAY + lags) * beams, channels), jnp.bfloat16),
+            pltpu.VMEM((WMAX, (late + lags) * beams, trials), jnp.float32),
+            pltpu.VMEM((widths, late * beams, trials), jnp.float32),
+            pltpu.SemaphoreType.DMA((widths,)),
+        ],
+        input_output_aliases={5: 0},
+        compiler_params=params,
+        name="search_late",
+    )(box_widths, picks, levels, halo, kept, found)
 
 
 def exchange(value):
@@ -433,15 +498,14 @@
         axis=1,
         keepdims=True,
     )
-    reach = MAXDELAY + WMAX - 1
-    levels = form_levels(mask, count, exchange(sums), powers, wide, tm, reach)
+    levels = form_levels(mask, count, exchange(sums), powers, wide, tm)
     arrived = exchange(levels).reshape(channel_rows, levels.shape[2])
 
     steps = jnp.arange(MAXDELAY + 1, dtype=jnp.int32)
     picks = (delays.T[None, :, :] == steps[:, None, None]).astype(jnp.bfloat16)
     picks = picks.reshape((MAXDELAY + 1) * channel_rows, delays.shape[0])
     own_beams = beam_count // wide
-    found = search(box_widths, picks, arrived, frame_rows, own_beams)
+    found = search(box_widths, picks, arrived, own_beams)
     found = found.reshape(box_widths.shape[0], frame_rows, own_beams, delays.shape[0])
     return found.transpose(3, 0, 1, 2)
 

time: 227 us -> 221 us (0.974)
  waiting for transfers between devices: 104 us -> 78.6 us
  blocking collectives: 0 us -> 22.3 us
    all_to_all x4 -> x3, waiting for transfers between devices: 103 us -> 74.1 us  [exchange(): return lax.all_to_all(value, AXES, split_axis=0, concat_axis=0, tiled=True)]
    all_to_all x0 -> x1, blocking collectives: none -> 22.3 us  [exchange(): return lax.all_to_all(value, AXES, split_axis=0, concat_axis=0, tiled=True)]
    ppermute x0 -> x1, waiting for transfers between devices: none -> 3.57 us  [search(): lax.ppermute(levels[:, :(MAXDELAY + lags) * beams], 'tm', [(i, (i - 1) %...]
    all_to_all x4 -> x3, starting transfers between devices: 18 us -> 15 us  [exchange(): return lax.all_to_all(value, AXES, split_axis=0, concat_axis=0, tiled=True)]
    pallas_call x2 -> x3, Pallas kernels: 7.13 us -> 7.47 us  [the longest x1 3.32 us: search(): pl.pallas_call(functools.partial(search_late_kernel, beams), in_specs=[pl...]
  transfers between devices with their start and end apart: 5 -> 5, of which waited for: 5 -> 5; matrix products, arithmetic and copies ran while one was open for 3% -> 3% of each run, Pallas kernels for 33% -> 35%
where the time goes in v4:
time: 221 us
  Pallas kernels  91 us (41%)
  waiting for transfers between devices  78.6 us (36%)
  blocking collectives  22.3 us (10%)
  starting transfers between devices  18.5 us (8%)
  local copies, waits for them, and re-layouts  9.04 us (4%)
    all_to_all x3, waiting for transfers between devices, exchange(): return lax.all_to_all(value, AXES, split_axis=0, concat_axis=0, tiled=True)  74.1 us
    pallas_call x1, Pallas kernels, beam_weights(): pl.pallas_call(weights_kernel, grid=(antennas // block, channels), in_spe...  51.5 us
    all_to_all x1, blocking collectives, exchange(): return lax.all_to_all(value, AXES, split_axis=0, concat_axis=0, tiled=True)  22.3 us
    pallas_call x2, Pallas kernels, form_beams(): pl.pallas_call(functools.partial(beam_kernel, wide, tm, first), grid=(cha...  18.7 us
    all_to_all x3, starting transfers between devices, exchange(): return lax.all_to_all(value, AXES, split_axis=0, concat_axis=0, tiled=True)  15 us
    pallas_call x2, Pallas kernels, spectra(): pl.pallas_call(functools.partial(spectra_kernel, (5 - taps) * width if ea...  13.3 us
    optimization_barrier x1, local copies, waits for them, and re-layouts, body(): lax.optimization_barrier((early, frequency, steering))  5.36 us
  transfers between devices with their start and end apart: 5, of which 5 were waited for; matrix products, arithmetic and copies ran while one was open for 3% of the time, Pallas kernels for 35%

profile of v4, /device:TPU:1, one launch (start us, length us, event | category | flops | bytes accessed | tf_op | source)
XLA Modules:
  0.0 220.6 jit_solution(2372695254096257835)
XLA Ops:
  0.0 1.2 slice.6
  1.2 2.7 %collective-permute-start = (bf16[2,256,768]{2,1,0:T(8,128)(2,1)S(1)}, bf16[2,256,768]{2,1,0:T(8,128)(2,1)S(1)}, u32[]{:S(2)}, u32[]{:S(2)}) collective-permute-start(bf16[2,256,768]{2,1,0:T(8,128)(2,1)S(1)} %slice.6), channel_id=1, source_target_pairs={{0,1},{1,2},{2,3},{3,0},{4,5},{5,6},{6,7},{7,4},{8,9},{9,10},{10,1... | collective-permute-start | bytes 2359304 | tf_op jit(solution)/shard_map/ppermute | solution.py:459
  3.8 8.0 %spectra.2 = (bf16[224,3,16,256]{3,2,1,0:T(8,128)(2,1)}, bf16[32,3,16,256]{3,2,1,0:T(8,128)(2,1)}) custom-call(f32[4,256]{1,0:T(4,128)} %taps_ref.3, bf16[512,512]{1,0:T(8,128)(2,1)} %constant.38.clone.table_ref, bf16[2,256,6144]{2,1,0:T(8,128)(2,1)} %volt_ref.3, bf16[2,256,6144]{2,1,0:T(8,128)(2,1)} %volt_ref.3), custom_call_target="tpu_custom_call" | custom-call | flops 2147483648 | bytes 8388608 | tf_op jit(solution)/shard_map/spectra/pallas_call | solution.py:101
  11.8 1.0 collective-permute-done.past_ref
  12.8 5.4 %spectra.3 = (bf16[224,3,16,256]{3,2,1,0:T(8,128)(2,1)}, bf16[32,3,16,256]{3,2,1,0:T(8,128)(2,1)}) custom-call(f32[4,256]{1,0:T(4,128)} %taps_ref.3, bf16[512,512]{1,0:T(8,128)(2,1)} %constant.38.clone.table_ref, bf16[2,256,768]{2,1,0:T(8,128)(2,1)S(1)} %collective-permute-done.past_ref, ...), custom_call_target="tpu_custom_call", output_to_operand_aliasing={{0}: (4, {}), {1}: (5, {})} | custom-call | flops 1073741824 | bytes 4194304 | tf_op jit(solution)/shard_map/spectra/pallas_call | solution.py:101
  18.1 0.0 copy-start.3
  18.1 7.0 %all-to-all-start = ((bf16[32,336,256]{2,1,0:T(8,128)(2,1)}), bf16[32,336,256]{2,1,0:T(8,128)(2,1)}, u32[]{:S(2)}, u32[]{:S(2)}) async-start(bf16[32,336,256]{2,1,0:T(8,128)(2,1)} %bitcast.31), calls=%async_computation | async-start | bytes 11010048 | tf_op jit(solution)/shard_map/all_to_all | solution.py:441
  25.2 0.0 copy-done.3
  25.2 0.2 reduce-window.9
  25.4 0.1 convert_reduce_fusion
  25.5 5.4 %copy.22 = f32[512,2048]{0,1:T(8,128)} copy(f32[512,2048]{1,0:T(8,128)} %param.9) | data formatting | bytes 8388608 | tf_op jit(solution)/shard_map/optimization_barrier | solution.py:477
  30.8 0.0 copy-start
  30.8 2.2 copy-done
  33.0 51.5 %weights.1.weight_ref = bf16[8,2048,1024]{2,1,0:T(8,128)(2,1)} custom-call(f32[8]{0:T(128)S(1)} %multiply_add_fusion.freq_ref, f32[2048,512]{1,0:T(8,128)S(1)} %bitcast.25), custom_call_target="tpu_custom_call" | custom-call | flops 251658240 | bytes 33554432 | tf_op jit(solution)/shard_map/weights/pallas_call | solution.py:185
  84.5 62.7 %all-to-all-done = bf16[32,336,256]{2,1,0:T(8,128)(2,1)} async-done(((bf16[32,336,256]{2,1,0:T(8,128)(2,1)}), bf16[32,336,256]{2,1,0:T(8,128)(2,1)}, u32[]{:S(2)}, u32[]{:S(2)}) %all-to-all-start) | async-done | bytes 5505056 | tf_op jit(solution)/shard_map/all_to_all | solution.py:441
  147.2 4.0 %all-to-all-start.1 = ((bf16[32,48,256]{2,1,0:T(8,128)(2,1)}), bf16[32,48,256]{2,1,0:T(8,128)(2,1)S(1)}, u32[]{:S(2)}, u32[]{:S(2)}) async-start(bf16[32,48,256]{2,1,0:T(8,128)(2,1)} %bitcast.8), calls=%async_computation.1 | async-start | bytes 1572864 | tf_op jit(solution)/shard_map/all_to_all | solution.py:441
  151.2 0.1 sub.15
  151.2 0.2 convert_reduce_fusion.1
  151.4 0.1 broadcast_compare_fusion
  151.6 14.7 %beams.2 = (f32[7,96,512]{2,1,0:T(8,128)S(1)}, f32[32,128]{1,0:T(8,128)S(1)}) custom-call(f32[32,128]{1,0:T(8,128)S(1)} %broadcast_in_dim.19.before_ref, bf16[32,7,3,16,256]{4,3,2,1,0:T(8,128)(2,1)} %bitcast.6.data_ref, bf16[8,2048,1024]{2,1,0:T(8,128)(2,1)} %weights.1.weight_ref), custom_call_target="tpu_custom_call" | custom-call | flops 5637144576 | bytes 29360128 | tf_op jit(solution)/shard_map/beams/pallas_call | solution.py:242
  166.3 5.0 %all-to-all-done.1 = bf16[32,48,256]{2,1,0:T(8,128)(2,1)S(1)} async-done(((bf16[32,48,256]{2,1,0:T(8,128)(2,1)}), bf16[32,48,256]{2,1,0:T(8,128)(2,1)S(1)}, u32[]{:S(2)}, u32[]{:S(2)}) %all-to-all-start.1) | async-done | bytes 786464 | tf_op jit(solution)/shard_map/all_to_all | solution.py:441
  171.3 0.0 copy-start.2
  171.3 4.0 %beams.3 = (f32[1,96,512]{2,1,0:T(8,128)S(1)}, f32[32,128]{1,0:T(8,128)}) custom-call(f32[32,128]{1,0:T(8,128)S(1)} %get-tuple-element.30.before_ref, bf16[32,1,3,16,256]{4,3,2,1,0:T(8,128)(2,1)S(1)} %bitcast.29, bf16[8,2048,1024]{2,1,0:T(8,128)(2,1)} %weights.1.weight_ref), custom_call_target="tpu_custom_call" | custom-call | flops 805306368 | bytes 4194304 | tf_op jit(solution)/shard_map/beams/pallas_call | solution.py:242
  175.3 0.0 copy-start.1
  175.3 4.1 %all-to-all-start.2 = ((f32[32,1,128]{2,1,0:T(1,128)}), f32[32,1,128]{2,1,0:T(1,128)S(1)}, u32[]{:S(2)}, u32[]{:S(2)}) async-start(f32[32,1,128]{2,1,0:T(1,128)} %bitcast.11), calls=%async_computation.2 | async-start | bytes 32768 | tf_op jit(solution)/shard_map/all_to_all | solution.py:441
  179.4 0.2 select_reduce_fusion
  179.5 0.1 copy.24.count_ref
  179.6 6.4 %all-to-all-done.2 = f32[32,1,128]{2,1,0:T(1,128)S(1)} async-done(((f32[32,1,128]{2,1,0:T(1,128)}), f32[32,1,128]{2,1,0:T(1,128)S(1)}, u32[]{:S(2)}, u32[]{:S(2)}) %all-to-all-start.2) | async-done | bytes 16416 | tf_op jit(solution)/shard_map/all_to_all | solution.py:441
  186.1 0.9 levels.1
  187.0 22.3 %all_to_all.26 = bf16[32,8,1536]{2,1,0:T(8,128)(2,1)S(1)} all-to-all(bf16[32,8,1536]{2,1,0:T(8,128)(2,1)S(1)} %levels.1), channel_id=1, replica_groups=mesh['wide'=8,'tm'=4] {'wide','tm'}, dimensions={0} | all-to-all | bytes 1572864 | tf_op jit(solution)/shard_map/all_to_all | solution.py:441
  209.3 0.8 collective-permute-start.1
  210.1 0.0 copy-done.2
  210.1 0.1 copy.21
  210.2 0.3 fusion.pick_ref
  210.5 0.0 copy-done.1
  210.5 3.2 %search_early.1 = (f32[4,1536,128]{2,1,0:T(8,128)}, f32[448,128]{1,0:T(8,128)S(1)}) custom-call(s32[4]{0:T(128)S(1)} %copy-done.1, bf16[2048,128]{1,0:T(8,128)(2,1)S(1)} %fusion.pick_ref, bf16[256,1536]{1,0:T(8,128)(2,1)S(1)} %bitcast.27), custom_call_target="tpu_custom_call" | custom-call | tf_op jit(solution)/shard_map/search_early/pallas_call | solution.py:395
  213.7 3.6 %collective-permute-done.1.halo_ref = bf16[256,896]{1,0:T(8,128)(2,1)S(1)} collective-permute-done((bf16[256,896]{1,0:T(8,128)(2,1)S(1)}, bf16[256,896]{1,0:T(8,128)(2,1)S(1)}, u32[]{:S(2)}, u32[]{:S(2)}) %collective-permute-start.1) | collective-permute-done | bytes 458784 | tf_op jit(solution)/shard_map/ppermute | solution.py:413
  217.3 3.3 %search_late.1 = f32[4,1536,128]{2,1,0:T(8,128)} custom-call(s32[4]{0:T(128)S(1)} %copy-done.1, bf16[2048,128]{1,0:T(8,128)(2,1)S(1)} %fusion.pick_ref, bf16[256,1536]{1,0:T(8,128)(2,1)S(1)} %bitcast.28, bf16[256,896]{1,0:T(8,128)(2,1)S(1)} %collective-permute-done.1.halo_ref, ...), custom_call_target="tpu_custom_call", output_to_operand_aliasing={{}: (5, {})} | custom-call | tf_op jit(solution)/shard_map/search_late/pallas_call | solution.py:416
  (10 shorter events, 0.1 us)
Async XLA Ops:
  1.2 11.6 %collective-permute-start = (bf16[2,256,768]{2,1,0:T(8,128)(2,1)S(1)}, bf16[2,256,768]{2,1,0:T(8,128)(2,1)S(1)}, u32[]{:S(2)}, u32[]{:S(2)}) collective-permute-start(bf16[2,256,768]{2,1,0:T(8,128)(2,1)S(1)} %slice.6), channel_id=1, source_target_pairs={{0,1},{1,2},{2,3},{3,0},{4,5},{5,6},{6,7},{7,4},{8,9},{9,10},{10,1... | collective-permute-start | bytes 2359304 | tf_op jit(solution)/shard_map/ppermute | solution.py:459
  18.1 7.0 %copy-start.3 = (s32[8]{0:T(128)S(1)}, s32[8]{0:T(128)}, u32[]{:S(2)}) copy-start(s32[8]{0:T(128)} %param.10) | copy-start | bytes 100
  18.1 129.0 %all-to-all-start = ((bf16[32,336,256]{2,1,0:T(8,128)(2,1)}), bf16[32,336,256]{2,1,0:T(8,128)(2,1)}, u32[]{:S(2)}, u32[]{:S(2)}) async-start(bf16[32,336,256]{2,1,0:T(8,128)(2,1)} %bitcast.31), calls=%async_computation | async-start | bytes 11010048 | tf_op jit(solution)/shard_map/all_to_all | solution.py:441
  30.8 2.2 copy-start
  147.2 24.1 %all-to-all-start.1 = ((bf16[32,48,256]{2,1,0:T(8,128)(2,1)}), bf16[32,48,256]{2,1,0:T(8,128)(2,1)S(1)}, u32[]{:S(2)}, u32[]{:S(2)}) async-start(bf16[32,48,256]{2,1,0:T(8,128)(2,1)} %bitcast.8), calls=%async_computation.1 | async-start | bytes 1572864 | tf_op jit(solution)/shard_map/all_to_all | solution.py:441
  171.3 38.8 %copy-start.2 = (s32[128,256]{1,0:T(8,128)S(1)}, s32[128,256]{1,0:T(8,128)}, u32[]{:S(2)}) copy-start(s32[128,256]{1,0:T(8,128)} %param.11) | copy-start | bytes 393220
  175.3 35.3 %copy-start.1 = (s32[4]{0:T(128)S(1)}, s32[4]{0:T(128)}, u32[]{:S(2)}) copy-start(s32[4]{0:T(128)} %width_ref.3) | copy-start | bytes 52
  175.3 10.8 %all-to-all-start.2 = ((f32[32,1,128]{2,1,0:T(1,128)}), f32[32,1,128]{2,1,0:T(1,128)S(1)}, u32[]{:S(2)}, u32[]{:S(2)}) async-start(f32[32,1,128]{2,1,0:T(1,128)} %bitcast.11), calls=%async_computation.2 | async-start | bytes 32768 | tf_op jit(solution)/shard_map/all_to_all | solution.py:441
  209.3 8.0 %collective-permute-start.1 = (bf16[256,896]{1,0:T(8,128)(2,1)S(1)}, bf16[256,896]{1,0:T(8,128)(2,1)S(1)}, u32[]{:S(2)}, u32[]{:S(2)}) collective-permute-start(bf16[256,896]{1,0:T(8,128)(2,1)S(1)} %slice.8), channel_id=1, source_target_pairs={{0,3},{1,0},{2,1},{3,2},{4,7},{5,4},{6,5},{7,6},{8,11},{9,8},{10,9... | collective-permute-start | bytes 1376264 | tf_op jit(solution)/shard_map/ppermute | solution.py:413

commit v5 on v4

--- a/solution.py
+++ b/solution.py
@@ -37,11 +37,10 @@
     return np.concatenate(ordered).astype(jnp.bfloat16)
 
 
-def spectra_kernel(skip, parts, taps_ref, table_ref, past_ref, volt_ref, *rest):
-    out_refs, part_ref = rest[-1 - parts : -1], rest[-1]
+def transform(inners, skip, taps_ref, table_ref, past_ref, volt_ref, part_ref):
     taps = taps_ref.shape[0]
     width = taps_ref.shape[1]
-    for inner in range(8):
+    for inner in inners:
         pieces = []
         for part in range(2):
             total = None
@@ -69,60 +68,103 @@
             part_ref[half, pl.ds(inner, rows, stride=8), :] = spectrum[
                 :, half * 128 : half * 128 + 128
             ]
-    for half in range(lanes // 128):
+
+
+def write_out(part_ref, out_refs, kept_ref=None, fresh=8):
+    antennas = out_refs[0].shape[3]
+    for half in range(part_ref.shape[0]):
         size = min(128, antennas - half * 128)
         first = 0
         for out_ref in out_refs:
             count = out_ref.shape[0]
-            value = part_ref[half, first * 16 : (first + count) * 16].astype(jnp.bfloat16)
-            value = value.reshape(count, 16, 128)
+            value = part_ref[half, first * 16 : (first + count) * 16]
+            if kept_ref is not None:
+                kept = kept_ref[half, first * 16 : (first + count) * 16]
+                frame = lax.broadcasted_iota(jnp.int32, value.shape, 0) % 8
+                value = jnp.where(frame < fresh, value, kept)
+            value = value.astype(jnp.bfloat16).reshape(count, 16, 128)
             out_ref[:, 0, :, half * 128 : half * 128 + size] = value[:, :, :size]
             first += count
 
 
-def spectra(counts, table, past, voltages, fir_taps, earlier=None):
+def spectra_kernel(skip, taps_ref, table_ref, past_ref, volt_ref, *rest):
+    out_refs, kept_ref, part_ref = rest[:-2], rest[-2], rest[-1]
+    taps = taps_ref.shape[0]
+
+    @pl.when(pl.program_id(0) == 0)
+    def _():
+        transform(range(taps - 1, 8), 0, taps_ref, table_ref, past_ref, volt_ref, kept_ref)
+
+    @pl.when(pl.program_id(0) > 0)
+    def _():
+        transform(range(8), skip, taps_ref, table_ref, past_ref, volt_ref, part_ref)
+        write_out(part_ref, out_refs)
+
+
+def spectra_first_kernel(taps_ref, table_ref, past_ref, volt_ref, kept_ref, *rest):
+    count = (len(rest) - 1) // 2
+    out_refs, part_ref = rest[count:-1], rest[-1]
+    fresh = taps_ref.shape[0] - 1
+    transform(range(fresh), 0, taps_ref, table_ref, past_ref, volt_ref, part_ref)
+    write_out(part_ref, out_refs, kept_ref, fresh)
+
+
+def spectra(counts, table, halo, voltages, fir_taps):
     taps, width = fir_taps.shape
     antennas = voltages.shape[1]
     groups = voltages.shape[2] // (8 * width)
-    first = 1 if earlier is None else 0
-    steps = groups - 1 if earlier is None else 1
-    operands = [fir_taps, table, past, voltages]
-    in_specs = [
+    part = pltpu.VMEM((-(-antennas // 128), 2 * width * 8, 128), jnp.float32)
+    shapes = [pltpu.HBM((count, groups, 16, antennas), jnp.bfloat16) for count in counts]
+
+    def blocks(place):
+        return [pl.BlockSpec((count, 1, 16, antennas), place) for count in counts]
+
+    def cost(frames):
+        return pl.CostEstimate(
+            flops=8 * frames * antennas * width * width,
+            bytes_accessed=8 * frames * antennas * width,
+            transcendentals=0,
+        )
+
+    common = [
         pl.BlockSpec(fir_taps.shape, lambda g: (0, 0)),
         pl.BlockSpec(table.shape, lambda g: (0, 0)),
-        pl.BlockSpec((2, antennas, 4 * width), lambda g: (0, 0, 2 * g + 1))
-        if earlier is None
-        else pl.BlockSpec(past.shape, lambda g: (0, 0, 0)),
-        pl.BlockSpec((2, antennas, 8 * width), lambda g: (0, 0, g + first)),
     ]
-    if earlier is not None:
-        operands.extend(earlier)
-        in_specs.extend([pl.BlockSpec(memory_space=pl.ANY)] * len(counts))
+    *outgoing, kept = pl.pallas_call(
+        functools.partial(spectra_kernel, (5 - taps) * width),
+        grid=(groups,),
+        in_specs=common
+        + [
+            pl.BlockSpec((2, antennas, 4 * width), lambda g: (0, 0, jnp.maximum(2 * g - 1, 1))),
+            pl.BlockSpec((2, antennas, 8 * width), lambda g: (0, 0, g)),
+        ],
+        out_specs=blocks(lambda g: (0, jnp.maximum(g, 1), 0, 0))
+        + [pl.BlockSpec(memory_space=pltpu.VMEM)],
+        out_shape=shapes + [part],
+        scratch_shapes=[part],
+        compiler_params=pltpu.CompilerParams(vmem_limit_bytes=40 * MIB),
+        cost_estimate=cost(8 * groups),
+        name="spectra",
+    )(fir_taps, table, voltages, voltages)
+    kept = pltpu.with_memory_space_constraint(kept, pltpu.VMEM)
     return pl.pallas_call(
-        functools.partial(
-            spectra_kernel, (5 - taps) * width if earlier is None else 0, len(counts)
-        ),
-        grid=(steps,),
-        in_specs=in_specs,
-        out_specs=[
-            pl.BlockSpec((count, 1, 16, antennas), lambda g: (0, g + first, 0, 0))
-            for count in counts
-        ],
-        out_shape=[
-            jax.ShapeDtypeStruct((count, groups, 16, antennas), jnp.bfloat16) for count in counts
-        ],
-        scratch_shapes=[
-            pltpu.VMEM((-(-antennas // 128), 2 * width * 8, 128), jnp.float32),
-        ],
-        input_output_aliases={} if earlier is None else {4 + i: i for i in range(len(counts))},
-        compiler_params=pltpu.CompilerParams(vmem_limit_bytes=48 * MIB),
-        cost_estimate=pl.CostEstimate(
-            flops=64 * steps * antennas * width * width,
-            bytes_accessed=64 * steps * antennas * width,
-            transcendentals=0,
-        ),
-        name="spectra",
-    )(*operands)
+        spectra_first_kernel,
+        grid=(1,),
+        in_specs=common
+        + [
+            pl.BlockSpec(halo.shape, lambda g: (0, 0, 0)),
+            pl.BlockSpec((2, antennas, 4 * width), lambda g: (0, 0, 0)),
+            pl.BlockSpec(memory_space=pltpu.VMEM),
+        ]
+        + [pl.BlockSpec(memory_space=pl.ANY)] * len(counts),
+        out_specs=blocks(lambda g: (0, 0, 0, 0)),
+        out_shape=shapes,
+        scratch_shapes=[part],
+        input_output_aliases={5 + i: i for i in range(len(counts))},
+        compiler_params=pltpu.CompilerParams(vmem_limit_bytes=32 * MIB),
+        cost_estimate=cost(taps - 1),
+        name="spectra_first",
+    )(fir_taps, table, halo, voltages, kept, *outgoing)
 
 
 def sincos(phase):
@@ -465,8 +507,8 @@
         jnp.asarray(dft_rows(channel_rows, slots)), pltpu.HBM
     )
     fir_taps = pltpu.with_memory_space_constraint(fir_taps, pltpu.HBM)
-    outgoing = spectra(counts, table, voltages, voltages, fir_taps)
-    early, tail = spectra(counts, table, halo, voltages, fir_taps, outgoing)
+    voltages = pltpu.with_memory_space_constraint(voltages, pltpu.HBM)
+    early, tail = spectra(counts, table, halo, voltages, fir_taps)
     groups = frame_rows // 8
 
     def arrive(piece, part):

time: 221 us -> 220 us (level)
  transfers between devices with their start and end apart: 5 -> 5, of which waited for: 5 -> 4; matrix products, arithmetic and copies ran while one was open for 3% -> 3% of each run, Pallas kernels for 35% -> 36%
where the time goes in v5:
time: 220 us; the launch traced here: 219 us
  Pallas kernels  91.3 us (42%)
  waiting for transfers between devices  77.7 us (35%)
  blocking collectives  22.3 us (10%)
  starting transfers between devices  17.9 us (8%)
  local copies, waits for them, and re-layouts  9.04 us (4%)
    all_to_all x3, waiting for transfers between devices, exchange(): return lax.all_to_all(value, AXES, split_axis=0, concat_axis=0, tiled=True)  74.1 us
    pallas_call x1, Pallas kernels, beam_weights(): pl.pallas_call(weights_kernel, grid=(antennas // block, channels), in_spe...  51.5 us
    all_to_all x1, blocking collectives, exchange(): return lax.all_to_all(value, AXES, split_axis=0, concat_axis=0, tiled=True)  22.3 us
    pallas_call x2, Pallas kernels, form_beams(): pl.pallas_call(functools.partial(beam_kernel, wide, tm, first), grid=(cha...  18.6 us
    all_to_all x3, starting transfers between devices, exchange(): return lax.all_to_all(value, AXES, split_axis=0, concat_axis=0, tiled=True)  14.5 us
    pallas_call x1, Pallas kernels, spectra(): pl.pallas_call(functools.partial(spectra_kernel, (5 - taps) * width), gri...  9.5 us
    optimization_barrier x1, local copies, waits for them, and re-layouts, body(): lax.optimization_barrier((early, frequency, steering))  5.36 us
  transfers between devices with their start and end apart: 5, of which 4 were waited for; matrix products, arithmetic and copies ran while one was open for 3% of the time, Pallas kernels for 36%

profile of v5, /device:TPU:1, one launch (start us, length us, event | category | flops | bytes accessed | tf_op | source)
XLA Modules:
  0.0 219.5 jit_solution(6585091248062938326)
XLA Ops:
  0.0 1.2 slice.6
  1.2 2.7 %collective-permute-start = (bf16[2,256,768]{2,1,0:T(8,128)(2,1)S(1)}, bf16[2,256,768]{2,1,0:T(8,128)(2,1)S(1)}, u32[]{:S(2)}, u32[]{:S(2)}) collective-permute-start(bf16[2,256,768]{2,1,0:T(8,128)(2,1)S(1)} %slice.6), channel_id=1, source_target_pairs={{0,1},{1,2},{2,3},{3,0},{4,5},{5,6},{6,7},{7,4},{8,9},{9,10},{10,1... | collective-permute-start | bytes 2359304 | tf_op jit(solution)/shard_map/ppermute | solution.py:501
  3.8 9.5 %spectra.1 = (bf16[224,3,16,256]{3,2,1,0:T(8,128)(2,1)}, bf16[32,3,16,256]{3,2,1,0:T(8,128)(2,1)}, f32[2,4096,128]{2,1,0:T(8,128)S(1)}) custom-call(f32[4,256]{1,0:T(4,128)} %taps_ref.3, bf16[512,512]{1,0:T(8,128)(2,1)} %constant.38.clone.table_ref, bf16[2,256,6144]{2,1,0:T(8,128)(2,1)} %volt_ref.3, bf16[2,256,6144]{2,1,0:T(8,128)(2,1)} %volt_ref.3), custom_call_target="tpu_custom_call" | custom-call | flops 3221225472 | bytes 12582912 | tf_op jit(solution)/shard_map/spectra/pallas_call | solution.py:133
  13.3 0.0 collective-permute-done.past_ref
  13.3 4.2 %spectra_first.1 = (bf16[224,3,16,256]{3,2,1,0:T(8,128)(2,1)}, bf16[32,3,16,256]{3,2,1,0:T(8,128)(2,1)}) custom-call(f32[4,256]{1,0:T(4,128)} %taps_ref.3, bf16[512,512]{1,0:T(8,128)(2,1)} %constant.38.clone.table_ref, bf16[2,256,768]{2,1,0:T(8,128)(2,1)S(1)} %collective-permute-done.past_ref, ...), custom_call_target="tpu_custom_call", output_to_operand_aliasing={{0}: (5, {}), {1}: (6, {})} | custom-call | flops 402653184 | bytes 1572864 | tf_op jit(solution)/shard_map/spectra_first/pallas_call | solution.py:150
  17.5 0.0 copy-start.3
  17.5 6.4 %all-to-all-start = ((bf16[32,336,256]{2,1,0:T(8,128)(2,1)}), bf16[32,336,256]{2,1,0:T(8,128)(2,1)}, u32[]{:S(2)}, u32[]{:S(2)}) async-start(bf16[32,336,256]{2,1,0:T(8,128)(2,1)} %bitcast.31), calls=%async_computation | async-start | bytes 11010048 | tf_op jit(solution)/shard_map/all_to_all | solution.py:483
  24.0 0.0 copy-done.3
  24.0 0.2 reduce-window.9
  24.2 0.1 convert_reduce_fusion
  24.3 5.4 %copy.22 = f32[512,2048]{0,1:T(8,128)} copy(f32[512,2048]{1,0:T(8,128)} %param.9) | data formatting | bytes 8388608 | tf_op jit(solution)/shard_map/optimization_barrier | solution.py:519
  29.6 0.0 copy-start
  29.7 2.2 copy-done
  31.8 51.5 %weights.1.weight_ref = bf16[8,2048,1024]{2,1,0:T(8,128)(2,1)} custom-call(f32[8]{0:T(128)S(1)} %multiply_add_fusion.freq_ref, f32[2048,512]{1,0:T(8,128)S(1)} %bitcast.25), custom_call_target="tpu_custom_call" | custom-call | flops 251658240 | bytes 33554432 | tf_op jit(solution)/shard_map/weights/pallas_call | solution.py:227
  83.3 62.7 %all-to-all-done = bf16[32,336,256]{2,1,0:T(8,128)(2,1)} async-done(((bf16[32,336,256]{2,1,0:T(8,128)(2,1)}), bf16[32,336,256]{2,1,0:T(8,128)(2,1)}, u32[]{:S(2)}, u32[]{:S(2)}) %all-to-all-start) | async-done | bytes 5505056 | tf_op jit(solution)/shard_map/all_to_all | solution.py:483
  146.0 4.0 %all-to-all-start.1 = ((bf16[32,48,256]{2,1,0:T(8,128)(2,1)}), bf16[32,48,256]{2,1,0:T(8,128)(2,1)S(1)}, u32[]{:S(2)}, u32[]{:S(2)}) async-start(bf16[32,48,256]{2,1,0:T(8,128)(2,1)} %bitcast.8), calls=%async_computation.1 | async-start | bytes 1572864 | tf_op jit(solution)/shard_map/all_to_all | solution.py:483
  150.0 0.1 sub.15
  150.1 0.2 convert_reduce_fusion.1
  150.3 0.1 broadcast_compare_fusion
  150.4 14.7 %beams.2 = (f32[7,96,512]{2,1,0:T(8,128)S(1)}, f32[32,128]{1,0:T(8,128)S(1)}) custom-call(f32[32,128]{1,0:T(8,128)S(1)} %broadcast_in_dim.19.before_ref, bf16[32,7,3,16,256]{4,3,2,1,0:T(8,128)(2,1)} %bitcast.6.data_ref, bf16[8,2048,1024]{2,1,0:T(8,128)(2,1)} %weights.1.weight_ref), custom_call_target="tpu_custom_call" | custom-call | flops 5637144576 | bytes 29360128 | tf_op jit(solution)/shard_map/beams/pallas_call | solution.py:284
  165.1 5.0 %all-to-all-done.1 = bf16[32,48,256]{2,1,0:T(8,128)(2,1)S(1)} async-done(((bf16[32,48,256]{2,1,0:T(8,128)(2,1)}), bf16[32,48,256]{2,1,0:T(8,128)(2,1)S(1)}, u32[]{:S(2)}, u32[]{:S(2)}) %all-to-all-start.1) | async-done | bytes 786464 | tf_op jit(solution)/shard_map/all_to_all | solution.py:483
  170.1 3.9 %beams.3 = (f32[1,96,512]{2,1,0:T(8,128)S(1)}, f32[32,128]{1,0:T(8,128)}) custom-call(f32[32,128]{1,0:T(8,128)S(1)} %get-tuple-element.32.before_ref, bf16[32,1,3,16,256]{4,3,2,1,0:T(8,128)(2,1)S(1)} %bitcast.29, bf16[8,2048,1024]{2,1,0:T(8,128)(2,1)} %weights.1.weight_ref), custom_call_target="tpu_custom_call" | custom-call | flops 805306368 | bytes 4194304 | tf_op jit(solution)/shard_map/beams/pallas_call | solution.py:284
  174.1 0.0 copy-start.2
  174.1 0.0 copy-start.1
  174.1 4.1 %all-to-all-start.2 = ((f32[32,1,128]{2,1,0:T(1,128)}), f32[32,1,128]{2,1,0:T(1,128)S(1)}, u32[]{:S(2)}, u32[]{:S(2)}) async-start(f32[32,1,128]{2,1,0:T(1,128)} %bitcast.11), calls=%async_computation.2 | async-start | bytes 32768 | tf_op jit(solution)/shard_map/all_to_all | solution.py:483
  178.2 0.2 select_reduce_fusion
  178.4 0.1 copy.24.count_ref
  178.4 6.4 %all-to-all-done.2 = f32[32,1,128]{2,1,0:T(1,128)S(1)} async-done(((f32[32,1,128]{2,1,0:T(1,128)}), f32[32,1,128]{2,1,0:T(1,128)S(1)}, u32[]{:S(2)}, u32[]{:S(2)}) %all-to-all-start.2) | async-done | bytes 16416 | tf_op jit(solution)/shard_map/all_to_all | solution.py:483
  184.9 0.9 levels.1
  185.8 22.3 %all_to_all.26 = bf16[32,8,1536]{2,1,0:T(8,128)(2,1)S(1)} all-to-all(bf16[32,8,1536]{2,1,0:T(8,128)(2,1)S(1)} %levels.1), channel_id=1, replica_groups=mesh['wide'=8,'tm'=4] {'wide','tm'}, dimensions={0} | all-to-all | bytes 1572864 | tf_op jit(solution)/shard_map/all_to_all | solution.py:483
  208.1 0.8 collective-permute-start.1
  208.9 0.0 copy-done.2
  208.9 0.1 copy.21
  209.0 0.3 fusion.pick_ref
  209.3 0.0 copy-done.1
  209.4 3.2 %search_early.1 = (f32[4,1536,128]{2,1,0:T(8,128)}, f32[448,128]{1,0:T(8,128)S(1)}) custom-call(s32[4]{0:T(128)S(1)} %copy-done.1, bf16[2048,128]{1,0:T(8,128)(2,1)S(1)} %fusion.pick_ref, bf16[256,1536]{1,0:T(8,128)(2,1)S(1)} %bitcast.27), custom_call_target="tpu_custom_call" | custom-call | tf_op jit(solution)/shard_map/search_early/pallas_call | solution.py:437
  212.5 3.6 %collective-permute-done.1.halo_ref = bf16[256,896]{1,0:T(8,128)(2,1)S(1)} collective-permute-done((bf16[256,896]{1,0:T(8,128)(2,1)S(1)}, bf16[256,896]{1,0:T(8,128)(2,1)S(1)}, u32[]{:S(2)}, u32[]{:S(2)}) %collective-permute-start.1) | collective-permute-done | bytes 458784 | tf_op jit(solution)/shard_map/ppermute | solution.py:455
  216.1 3.3 %search_late.1 = f32[4,1536,128]{2,1,0:T(8,128)} custom-call(s32[4]{0:T(128)S(1)} %copy-done.1, bf16[2048,128]{1,0:T(8,128)(2,1)S(1)} %fusion.pick_ref, bf16[256,1536]{1,0:T(8,128)(2,1)S(1)} %bitcast.28, bf16[256,896]{1,0:T(8,128)(2,1)S(1)} %collective-permute-done.1.halo_ref, ...), custom_call_target="tpu_custom_call", output_to_operand_aliasing={{}: (5, {})} | custom-call | tf_op jit(solution)/shard_map/search_late/pallas_call | solution.py:458
  (10 shorter events, 0.1 us)
Async XLA Ops:
  1.2 12.2 %collective-permute-start = (bf16[2,256,768]{2,1,0:T(8,128)(2,1)S(1)}, bf16[2,256,768]{2,1,0:T(8,128)(2,1)S(1)}, u32[]{:S(2)}, u32[]{:S(2)}) collective-permute-start(bf16[2,256,768]{2,1,0:T(8,128)(2,1)S(1)} %slice.6), channel_id=1, source_target_pairs={{0,1},{1,2},{2,3},{3,0},{4,5},{5,6},{6,7},{7,4},{8,9},{9,10},{10,1... | collective-permute-start | bytes 2359304 | tf_op jit(solution)/shard_map/ppermute | solution.py:501
  17.5 6.5 %copy-start.3 = (s32[8]{0:T(128)S(1)}, s32[8]{0:T(128)}, u32[]{:S(2)}) copy-start(s32[8]{0:T(128)} %param.10) | copy-start | bytes 100
  17.5 128.5 %all-to-all-start = ((bf16[32,336,256]{2,1,0:T(8,128)(2,1)}), bf16[32,336,256]{2,1,0:T(8,128)(2,1)}, u32[]{:S(2)}, u32[]{:S(2)}) async-start(bf16[32,336,256]{2,1,0:T(8,128)(2,1)} %bitcast.31), calls=%async_computation | async-start | bytes 11010048 | tf_op jit(solution)/shard_map/all_to_all | solution.py:483
  29.6 2.2 copy-start
  146.0 24.1 %all-to-all-start.1 = ((bf16[32,48,256]{2,1,0:T(8,128)(2,1)}), bf16[32,48,256]{2,1,0:T(8,128)(2,1)S(1)}, u32[]{:S(2)}, u32[]{:S(2)}) async-start(bf16[32,48,256]{2,1,0:T(8,128)(2,1)} %bitcast.8), calls=%async_computation.1 | async-start | bytes 1572864 | tf_op jit(solution)/shard_map/all_to_all | solution.py:483
  174.1 34.8 %copy-start.2 = (s32[128,256]{1,0:T(8,128)S(1)}, s32[128,256]{1,0:T(8,128)}, u32[]{:S(2)}) copy-start(s32[128,256]{1,0:T(8,128)} %param.11) | copy-start | bytes 393220
  174.1 35.3 %copy-start.1 = (s32[4]{0:T(128)S(1)}, s32[4]{0:T(128)}, u32[]{:S(2)}) copy-start(s32[4]{0:T(128)} %width_ref.3) | copy-start | bytes 52
  174.1 10.8 %all-to-all-start.2 = ((f32[32,1,128]{2,1,0:T(1,128)}), f32[32,1,128]{2,1,0:T(1,128)S(1)}, u32[]{:S(2)}, u32[]{:S(2)}) async-start(f32[32,1,128]{2,1,0:T(1,128)} %bitcast.11), calls=%async_computation.2 | async-start | bytes 32768 | tf_op jit(solution)/shard_map/all_to_all | solution.py:483
  208.1 8.0 %collective-permute-start.1 = (bf16[256,896]{1,0:T(8,128)(2,1)S(1)}, bf16[256,896]{1,0:T(8,128)(2,1)S(1)}, u32[]{:S(2)}, u32[]{:S(2)}) collective-permute-start(bf16[256,896]{1,0:T(8,128)(2,1)S(1)} %slice.8), channel_id=1, source_target_pairs={{0,3},{1,0},{2,1},{3,2},{4,7},{5,4},{6,5},{7,6},{8,11},{9,8},{10,9... | collective-permute-start | bytes 1376264 | tf_op jit(solution)/shard_map/ppermute | solution.py:455

commit v6 on v5

--- a/solution.py
+++ b/solution.py
@@ -106,7 +106,7 @@
     out_refs, part_ref = rest[count:-1], rest[-1]
     fresh = taps_ref.shape[0] - 1
     transform(range(fresh), 0, taps_ref, table_ref, past_ref, volt_ref, part_ref)
-    write_out(part_ref, out_refs, kept_ref, fresh)
+    write_out(part_ref, out_refs, kept_ref.at[pl.ds(pl.program_id(0), 1)], fresh)
 
 
 def spectra(counts, table, halo, voltages, fir_taps):
@@ -116,8 +116,10 @@
     part = pltpu.VMEM((-(-antennas // 128), 2 * width * 8, 128), jnp.float32)
     shapes = [pltpu.HBM((count, groups, 16, antennas), jnp.bfloat16) for count in counts]
 
-    def blocks(place):
-        return [pl.BlockSpec((count, 1, 16, antennas), place) for count in counts]
+    size = 128 if antennas % 128 == 0 else antennas
+
+    def blocks(place, size):
+        return [pl.BlockSpec((count, 1, 16, size), place) for count in counts]
 
     def cost(frames):
         return pl.CostEstimate(
@@ -138,7 +140,7 @@
             pl.BlockSpec((2, antennas, 4 * width), lambda g: (0, 0, jnp.maximum(2 * g - 1, 1))),
             pl.BlockSpec((2, antennas, 8 * width), lambda g: (0, 0, g)),
         ],
-        out_specs=blocks(lambda g: (0, jnp.maximum(g, 1), 0, 0))
+        out_specs=blocks(lambda g: (0, jnp.maximum(g, 1), 0, 0), antennas)
         + [pl.BlockSpec(memory_space=pltpu.VMEM)],
         out_shape=shapes + [part],
         scratch_shapes=[part],
@@ -149,17 +151,17 @@
     kept = pltpu.with_memory_space_constraint(kept, pltpu.VMEM)
     return pl.pallas_call(
         spectra_first_kernel,
-        grid=(1,),
+        grid=(antennas // size,),
         in_specs=common
         + [
-            pl.BlockSpec(halo.shape, lambda g: (0, 0, 0)),
-            pl.BlockSpec((2, antennas, 4 * width), lambda g: (0, 0, 0)),
+            pl.BlockSpec((2, size, halo.shape[2]), lambda h: (0, h, 0)),
+            pl.BlockSpec((2, size, 4 * width), lambda h: (0, h, 0)),
             pl.BlockSpec(memory_space=pltpu.VMEM),
         ]
         + [pl.BlockSpec(memory_space=pl.ANY)] * len(counts),
-        out_specs=blocks(lambda g: (0, 0, 0, 0)),
+        out_specs=blocks(lambda h: (0, 0, 0, h), size),
         out_shape=shapes,
-        scratch_shapes=[part],
+        scratch_shapes=[pltpu.VMEM((1, 2 * width * 8, 128), jnp.float32)],
         input_output_aliases={5 + i: i for i in range(len(counts))},
         compiler_params=pltpu.CompilerParams(vmem_limit_bytes=32 * MIB),
         cost_estimate=cost(taps - 1),
@@ -243,8 +245,24 @@
     )(frequency, steering_t)
 
 
-def beam_kernel(wide, tm, first, before_ref, data_ref, weight_ref, power_ref, sum_ref, gather_ref, acc_ref):
+def beam_kernel(
+    wide, tm, first, before_ref, data_ref, weight_ref, power_ref, sum_ref, gather_ref, acc_ref,
+    *rest,
+):
     channel = pl.program_id(0)
+    copies = []
+    if rest:
+        held_ref, sems = rest
+        steps = sems.shape[0]
+        depth = held_ref.shape[0] // steps
+        for step in range(steps):
+            rows = pl.ds(step * depth, depth)
+            copies.append(
+                pltpu.make_async_copy(
+                    weight_ref.at[channel + first, rows], held_ref.at[rows], sems.at[step]
+                )
+            )
+            copies[-1].start()
     groups = data_ref.shape[2]
     antennas = data_ref.shape[4]
     rows = groups * 16
@@ -253,7 +271,17 @@
             gather_ref[m * rows : (m + 1) * rows, w * antennas : (w + 1) * antennas] = data_ref[
                 w * tm + m, 0
             ].reshape(rows, antennas)
-    products = jnp.dot(gather_ref[...], weight_ref[0], preferred_element_type=jnp.float32)
+    if copies:
+        products = None
+        for step, copy in enumerate(copies):
+            copy.wait()
+            own = slice(step * depth, (step + 1) * depth)
+            term = jnp.dot(
+                gather_ref[:, own], held_ref[own, :], preferred_element_type=jnp.float32
+            )
+            products = term if products is None else products + term
+    else:
+        products = jnp.dot(gather_ref[...], weight_ref[0], preferred_element_type=jnp.float32)
     beams = products.shape[1] // 2
     products = products.reshape(tm * groups, 2, 8, 2 * beams)
     real_in = products[:, 0]
@@ -276,7 +304,7 @@
         sum_ref[...] = jnp.broadcast_to(acc_ref[...], sum_ref.shape)
 
 
-def form_beams(received, weights, before, first, wide, tm):
+def form_beams(received, weights, before, first, wide, tm, quarters):
     devices, channels, groups, _, antennas = received.shape
     _, antenna_full, twice = weights.shape
     frames = tm * groups * 8
@@ -287,7 +315,9 @@
         in_specs=[
             pl.BlockSpec((devices, 128), lambda c: (0, 0)),
             pl.BlockSpec((devices, 1, groups, 16, antennas), lambda c: (0, c, 0, 0, 0)),
-            pl.BlockSpec((1, antenna_full, twice), lambda c: (c + first, 0, 0)),
+            pl.BlockSpec(memory_space=pl.ANY)
+            if quarters
+            else pl.BlockSpec((1, antenna_full, twice), lambda c: (c + first, 0, 0)),
         ],
         out_specs=[
             pl.BlockSpec((1, frames, beams), lambda c: (c, 0, 0)),
@@ -300,7 +330,15 @@
         scratch_shapes=[
             pltpu.VMEM((2 * frames, antenna_full), jnp.bfloat16),
             pltpu.VMEM((1, 128), jnp.float32),
-        ],
+        ]
+        + (
+            [
+                pltpu.VMEM((antenna_full, twice), jnp.bfloat16),
+                pltpu.SemaphoreType.DMA((quarters,)),
+            ]
+            if quarters
+            else []
+        ),
         compiler_params=pltpu.CompilerParams(vmem_limit_bytes=48 * MIB),
         cost_estimate=pl.CostEstimate(
             flops=4 * channels * frames * antenna_full * twice,
@@ -521,8 +559,10 @@
     early = arrive(early, parts[0])
     early, tail, weights = lax.optimization_barrier((early, tail, weights))
     sums = jnp.zeros((devices, 128), jnp.float32)
-    power, sums = form_beams(early, weights, sums, 0, wide, tm)
-    late, sums = form_beams(arrive(tail, parts[1]), weights, sums, parts[0], wide, tm)
+    power, sums = form_beams(early, weights, sums, 0, wide, tm, 0)
+    late, sums = form_beams(
+        arrive(tail, parts[1]), weights, sums, parts[0], wide, tm, 4
+    )
     powers = [power, late]
 
     starts = jnp.cumsum(band_widths) - band_widths

time: 220 us -> 219 us (level)
  no operation moved by 1% of the time
where the time goes in v6:
time: 219 us
  Pallas kernels  90.6 us (41%)
  waiting for transfers between devices  77.7 us (35%)
  blocking collectives  22.3 us (10%)
  starting transfers between devices  17.9 us (8%)
  local copies, waits for them, and re-layouts  9.05 us (4%)
    all_to_all x3, waiting for transfers between devices, exchange(): return lax.all_to_all(value, AXES, split_axis=0, concat_axis=0, tiled=True)  74.1 us
    pallas_call x1, Pallas kernels, beam_weights(): pl.pallas_call(weights_kernel, grid=(antennas // block, channels), in_spe...  51.5 us
    all_to_all x1, blocking collectives, exchange(): return lax.all_to_all(value, AXES, split_axis=0, concat_axis=0, tiled=True)  22.3 us
    pallas_call x2, Pallas kernels, form_beams(): pl.pallas_call(functools.partial(beam_kernel, wide, tm, first), grid=(cha...  18.1 us
    all_to_all x3, starting transfers between devices, exchange(): return lax.all_to_all(value, AXES, split_axis=0, concat_axis=0, tiled=True)  14.5 us
    pallas_call x1, Pallas kernels, spectra(): pl.pallas_call(functools.partial(spectra_kernel, (5 - taps) * width), gri...  9.5 us
    optimization_barrier x1, local copies, waits for them, and re-layouts, body(): lax.optimization_barrier((early, frequency, steering))  5.36 us
  transfers between devices with their start and end apart: 5, of which 4 were waited for; matrix products, arithmetic and copies ran while one was open for 3% of the time, Pallas kernels for 36%

profile of v6, /device:TPU:1, one launch (start us, length us, event | category | flops | bytes accessed | tf_op | source)
XLA Modules:
  0.0 218.8 jit_solution(16665801295536546117)
XLA Ops:
  0.0 1.2 slice.6
  1.2 2.7 %collective-permute-start = (bf16[2,256,768]{2,1,0:T(8,128)(2,1)S(1)}, bf16[2,256,768]{2,1,0:T(8,128)(2,1)S(1)}, u32[]{:S(2)}, u32[]{:S(2)}) collective-permute-start(bf16[2,256,768]{2,1,0:T(8,128)(2,1)S(1)} %slice.6), channel_id=1, source_target_pairs={{0,1},{1,2},{2,3},{3,0},{4,5},{5,6},{6,7},{7,4},{8,9},{9,10},{10,1... | collective-permute-start | bytes 2359304 | tf_op jit(solution)/shard_map/ppermute | solution.py:539
  3.8 9.5 %spectra.1 = (bf16[224,3,16,256]{3,2,1,0:T(8,128)(2,1)}, bf16[32,3,16,256]{3,2,1,0:T(8,128)(2,1)}, f32[2,4096,128]{2,1,0:T(8,128)S(1)}) custom-call(f32[4,256]{1,0:T(4,128)} %taps_ref.3, bf16[512,512]{1,0:T(8,128)(2,1)} %constant.38.clone.table_ref, bf16[2,256,6144]{2,1,0:T(8,128)(2,1)} %volt_ref.3, bf16[2,256,6144]{2,1,0:T(8,128)(2,1)} %volt_ref.3), custom_call_target="tpu_custom_call" | custom-call | flops 3221225472 | bytes 12582912 | tf_op jit(solution)/shard_map/spectra/pallas_call | solution.py:135
  13.3 0.0 collective-permute-done.past_ref
  13.3 4.0 %spectra_first.1 = (bf16[224,3,16,256]{3,2,1,0:T(8,128)(2,1)}, bf16[32,3,16,256]{3,2,1,0:T(8,128)(2,1)}) custom-call(f32[4,256]{1,0:T(4,128)} %taps_ref.3, bf16[512,512]{1,0:T(8,128)(2,1)} %constant.38.clone.table_ref, bf16[2,256,768]{2,1,0:T(8,128)(2,1)S(1)} %collective-permute-done.past_ref, ...), custom_call_target="tpu_custom_call", output_to_operand_aliasing={{0}: (5, {}), {1}: (6, {})} | custom-call | flops 402653184 | bytes 1572864 | tf_op jit(solution)/shard_map/spectra_first/pallas_call | solution.py:152
  17.4 0.0 copy-start.3
  17.4 6.4 %all-to-all-start = ((bf16[32,336,256]{2,1,0:T(8,128)(2,1)}), bf16[32,336,256]{2,1,0:T(8,128)(2,1)}, u32[]{:S(2)}, u32[]{:S(2)}) async-start(bf16[32,336,256]{2,1,0:T(8,128)(2,1)} %bitcast.31), calls=%async_computation | async-start | bytes 11010048 | tf_op jit(solution)/shard_map/all_to_all | solution.py:521
  23.8 0.0 copy-done.3
  23.8 0.2 reduce-window.9
  24.0 0.1 convert_reduce_fusion
  24.1 5.4 %copy.22 = f32[512,2048]{0,1:T(8,128)} copy(f32[512,2048]{1,0:T(8,128)} %param.9) | data formatting | bytes 8388608 | tf_op jit(solution)/shard_map/optimization_barrier | solution.py:557
  29.4 0.0 copy-start
  29.4 2.2 copy-done
  31.6 51.5 %weights.1.weight_ref = bf16[8,2048,1024]{2,1,0:T(8,128)(2,1)} custom-call(f32[8]{0:T(128)S(1)} %multiply_add_fusion.freq_ref, f32[2048,512]{1,0:T(8,128)S(1)} %bitcast.25), custom_call_target="tpu_custom_call" | custom-call | flops 251658240 | bytes 33554432 | tf_op jit(solution)/shard_map/weights/pallas_call | solution.py:229
  83.1 62.7 %all-to-all-done = bf16[32,336,256]{2,1,0:T(8,128)(2,1)} async-done(((bf16[32,336,256]{2,1,0:T(8,128)(2,1)}), bf16[32,336,256]{2,1,0:T(8,128)(2,1)}, u32[]{:S(2)}, u32[]{:S(2)}) %all-to-all-start) | async-done | bytes 5505056 | tf_op jit(solution)/shard_map/all_to_all | solution.py:521
  145.8 4.0 %all-to-all-start.1 = ((bf16[32,48,256]{2,1,0:T(8,128)(2,1)}), bf16[32,48,256]{2,1,0:T(8,128)(2,1)S(1)}, u32[]{:S(2)}, u32[]{:S(2)}) async-start(bf16[32,48,256]{2,1,0:T(8,128)(2,1)} %bitcast.8), calls=%async_computation.1 | async-start | bytes 1572864 | tf_op jit(solution)/shard_map/all_to_all | solution.py:521
  149.8 0.1 sub.15
  149.8 0.2 convert_reduce_fusion.1
  150.0 0.1 broadcast_compare_fusion
  150.2 14.7 %beams.2 = (f32[7,96,512]{2,1,0:T(8,128)S(1)}, f32[32,128]{1,0:T(8,128)S(1)}) custom-call(f32[32,128]{1,0:T(8,128)S(1)} %broadcast_in_dim.19.before_ref, bf16[32,7,3,16,256]{4,3,2,1,0:T(8,128)(2,1)} %bitcast.6.data_ref, bf16[8,2048,1024]{2,1,0:T(8,128)(2,1)} %weights.1.weight_ref), custom_call_target="tpu_custom_call" | custom-call | flops 5637144576 | bytes 29360128 | tf_op jit(solution)/shard_map/beams/pallas_call | solution.py:312
  164.9 5.0 %all-to-all-done.1 = bf16[32,48,256]{2,1,0:T(8,128)(2,1)S(1)} async-done(((bf16[32,48,256]{2,1,0:T(8,128)(2,1)}), bf16[32,48,256]{2,1,0:T(8,128)(2,1)S(1)}, u32[]{:S(2)}, u32[]{:S(2)}) %all-to-all-start.1) | async-done | bytes 786464 | tf_op jit(solution)/shard_map/all_to_all | solution.py:521
  169.9 3.4 %beams.3 = (f32[1,96,512]{2,1,0:T(8,128)S(1)}, f32[32,128]{1,0:T(8,128)}) custom-call(f32[32,128]{1,0:T(8,128)S(1)} %get-tuple-element.32.before_ref, bf16[32,1,3,16,256]{4,3,2,1,0:T(8,128)(2,1)S(1)} %bitcast.29, bf16[8,2048,1024]{2,1,0:T(8,128)(2,1)} %weights.1.weight_ref), custom_call_target="tpu_custom_call" | custom-call | flops 805306368 | bytes 4194304 | tf_op jit(solution)/shard_map/beams/pallas_call | solution.py:312
  173.4 0.0 copy-start.2
  173.4 0.0 copy-start.1
  173.4 4.1 %all-to-all-start.2 = ((f32[32,1,128]{2,1,0:T(1,128)}), f32[32,1,128]{2,1,0:T(1,128)S(1)}, u32[]{:S(2)}, u32[]{:S(2)}) async-start(f32[32,1,128]{2,1,0:T(1,128)} %bitcast.11), calls=%async_computation.2 | async-start | bytes 32768 | tf_op jit(solution)/shard_map/all_to_all | solution.py:521
  177.5 0.2 select_reduce_fusion
  177.7 0.1 copy.24.count_ref
  177.7 6.4 %all-to-all-done.2 = f32[32,1,128]{2,1,0:T(1,128)S(1)} async-done(((f32[32,1,128]{2,1,0:T(1,128)}), f32[32,1,128]{2,1,0:T(1,128)S(1)}, u32[]{:S(2)}, u32[]{:S(2)}) %all-to-all-start.2) | async-done | bytes 16416 | tf_op jit(solution)/shard_map/all_to_all | solution.py:521
  184.2 0.9 levels.1
  185.1 22.3 %all_to_all.26 = bf16[32,8,1536]{2,1,0:T(8,128)(2,1)S(1)} all-to-all(bf16[32,8,1536]{2,1,0:T(8,128)(2,1)S(1)} %levels.1), channel_id=1, replica_groups=mesh['wide'=8,'tm'=4] {'wide','tm'}, dimensions={0} | all-to-all | bytes 1572864 | tf_op jit(solution)/shard_map/all_to_all | solution.py:521
  207.4 0.8 collective-permute-start.1
  208.2 0.0 copy-done.2
  208.2 0.1 copy.21
  208.3 0.3 fusion.pick_ref
  208.6 0.0 copy-done.1
  208.7 3.2 %search_early.1 = (f32[4,1536,128]{2,1,0:T(8,128)}, f32[448,128]{1,0:T(8,128)S(1)}) custom-call(s32[4]{0:T(128)S(1)} %copy-done.1, bf16[2048,128]{1,0:T(8,128)(2,1)S(1)} %fusion.pick_ref, bf16[256,1536]{1,0:T(8,128)(2,1)S(1)} %bitcast.27), custom_call_target="tpu_custom_call" | custom-call | tf_op jit(solution)/shard_map/search_early/pallas_call | solution.py:475
  211.9 3.6 %collective-permute-done.1.halo_ref = bf16[256,896]{1,0:T(8,128)(2,1)S(1)} collective-permute-done((bf16[256,896]{1,0:T(8,128)(2,1)S(1)}, bf16[256,896]{1,0:T(8,128)(2,1)S(1)}, u32[]{:S(2)}, u32[]{:S(2)}) %collective-permute-start.1) | collective-permute-done | bytes 458784 | tf_op jit(solution)/shard_map/ppermute | solution.py:493
  215.4 3.3 %search_late.1 = f32[4,1536,128]{2,1,0:T(8,128)} custom-call(s32[4]{0:T(128)S(1)} %copy-done.1, bf16[2048,128]{1,0:T(8,128)(2,1)S(1)} %fusion.pick_ref, bf16[256,1536]{1,0:T(8,128)(2,1)S(1)} %bitcast.28, bf16[256,896]{1,0:T(8,128)(2,1)S(1)} %collective-permute-done.1.halo_ref, ...), custom_call_target="tpu_custom_call", output_to_operand_aliasing={{}: (5, {})} | custom-call | tf_op jit(solution)/shard_map/search_late/pallas_call | solution.py:496
  (10 shorter events, 0.1 us)
Async XLA Ops:
  1.2 12.2 %collective-permute-start = (bf16[2,256,768]{2,1,0:T(8,128)(2,1)S(1)}, bf16[2,256,768]{2,1,0:T(8,128)(2,1)S(1)}, u32[]{:S(2)}, u32[]{:S(2)}) collective-permute-start(bf16[2,256,768]{2,1,0:T(8,128)(2,1)S(1)} %slice.6), channel_id=1, source_target_pairs={{0,1},{1,2},{2,3},{3,0},{4,5},{5,6},{6,7},{7,4},{8,9},{9,10},{10,1... | collective-permute-start | bytes 2359304 | tf_op jit(solution)/shard_map/ppermute | solution.py:539
  17.4 6.4 %copy-start.3 = (s32[8]{0:T(128)S(1)}, s32[8]{0:T(128)}, u32[]{:S(2)}) copy-start(s32[8]{0:T(128)} %param.10) | copy-start | bytes 100
  17.4 128.4 %all-to-all-start = ((bf16[32,336,256]{2,1,0:T(8,128)(2,1)}), bf16[32,336,256]{2,1,0:T(8,128)(2,1)}, u32[]{:S(2)}, u32[]{:S(2)}) async-start(bf16[32,336,256]{2,1,0:T(8,128)(2,1)} %bitcast.31), calls=%async_computation | async-start | bytes 11010048 | tf_op jit(solution)/shard_map/all_to_all | solution.py:521
  29.4 2.2 %copy-start = (f32[512,2048]{0,1:T(8,128)S(1)}, f32[512,2048]{0,1:T(8,128)}, u32[]{:S(2)}) copy-start(f32[512,2048]{0,1:T(8,128)} %copy.22) | copy-start | bytes 12582916
  145.8 24.1 %all-to-all-start.1 = ((bf16[32,48,256]{2,1,0:T(8,128)(2,1)}), bf16[32,48,256]{2,1,0:T(8,128)(2,1)S(1)}, u32[]{:S(2)}, u32[]{:S(2)}) async-start(bf16[32,48,256]{2,1,0:T(8,128)(2,1)} %bitcast.8), calls=%async_computation.1 | async-start | bytes 1572864 | tf_op jit(solution)/shard_map/all_to_all | solution.py:521
  173.4 34.8 %copy-start.2 = (s32[128,256]{1,0:T(8,128)S(1)}, s32[128,256]{1,0:T(8,128)}, u32[]{:S(2)}) copy-start(s32[128,256]{1,0:T(8,128)} %param.11) | copy-start | bytes 393220
  173.4 35.3 %copy-start.1 = (s32[4]{0:T(128)S(1)}, s32[4]{0:T(128)}, u32[]{:S(2)}) copy-start(s32[4]{0:T(128)} %width_ref.3) | copy-start | bytes 52
  173.4 10.8 %all-to-all-start.2 = ((f32[32,1,128]{2,1,0:T(1,128)}), f32[32,1,128]{2,1,0:T(1,128)S(1)}, u32[]{:S(2)}, u32[]{:S(2)}) async-start(f32[32,1,128]{2,1,0:T(1,128)} %bitcast.11), calls=%async_computation.2 | async-start | bytes 32768 | tf_op jit(solution)/shard_map/all_to_all | solution.py:521
  207.4 8.0 %collective-permute-start.1 = (bf16[256,896]{1,0:T(8,128)(2,1)S(1)}, bf16[256,896]{1,0:T(8,128)(2,1)S(1)}, u32[]{:S(2)}, u32[]{:S(2)}) collective-permute-start(bf16[256,896]{1,0:T(8,128)(2,1)S(1)} %slice.8), channel_id=1, source_target_pairs={{0,3},{1,0},{2,1},{3,2},{4,7},{5,4},{6,5},{7,6},{8,11},{9,8},{10,9... | collective-permute-start | bytes 1376264 | tf_op jit(solution)/shard_map/ppermute | solution.py:493

commit v7 on v6

--- a/solution.py
+++ b/solution.py
@@ -436,28 +436,29 @@
 
 
 def search_early_kernel(
-    beams, width_ref, pick_ref, level_ref, out_ref, kept_ref, turn_ref, sum_ref, stage_ref, sems
+    beams, width_ref, pick_ref, level_ref, out_ref, kept_ref, last_ref, turn_ref, sum_ref, stage_ref,
+    sems,
 ):
     channels, lanes = level_ref.shape
     turn(level_ref, 0, lanes, turn_ref, 0)
     known = sum_ref.shape[1]
     dedisperse(turn_ref, pick_ref, sum_ref, 0, known // beams, beams)
     kept_ref[...] = sum_ref[0, known - kept_ref.shape[0] :, :]
+    last_ref[...] = turn_ref[lanes - last_ref.shape[0] :, :]
     boxcars(channels, width_ref, sum_ref, stage_ref, out_ref, sems, 0, beams)
 
 
 def search_late_kernel(
-    beams, width_ref, pick_ref, level_ref, halo_ref, kept_ref, given_ref, out_ref, turn_ref,
+    beams, width_ref, pick_ref, last_ref, halo_ref, kept_ref, given_ref, out_ref, turn_ref,
     sum_ref, stage_ref, sems,
 ):
-    channels, lanes = level_ref.shape
-    held = MAXDELAY * beams
-    turn(level_ref, lanes - held, held, turn_ref, 0)
+    held, channels = last_ref.shape
+    turn_ref[:held, :] = last_ref[...]
     turn(halo_ref, 0, halo_ref.shape[1], turn_ref, held)
     kept = kept_ref.shape[0]
     sum_ref[0, :kept, :] = kept_ref[...]
     dedisperse(turn_ref, pick_ref, sum_ref, kept, sum_ref.shape[1] // beams - WMAX + 1, beams)
-    row = lanes - stage_ref.shape[1]
+    row = out_ref.shape[1] - stage_ref.shape[1]
     boxcars(channels, width_ref, sum_ref, stage_ref, out_ref, sems, row, beams)
 
 
@@ -472,13 +473,14 @@
     late = frames - early
     whole = pl.BlockSpec(memory_space=pltpu.VMEM)
     params = pltpu.CompilerParams(vmem_limit_bytes=32 * MIB)
-    found, kept = pl.pallas_call(
+    found, kept, last = pl.pallas_call(
         functools.partial(search_early_kernel, beams),
         in_specs=[pl.BlockSpec(memory_space=pltpu.SMEM), whole, whole],
-        out_specs=[pl.BlockSpec(memory_space=pl.ANY), whole],
+        out_specs=[pl.BlockSpec(memory_space=pl.ANY), whole, whole],
         out_shape=[
             jax.ShapeDtypeStruct((widths, lanes, trials), jnp.float32),
             jax.ShapeDtypeStruct((lags * beams, trials), jnp.float32),
+            jax.ShapeDtypeStruct((MAXDELAY * beams, channels), jnp.bfloat16),
         ],
         scratch_shapes=[
             pltpu.VMEM((lanes, channels), jnp.bfloat16),
@@ -514,7 +516,7 @@
         input_output_aliases={5: 0},
         compiler_params=params,
         name="search_late",
-    )(box_widths, picks, levels, halo, kept, found)
+    )(box_widths, picks, last, halo, kept, found)
 
 
 def exchange(value):

time: 219 us -> 219 us (level)
  no operation moved by 1% of the time
where the time goes in v7:
time: 219 us
  Pallas kernels  90.4 us (41%)
  waiting for transfers between devices  77.7 us (35%)
  blocking collectives  22.3 us (10%)
  starting transfers between devices  17.9 us (8%)
  local copies, waits for them, and re-layouts  9.05 us (4%)
    all_to_all x3, waiting for transfers between devices, exchange(): return lax.all_to_all(value, AXES, split_axis=0, concat_axis=0, tiled=True)  74.1 us
    pallas_call x1, Pallas kernels, beam_weights(): pl.pallas_call(weights_kernel, grid=(antennas // block, channels), in_spe...  51.5 us
    all_to_all x1, blocking collectives, exchange(): return lax.all_to_all(value, AXES, split_axis=0, concat_axis=0, tiled=True)  22.3 us
    pallas_call x2, Pallas kernels, form_beams(): pl.pallas_call(functools.partial(beam_kernel, wide, tm, first), grid=(cha...  18.1 us
    all_to_all x3, starting transfers between devices, exchange(): return lax.all_to_all(value, AXES, split_axis=0, concat_axis=0, tiled=True)  14.5 us
    pallas_call x1, Pallas kernels, spectra(): pl.pallas_call(functools.partial(spectra_kernel, (5 - taps) * width), gri...  9.5 us
    optimization_barrier x1, local copies, waits for them, and re-layouts, body(): lax.optimization_barrier((early, frequency, steering))  5.36 us
  transfers between devices with their start and end apart: 5, of which 4 were waited for; matrix products, arithmetic and copies ran while one was open for 3% of the time, Pallas kernels for 36%

profile of v7, /device:TPU:1, one launch (start us, length us, event | category | flops | bytes accessed | tf_op | source)
XLA Modules:
  0.0 218.6 jit_solution(4739167241442951657)
XLA Ops:
  0.0 1.2 slice.6
  1.2 2.7 %collective-permute-start = (bf16[2,256,768]{2,1,0:T(8,128)(2,1)S(1)}, bf16[2,256,768]{2,1,0:T(8,128)(2,1)S(1)}, u32[]{:S(2)}, u32[]{:S(2)}) collective-permute-start(bf16[2,256,768]{2,1,0:T(8,128)(2,1)S(1)} %slice.6), channel_id=1, source_target_pairs={{0,1},{1,2},{2,3},{3,0},{4,5},{5,6},{6,7},{7,4},{8,9},{9,10},{10,1... | collective-permute-start | bytes 2359304 | tf_op jit(solution)/shard_map/ppermute | solution.py:541
  3.8 9.5 %spectra.1 = (bf16[224,3,16,256]{3,2,1,0:T(8,128)(2,1)}, bf16[32,3,16,256]{3,2,1,0:T(8,128)(2,1)}, f32[2,4096,128]{2,1,0:T(8,128)S(1)}) custom-call(f32[4,256]{1,0:T(4,128)} %taps_ref.3, bf16[512,512]{1,0:T(8,128)(2,1)} %constant.38.clone.table_ref, bf16[2,256,6144]{2,1,0:T(8,128)(2,1)} %volt_ref.3, bf16[2,256,6144]{2,1,0:T(8,128)(2,1)} %volt_ref.3), custom_call_target="tpu_custom_call" | custom-call | flops 3221225472 | bytes 12582912 | tf_op jit(solution)/shard_map/spectra/pallas_call | solution.py:135
  13.3 0.0 collective-permute-done.past_ref
  13.3 4.0 %spectra_first.1 = (bf16[224,3,16,256]{3,2,1,0:T(8,128)(2,1)}, bf16[32,3,16,256]{3,2,1,0:T(8,128)(2,1)}) custom-call(f32[4,256]{1,0:T(4,128)} %taps_ref.3, bf16[512,512]{1,0:T(8,128)(2,1)} %constant.38.clone.table_ref, bf16[2,256,768]{2,1,0:T(8,128)(2,1)S(1)} %collective-permute-done.past_ref, ...), custom_call_target="tpu_custom_call", output_to_operand_aliasing={{0}: (5, {}), {1}: (6, {})} | custom-call | flops 402653184 | bytes 1572864 | tf_op jit(solution)/shard_map/spectra_first/pallas_call | solution.py:152
  17.4 0.0 copy-start.3
  17.4 6.4 %all-to-all-start = ((bf16[32,336,256]{2,1,0:T(8,128)(2,1)}), bf16[32,336,256]{2,1,0:T(8,128)(2,1)}, u32[]{:S(2)}, u32[]{:S(2)}) async-start(bf16[32,336,256]{2,1,0:T(8,128)(2,1)} %bitcast.30), calls=%async_computation | async-start | bytes 11010048 | tf_op jit(solution)/shard_map/all_to_all | solution.py:523
  23.8 0.0 copy-done.3
  23.8 0.2 reduce-window.9
  24.0 0.1 convert_reduce_fusion
  24.1 5.4 %copy.22 = f32[512,2048]{0,1:T(8,128)} copy(f32[512,2048]{1,0:T(8,128)} %param.9) | data formatting | bytes 8388608 | tf_op jit(solution)/shard_map/optimization_barrier | solution.py:559
  29.4 0.0 copy-start
  29.4 2.2 %copy-done = f32[512,2048]{0,1:T(8,128)S(1)} copy-done((f32[512,2048]{0,1:T(8,128)S(1)}, f32[512,2048]{0,1:T(8,128)}, u32[]{:S(2)}) %copy-start) | copy-done | bytes 4194328
  31.6 51.5 %weights.1.weight_ref = bf16[8,2048,1024]{2,1,0:T(8,128)(2,1)} custom-call(f32[8]{0:T(128)S(1)} %multiply_add_fusion.freq_ref, f32[2048,512]{1,0:T(8,128)S(1)} %bitcast.25), custom_call_target="tpu_custom_call" | custom-call | flops 251658240 | bytes 33554432 | tf_op jit(solution)/shard_map/weights/pallas_call | solution.py:229
  83.1 62.7 %all-to-all-done = bf16[32,336,256]{2,1,0:T(8,128)(2,1)} async-done(((bf16[32,336,256]{2,1,0:T(8,128)(2,1)}), bf16[32,336,256]{2,1,0:T(8,128)(2,1)}, u32[]{:S(2)}, u32[]{:S(2)}) %all-to-all-start) | async-done | bytes 5505056 | tf_op jit(solution)/shard_map/all_to_all | solution.py:523
  145.8 4.0 %all-to-all-start.1 = ((bf16[32,48,256]{2,1,0:T(8,128)(2,1)}), bf16[32,48,256]{2,1,0:T(8,128)(2,1)S(1)}, u32[]{:S(2)}, u32[]{:S(2)}) async-start(bf16[32,48,256]{2,1,0:T(8,128)(2,1)} %bitcast.8), calls=%async_computation.1 | async-start | bytes 1572864 | tf_op jit(solution)/shard_map/all_to_all | solution.py:523
  149.8 0.1 sub.15
  149.8 0.2 convert_reduce_fusion.1
  150.0 0.1 broadcast_compare_fusion
  150.2 14.7 %beams.2 = (f32[7,96,512]{2,1,0:T(8,128)S(1)}, f32[32,128]{1,0:T(8,128)S(1)}) custom-call(f32[32,128]{1,0:T(8,128)S(1)} %broadcast_in_dim.19.before_ref, bf16[32,7,3,16,256]{4,3,2,1,0:T(8,128)(2,1)} %bitcast.6.data_ref, bf16[8,2048,1024]{2,1,0:T(8,128)(2,1)} %weights.1.weight_ref), custom_call_target="tpu_custom_call" | custom-call | flops 5637144576 | bytes 29360128 | tf_op jit(solution)/shard_map/beams/pallas_call | solution.py:312
  164.9 5.0 %all-to-all-done.1 = bf16[32,48,256]{2,1,0:T(8,128)(2,1)S(1)} async-done(((bf16[32,48,256]{2,1,0:T(8,128)(2,1)}), bf16[32,48,256]{2,1,0:T(8,128)(2,1)S(1)}, u32[]{:S(2)}, u32[]{:S(2)}) %all-to-all-start.1) | async-done | bytes 786464 | tf_op jit(solution)/shard_map/all_to_all | solution.py:523
  169.9 3.4 %beams.3 = (f32[1,96,512]{2,1,0:T(8,128)S(1)}, f32[32,128]{1,0:T(8,128)}) custom-call(f32[32,128]{1,0:T(8,128)S(1)} %get-tuple-element.33.before_ref, bf16[32,1,3,16,256]{4,3,2,1,0:T(8,128)(2,1)S(1)} %bitcast.28, bf16[8,2048,1024]{2,1,0:T(8,128)(2,1)} %weights.1.weight_ref), custom_call_target="tpu_custom_call" | custom-call | flops 805306368 | bytes 4194304 | tf_op jit(solution)/shard_map/beams/pallas_call | solution.py:312
  173.4 0.0 copy-start.2
  173.4 0.0 copy-start.1
  173.4 4.1 %all-to-all-start.2 = ((f32[32,1,128]{2,1,0:T(1,128)}), f32[32,1,128]{2,1,0:T(1,128)S(1)}, u32[]{:S(2)}, u32[]{:S(2)}) async-start(f32[32,1,128]{2,1,0:T(1,128)} %bitcast.11), calls=%async_computation.2 | async-start | bytes 32768 | tf_op jit(solution)/shard_map/all_to_all | solution.py:523
  177.5 0.2 select_reduce_fusion
  177.7 0.1 copy.24.count_ref
  177.7 6.4 %all-to-all-done.2 = f32[32,1,128]{2,1,0:T(1,128)S(1)} async-done(((f32[32,1,128]{2,1,0:T(1,128)}), f32[32,1,128]{2,1,0:T(1,128)S(1)}, u32[]{:S(2)}, u32[]{:S(2)}) %all-to-all-start.2) | async-done | bytes 16416 | tf_op jit(solution)/shard_map/all_to_all | solution.py:523
  184.2 0.9 levels.1
  185.1 22.3 %all_to_all.26 = bf16[32,8,1536]{2,1,0:T(8,128)(2,1)S(1)} all-to-all(bf16[32,8,1536]{2,1,0:T(8,128)(2,1)S(1)} %levels.1), channel_id=1, replica_groups=mesh['wide'=8,'tm'=4] {'wide','tm'}, dimensions={0} | all-to-all | bytes 1572864 | tf_op jit(solution)/shard_map/all_to_all | solution.py:523
  207.4 0.8 collective-permute-start.1
  208.2 0.0 copy-done.2
  208.2 0.1 copy.21
  208.3 0.3 fusion.pick_ref
  208.6 0.0 copy-done.1
  208.7 3.2 %search_early.1 = (f32[4,1536,128]{2,1,0:T(8,128)}, f32[448,128]{1,0:T(8,128)S(1)}, bf16[448,256]{1,0:T(8,128)(2,1)S(1)}) custom-call(s32[4]{0:T(128)S(1)} %copy-done.1, bf16[2048,128]{1,0:T(8,128)(2,1)S(1)} %fusion.pick_ref, bf16[256,1536]{1,0:T(8,128)(2,1)S(1)} %bitcast.27), custom_call_target="tpu_custom_call" | custom-call | tf_op jit(solution)/shard_map/search_early/pallas_call | solution.py:476
  211.9 3.6 %collective-permute-done.1.halo_ref = bf16[256,896]{1,0:T(8,128)(2,1)S(1)} collective-permute-done((bf16[256,896]{1,0:T(8,128)(2,1)S(1)}, bf16[256,896]{1,0:T(8,128)(2,1)S(1)}, u32[]{:S(2)}, u32[]{:S(2)}) %collective-permute-start.1) | collective-permute-done | bytes 458784 | tf_op jit(solution)/shard_map/ppermute | solution.py:495
  215.4 3.1 %search_late.1 = f32[4,1536,128]{2,1,0:T(8,128)} custom-call(s32[4]{0:T(128)S(1)} %copy-done.1, bf16[2048,128]{1,0:T(8,128)(2,1)S(1)} %fusion.pick_ref, bf16[448,256]{1,0:T(8,128)(2,1)S(1)} %get-tuple-element.38.last_ref, bf16[256,896]{1,0:T(8,128)(2,1)S(1)} %collective-permute-done.1.halo_ref, ...), custom_call_target="tpu_custom_call", output_to_operand_aliasing={{}: (5, {})} | custom-call | tf_op jit(solution)/shard_map/search_late/pallas_call | solution.py:498
  (10 shorter events, 0.1 us)
Async XLA Ops:
  1.2 12.2 %collective-permute-start = (bf16[2,256,768]{2,1,0:T(8,128)(2,1)S(1)}, bf16[2,256,768]{2,1,0:T(8,128)(2,1)S(1)}, u32[]{:S(2)}, u32[]{:S(2)}) collective-permute-start(bf16[2,256,768]{2,1,0:T(8,128)(2,1)S(1)} %slice.6), channel_id=1, source_target_pairs={{0,1},{1,2},{2,3},{3,0},{4,5},{5,6},{6,7},{7,4},{8,9},{9,10},{10,1... | collective-permute-start | bytes 2359304 | tf_op jit(solution)/shard_map/ppermute | solution.py:541
  17.4 6.4 %copy-start.3 = (s32[8]{0:T(128)S(1)}, s32[8]{0:T(128)}, u32[]{:S(2)}) copy-start(s32[8]{0:T(128)} %param.10) | copy-start | bytes 100
  17.4 128.4 %all-to-all-start = ((bf16[32,336,256]{2,1,0:T(8,128)(2,1)}), bf16[32,336,256]{2,1,0:T(8,128)(2,1)}, u32[]{:S(2)}, u32[]{:S(2)}) async-start(bf16[32,336,256]{2,1,0:T(8,128)(2,1)} %bitcast.30), calls=%async_computation | async-start | bytes 11010048 | tf_op jit(solution)/shard_map/all_to_all | solution.py:523
  29.4 2.2 %copy-start = (f32[512,2048]{0,1:T(8,128)S(1)}, f32[512,2048]{0,1:T(8,128)}, u32[]{:S(2)}) copy-start(f32[512,2048]{0,1:T(8,128)} %copy.22) | copy-start | bytes 12582916
  145.8 24.1 %all-to-all-start.1 = ((bf16[32,48,256]{2,1,0:T(8,128)(2,1)}), bf16[32,48,256]{2,1,0:T(8,128)(2,1)S(1)}, u32[]{:S(2)}, u32[]{:S(2)}) async-start(bf16[32,48,256]{2,1,0:T(8,128)(2,1)} %bitcast.8), calls=%async_computation.1 | async-start | bytes 1572864 | tf_op jit(solution)/shard_map/all_to_all | solution.py:523
  173.4 34.8 %copy-start.2 = (s32[128,256]{1,0:T(8,128)S(1)}, s32[128,256]{1,0:T(8,128)}, u32[]{:S(2)}) copy-start(s32[128,256]{1,0:T(8,128)} %param.11) | copy-start | bytes 393220
  173.4 35.3 %copy-start.1 = (s32[4]{0:T(128)S(1)}, s32[4]{0:T(128)}, u32[]{:S(2)}) copy-start(s32[4]{0:T(128)} %width_ref.3) | copy-start | bytes 52
  173.4 10.8 %all-to-all-start.2 = ((f32[32,1,128]{2,1,0:T(1,128)}), f32[32,1,128]{2,1,0:T(1,128)S(1)}, u32[]{:S(2)}, u32[]{:S(2)}) async-start(f32[32,1,128]{2,1,0:T(1,128)} %bitcast.11), calls=%async_computation.2 | async-start | bytes 32768 | tf_op jit(solution)/shard_map/all_to_all | solution.py:523
  207.4 8.0 %collective-permute-start.1 = (bf16[256,896]{1,0:T(8,128)(2,1)S(1)}, bf16[256,896]{1,0:T(8,128)(2,1)S(1)}, u32[]{:S(2)}, u32[]{:S(2)}) collective-permute-start(bf16[256,896]{1,0:T(8,128)(2,1)S(1)} %slice.8), channel_id=1, source_target_pairs={{0,3},{1,0},{2,1},{3,2},{4,7},{5,4},{6,5},{7,6},{8,11},{9,8},{10,9... | collective-permute-start | bytes 1376264 | tf_op jit(solution)/shard_map/ppermute | solution.py:495

commit v8 on v7

--- a/solution.py
+++ b/solution.py
@@ -563,7 +563,7 @@
     sums = jnp.zeros((devices, 128), jnp.float32)
     power, sums = form_beams(early, weights, sums, 0, wide, tm, 0)
     late, sums = form_beams(
-        arrive(tail, parts[1]), weights, sums, parts[0], wide, tm, 4
+        arrive(tail, parts[1]), weights, sums, parts[0], wide, tm, 8
     )
     powers = [power, late]
 

time: 219 us -> 219 us (level)
  no operation moved by 1% of the time
where the time goes in v8:
time: 219 us; the launch traced here: 218 us
  Pallas kernels  90.3 us (41%)
  waiting for transfers between devices  77.7 us (35%)
  blocking collectives  22.3 us (10%)
  starting transfers between devices  17.9 us (8%)
  local copies, waits for them, and re-layouts  9.05 us (4%)
    all_to_all x3, waiting for transfers between devices, exchange(): return lax.all_to_all(value, AXES, split_axis=0, concat_axis=0, tiled=True)  74.1 us
    pallas_call x1, Pallas kernels, beam_weights(): pl.pallas_call(weights_kernel, grid=(antennas // block, channels), in_spe...  51.5 us
    all_to_all x1, blocking collectives, exchange(): return lax.all_to_all(value, AXES, split_axis=0, concat_axis=0, tiled=True)  22.3 us
    pallas_call x2, Pallas kernels, form_beams(): pl.pallas_call(functools.partial(beam_kernel, wide, tm, first), grid=(cha...  18 us
    all_to_all x3, starting transfers between devices, exchange(): return lax.all_to_all(value, AXES, split_axis=0, concat_axis=0, tiled=True)  14.5 us
    pallas_call x1, Pallas kernels, spectra(): pl.pallas_call(functools.partial(spectra_kernel, (5 - taps) * width), gri...  9.5 us
    optimization_barrier x1, local copies, waits for them, and re-layouts, body(): lax.optimization_barrier((early, frequency, steering))  5.36 us
  transfers between devices with their start and end apart: 5, of which 4 were waited for; matrix products, arithmetic and copies ran while one was open for 3% of the time, Pallas kernels for 36%

profile of v8, /device:TPU:1, one launch (start us, length us, event | category | flops | bytes accessed | tf_op | source)
XLA Modules:
  0.0 218.4 jit_solution(3894289058022451812)
XLA Ops:
  0.0 1.2 slice.6
  1.2 2.7 %collective-permute-start = (bf16[2,256,768]{2,1,0:T(8,128)(2,1)S(1)}, bf16[2,256,768]{2,1,0:T(8,128)(2,1)S(1)}, u32[]{:S(2)}, u32[]{:S(2)}) collective-permute-start(bf16[2,256,768]{2,1,0:T(8,128)(2,1)S(1)} %slice.6), channel_id=1, source_target_pairs={{0,1},{1,2},{2,3},{3,0},{4,5},{5,6},{6,7},{7,4},{8,9},{9,10},{10,1... | collective-permute-start | bytes 2359304 | tf_op jit(solution)/shard_map/ppermute | solution.py:541
  3.8 9.5 %spectra.1 = (bf16[224,3,16,256]{3,2,1,0:T(8,128)(2,1)}, bf16[32,3,16,256]{3,2,1,0:T(8,128)(2,1)}, f32[2,4096,128]{2,1,0:T(8,128)S(1)}) custom-call(f32[4,256]{1,0:T(4,128)} %taps_ref.3, bf16[512,512]{1,0:T(8,128)(2,1)} %constant.38.clone.table_ref, bf16[2,256,6144]{2,1,0:T(8,128)(2,1)} %volt_ref.3, bf16[2,256,6144]{2,1,0:T(8,128)(2,1)} %volt_ref.3), custom_call_target="tpu_custom_call" | custom-call | flops 3221225472 | bytes 12582912 | tf_op jit(solution)/shard_map/spectra/pallas_call | solution.py:135
  13.3 0.0 collective-permute-done.past_ref
  13.3 4.0 %spectra_first.1 = (bf16[224,3,16,256]{3,2,1,0:T(8,128)(2,1)}, bf16[32,3,16,256]{3,2,1,0:T(8,128)(2,1)}) custom-call(f32[4,256]{1,0:T(4,128)} %taps_ref.3, bf16[512,512]{1,0:T(8,128)(2,1)} %constant.38.clone.table_ref, bf16[2,256,768]{2,1,0:T(8,128)(2,1)S(1)} %collective-permute-done.past_ref, ...), custom_call_target="tpu_custom_call", output_to_operand_aliasing={{0}: (5, {}), {1}: (6, {})} | custom-call | flops 402653184 | bytes 1572864 | tf_op jit(solution)/shard_map/spectra_first/pallas_call | solution.py:152
  17.4 0.0 copy-start.3
  17.4 6.4 %all-to-all-start = ((bf16[32,336,256]{2,1,0:T(8,128)(2,1)}), bf16[32,336,256]{2,1,0:T(8,128)(2,1)}, u32[]{:S(2)}, u32[]{:S(2)}) async-start(bf16[32,336,256]{2,1,0:T(8,128)(2,1)} %bitcast.30), calls=%async_computation | async-start | bytes 11010048 | tf_op jit(solution)/shard_map/all_to_all | solution.py:523
  23.8 0.0 copy-done.3
  23.8 0.2 reduce-window.9
  24.0 0.1 convert_reduce_fusion
  24.1 5.4 %copy.22 = f32[512,2048]{0,1:T(8,128)} copy(f32[512,2048]{1,0:T(8,128)} %param.9) | data formatting | bytes 8388608 | tf_op jit(solution)/shard_map/optimization_barrier | solution.py:559
  29.4 0.0 copy-start
  29.4 2.2 %copy-done = f32[512,2048]{0,1:T(8,128)S(1)} copy-done((f32[512,2048]{0,1:T(8,128)S(1)}, f32[512,2048]{0,1:T(8,128)}, u32[]{:S(2)}) %copy-start) | copy-done | bytes 4194328
  31.6 51.5 %weights.1.weight_ref = bf16[8,2048,1024]{2,1,0:T(8,128)(2,1)} custom-call(f32[8]{0:T(128)S(1)} %multiply_add_fusion.freq_ref, f32[2048,512]{1,0:T(8,128)S(1)} %bitcast.25), custom_call_target="tpu_custom_call" | custom-call | flops 251658240 | bytes 33554432 | tf_op jit(solution)/shard_map/weights/pallas_call | solution.py:229
  83.1 62.7 %all-to-all-done = bf16[32,336,256]{2,1,0:T(8,128)(2,1)} async-done(((bf16[32,336,256]{2,1,0:T(8,128)(2,1)}), bf16[32,336,256]{2,1,0:T(8,128)(2,1)}, u32[]{:S(2)}, u32[]{:S(2)}) %all-to-all-start) | async-done | bytes 5505056 | tf_op jit(solution)/shard_map/all_to_all | solution.py:523
  145.8 4.0 %all-to-all-start.1 = ((bf16[32,48,256]{2,1,0:T(8,128)(2,1)}), bf16[32,48,256]{2,1,0:T(8,128)(2,1)S(1)}, u32[]{:S(2)}, u32[]{:S(2)}) async-start(bf16[32,48,256]{2,1,0:T(8,128)(2,1)} %bitcast.8), calls=%async_computation.1 | async-start | bytes 1572864 | tf_op jit(solution)/shard_map/all_to_all | solution.py:523
  149.8 0.1 sub.15
  149.8 0.2 convert_reduce_fusion.1
  150.0 0.1 broadcast_compare_fusion
  150.2 14.7 %beams.2 = (f32[7,96,512]{2,1,0:T(8,128)S(1)}, f32[32,128]{1,0:T(8,128)S(1)}) custom-call(f32[32,128]{1,0:T(8,128)S(1)} %broadcast_in_dim.19.before_ref, bf16[32,7,3,16,256]{4,3,2,1,0:T(8,128)(2,1)} %bitcast.6.data_ref, bf16[8,2048,1024]{2,1,0:T(8,128)(2,1)} %weights.1.weight_ref), custom_call_target="tpu_custom_call" | custom-call | flops 5637144576 | bytes 29360128 | tf_op jit(solution)/shard_map/beams/pallas_call | solution.py:312
  164.9 5.0 %all-to-all-done.1 = bf16[32,48,256]{2,1,0:T(8,128)(2,1)S(1)} async-done(((bf16[32,48,256]{2,1,0:T(8,128)(2,1)}), bf16[32,48,256]{2,1,0:T(8,128)(2,1)S(1)}, u32[]{:S(2)}, u32[]{:S(2)}) %all-to-all-start.1) | async-done | bytes 786464 | tf_op jit(solution)/shard_map/all_to_all | solution.py:523
  169.9 3.3 %beams.3 = (f32[1,96,512]{2,1,0:T(8,128)S(1)}, f32[32,128]{1,0:T(8,128)}) custom-call(f32[32,128]{1,0:T(8,128)S(1)} %get-tuple-element.33.before_ref, bf16[32,1,3,16,256]{4,3,2,1,0:T(8,128)(2,1)S(1)} %bitcast.28, bf16[8,2048,1024]{2,1,0:T(8,128)(2,1)} %weights.1.weight_ref), custom_call_target="tpu_custom_call" | custom-call | flops 805306368 | bytes 4194304 | tf_op jit(solution)/shard_map/beams/pallas_call | solution.py:312
  173.2 0.0 copy-start.2
  173.2 0.0 copy-start.1
  173.3 4.1 %all-to-all-start.2 = ((f32[32,1,128]{2,1,0:T(1,128)}), f32[32,1,128]{2,1,0:T(1,128)S(1)}, u32[]{:S(2)}, u32[]{:S(2)}) async-start(f32[32,1,128]{2,1,0:T(1,128)} %bitcast.11), calls=%async_computation.2 | async-start | bytes 32768 | tf_op jit(solution)/shard_map/all_to_all | solution.py:523
  177.4 0.2 select_reduce_fusion
  177.5 0.1 copy.24.count_ref
  177.6 6.4 %all-to-all-done.2 = f32[32,1,128]{2,1,0:T(1,128)S(1)} async-done(((f32[32,1,128]{2,1,0:T(1,128)}), f32[32,1,128]{2,1,0:T(1,128)S(1)}, u32[]{:S(2)}, u32[]{:S(2)}) %all-to-all-start.2) | async-done | bytes 16416 | tf_op jit(solution)/shard_map/all_to_all | solution.py:523
  184.1 0.9 levels.1
  185.0 22.3 %all_to_all.26 = bf16[32,8,1536]{2,1,0:T(8,128)(2,1)S(1)} all-to-all(bf16[32,8,1536]{2,1,0:T(8,128)(2,1)S(1)} %levels.1), channel_id=1, replica_groups=mesh['wide'=8,'tm'=4] {'wide','tm'}, dimensions={0} | all-to-all | bytes 1572864 | tf_op jit(solution)/shard_map/all_to_all | solution.py:523
  207.3 0.8 collective-permute-start.1
  208.1 0.0 copy-done.2
  208.1 0.1 copy.21
  208.2 0.3 fusion.pick_ref
  208.5 0.0 copy-done.1
  208.5 3.2 %search_early.1 = (f32[4,1536,128]{2,1,0:T(8,128)}, f32[448,128]{1,0:T(8,128)S(1)}, bf16[448,256]{1,0:T(8,128)(2,1)S(1)}) custom-call(s32[4]{0:T(128)S(1)} %copy-done.1, bf16[2048,128]{1,0:T(8,128)(2,1)S(1)} %fusion.pick_ref, bf16[256,1536]{1,0:T(8,128)(2,1)S(1)} %bitcast.27), custom_call_target="tpu_custom_call" | custom-call | tf_op jit(solution)/shard_map/search_early/pallas_call | solution.py:476
  211.7 3.6 %collective-permute-done.1.halo_ref = bf16[256,896]{1,0:T(8,128)(2,1)S(1)} collective-permute-done((bf16[256,896]{1,0:T(8,128)(2,1)S(1)}, bf16[256,896]{1,0:T(8,128)(2,1)S(1)}, u32[]{:S(2)}, u32[]{:S(2)}) %collective-permute-start.1) | collective-permute-done | bytes 458784 | tf_op jit(solution)/shard_map/ppermute | solution.py:495
  215.3 3.1 %search_late.1 = f32[4,1536,128]{2,1,0:T(8,128)} custom-call(s32[4]{0:T(128)S(1)} %copy-done.1, bf16[2048,128]{1,0:T(8,128)(2,1)S(1)} %fusion.pick_ref, bf16[448,256]{1,0:T(8,128)(2,1)S(1)} %get-tuple-element.38.last_ref, bf16[256,896]{1,0:T(8,128)(2,1)S(1)} %collective-permute-done.1.halo_ref, ...), custom_call_target="tpu_custom_call", output_to_operand_aliasing={{}: (5, {})} | custom-call | tf_op jit(solution)/shard_map/search_late/pallas_call | solution.py:498
  (10 shorter events, 0.1 us)
Async XLA Ops:
  1.2 12.2 %collective-permute-start = (bf16[2,256,768]{2,1,0:T(8,128)(2,1)S(1)}, bf16[2,256,768]{2,1,0:T(8,128)(2,1)S(1)}, u32[]{:S(2)}, u32[]{:S(2)}) collective-permute-start(bf16[2,256,768]{2,1,0:T(8,128)(2,1)S(1)} %slice.6), channel_id=1, source_target_pairs={{0,1},{1,2},{2,3},{3,0},{4,5},{5,6},{6,7},{7,4},{8,9},{9,10},{10,1... | collective-permute-start | bytes 2359304 | tf_op jit(solution)/shard_map/ppermute | solution.py:541
  17.4 6.4 %copy-start.3 = (s32[8]{0:T(128)S(1)}, s32[8]{0:T(128)}, u32[]{:S(2)}) copy-start(s32[8]{0:T(128)} %param.10) | copy-start | bytes 100
  17.4 128.4 %all-to-all-start = ((bf16[32,336,256]{2,1,0:T(8,128)(2,1)}), bf16[32,336,256]{2,1,0:T(8,128)(2,1)}, u32[]{:S(2)}, u32[]{:S(2)}) async-start(bf16[32,336,256]{2,1,0:T(8,128)(2,1)} %bitcast.30), calls=%async_computation | async-start | bytes 11010048 | tf_op jit(solution)/shard_map/all_to_all | solution.py:523
  29.4 2.2 %copy-start = (f32[512,2048]{0,1:T(8,128)S(1)}, f32[512,2048]{0,1:T(8,128)}, u32[]{:S(2)}) copy-start(f32[512,2048]{0,1:T(8,128)} %copy.22) | copy-start | bytes 12582916
  145.8 24.1 %all-to-all-start.1 = ((bf16[32,48,256]{2,1,0:T(8,128)(2,1)}), bf16[32,48,256]{2,1,0:T(8,128)(2,1)S(1)}, u32[]{:S(2)}, u32[]{:S(2)}) async-start(bf16[32,48,256]{2,1,0:T(8,128)(2,1)} %bitcast.8), calls=%async_computation.1 | async-start | bytes 1572864 | tf_op jit(solution)/shard_map/all_to_all | solution.py:523
  173.2 34.9 %copy-start.2 = (s32[128,256]{1,0:T(8,128)S(1)}, s32[128,256]{1,0:T(8,128)}, u32[]{:S(2)}) copy-start(s32[128,256]{1,0:T(8,128)} %param.11) | copy-start | bytes 393220
  173.2 35.3 %copy-start.1 = (s32[4]{0:T(128)S(1)}, s32[4]{0:T(128)}, u32[]{:S(2)}) copy-start(s32[4]{0:T(128)} %width_ref.3) | copy-start | bytes 52
  173.3 10.8 %all-to-all-start.2 = ((f32[32,1,128]{2,1,0:T(1,128)}), f32[32,1,128]{2,1,0:T(1,128)S(1)}, u32[]{:S(2)}, u32[]{:S(2)}) async-start(f32[32,1,128]{2,1,0:T(1,128)} %bitcast.11), calls=%async_computation.2 | async-start | bytes 32768 | tf_op jit(solution)/shard_map/all_to_all | solution.py:523
  207.3 8.0 %collective-permute-start.1 = (bf16[256,896]{1,0:T(8,128)(2,1)S(1)}, bf16[256,896]{1,0:T(8,128)(2,1)S(1)}, u32[]{:S(2)}, u32[]{:S(2)}) collective-permute-start(bf16[256,896]{1,0:T(8,128)(2,1)S(1)} %slice.8), channel_id=1, source_target_pairs={{0,3},{1,0},{2,1},{3,2},{4,7},{5,4},{6,5},{7,6},{8,11},{9,8},{10,9... | collective-permute-start | bytes 1376264 | tf_op jit(solution)/shard_map/ppermute | solution.py:495
